TPU v7x, 128 devices: a whole 4x4x4 slice. The times are simulated.
128 devices in a mesh: dp: 4 (over z_hi, core), fsdp: 32 (over z_lo, y, x).
Axes of the slice: x: 4, y: 4, z: 4 (z_hi: 2, z_lo: 2; z = z_hi * 2 + z_lo), core: 2. Of those that a mesh axis runs over, the one named last changes fastest.
Arguments:
- grads: bfloat16 [4, 8192, 16384], P('dp', None, 'fsdp'), may hold values from -6 to 6
- basis: bfloat16 [8192, 1024], P(('dp', 'fsdp')), may hold values from -0.1875 to 0.1875
- first_moment: float32 [1024, 16384], P('dp', 'fsdp'), may hold values from -3 to 3
- second_moment: float32 [1024, 16384], P('dp', 'fsdp'), may hold values from 0.5 to 4
Outputs:
- update: bfloat16 [8192, 16384], P(None, 'fsdp')
- new_first: float32 [1024, 16384], P('dp', 'fsdp')
- new_second: float32 [1024, 16384], P('dp', 'fsdp')
All inputs are finite; a program needn't handle non-finite values.
Results may differ from a plain program's by a relative error of at most 0.005.
Values may be sent and summed in bfloat16 or wider, within the bound.
No kernel may reach another device: no remote copies, remote signals or barrier semaphores. Data moves between devices by JAX's collectives and lax.ppermute only.
A program may use at most 128 MiB of HBM per device.

v0:
```python
import math

import jax
import jax.numpy as jnp
from jax import lax
from jax.sharding import PartitionSpec as P

first_fix = 1.0 - math.exp(1000.0 * math.log(0.9))
second_fix = 1.0 - math.exp(1000.0 * math.log(0.999))


def local(grads, basis, first_moment, second_moment):
    local_grad = grads[0]
    groups = lax.axis_size("dp")
    share = first_moment.shape[0]
    whole_basis = lax.all_gather(basis, ("dp", "fsdp"), axis=0, tiled=True)
    partial_value = lax.dot_general(
        whole_basis, local_grad, (((0,), (0,)), ((), ())), preferred_element_type=jnp.float32
    )
    summed = lax.psum(partial_value, "dp")
    mine = lax.dynamic_slice_in_dim(summed, lax.axis_index("dp") * share, share, 0)
    projected = mine * (1.0 / groups)
    new_first = 0.9 * first_moment + 0.1 * projected
    new_second = 0.999 * second_moment + 0.001 * projected * projected
    direction = (new_first / first_fix / (jnp.sqrt(new_second / second_fix) + 1e-08)).astype(
        jnp.bfloat16
    )
    full_direction = lax.all_gather(direction, "dp", axis=0, tiled=True)
    update = jnp.dot(whole_basis, full_direction, preferred_element_type=jnp.float32).astype(
        jnp.bfloat16
    )
    return (update, new_first, new_second)


def solution(mesh):
    return jax.shard_map(
        local,
        mesh=mesh,
        in_specs=(P("dp", None, "fsdp"), P(("dp", "fsdp"), None), P("dp", "fsdp"), P("dp", "fsdp")),
        out_specs=(P(None, "fsdp"), P("dp", "fsdp"), P("dp", "fsdp")),
        check_vma=False,
    )
```

profile of v0, /device:TPU:1, one launch (start us, length us, event | category | flops | bytes accessed | tf_op | source)
XLA Modules:
  0.0 471.4 jit_solution(16001976137639074502)
XLA Ops:
  7.2 0.0 all-gather.3.cloned.1.call-start
  7.2 0.7 all-gather.3.cloned.1.call-update
  7.9 0.0 copy-start
  7.9 0.0 copy-start.1
  7.9 0.0 all-reduce.2.cloned.1.call-start
  8.0 332.2 %all-gather.3.cloned.1.call-done = bf16[8192,1024]{1,0:T(8,128)(2,1)} async-done(((bf16[64,1024]{1,0:T(8,128)(2,1)}), bf16[8192,1024]{1,0:T(8,128)(2,1)}) %all-gather.3.cloned.1.call-update) | async-done | bytes 16777232 | tf_op jit(solution)/shard_map/all_gather | solution.py:16
  340.1 15.8 %fusion.1 = f32[1024,512]{1,0:T(8,128)} fusion(bf16[8192,1024]{1,0:T(8,128)(2,1)} %all-gather.3.cloned.1.call-done, bf16[1,8192,512]{2,1,0:T(8,128)(2,1)} %param.4), kind=kOutput, calls=%fused_computation.2 | convolution fusion | flops 8589934592 | bytes 27262976 | tf_op jit(solution)/shard_map/dot_general | solution.py:17
  355.9 0.0 all-reduce.2.cloned.1.call-update
  355.9 0.0 all-gather.5.cloned.1.call-start
  356.0 59.6 %all-reduce.2.cloned.1.call-done = f32[1024,512]{1,0:T(8,128)} async-done(((f32[1024,512]{1,0:T(8,128)}), f32[1024,512]{1,0:T(8,128)}) %all-reduce.2.cloned.1.call-update) | async-done | bytes 2097168 | tf_op jit(solution)/shard_map/psum | solution.py:20
  415.6 0.0 copy-done
  415.6 0.0 copy-done.1
  415.6 2.3 divide_convert_fusion
  417.9 0.0 all-gather.5.cloned.1.call-update
  417.9 20.3 %all-gather.5.cloned.1.call-done = bf16[1024,512]{1,0:T(8,128)(2,1)} async-done(((bf16[256,512]{1,0:T(8,128)(2,1)}), bf16[1024,512]{1,0:T(8,128)(2,1)}) %all-gather.5.cloned.1.call-update) | async-done | bytes 1048592 | tf_op jit(solution)/shard_map/all_gather | solution.py:28
  438.3 14.7 %fusion = bf16[8192,512]{0,1:T(8,128)(2,1)} fusion(bf16[1024,512]{1,0:T(8,128)(2,1)} %all-gather.5.cloned.1.call-done, bf16[8192,1024]{1,0:T(8,128)(2,1)} %all-gather.3.cloned.1.call-done), kind=kOutput, calls=%fused_computation.1 | convolution fusion | flops 8594128896 | bytes 26214400 | tf_op jit(solution)/shard_map/dot_general | solution.py:29
  452.9 11.9 %copy.7 = bf16[8192,512]{1,0:T(8,128)(2,1)} copy(bf16[8192,512]{0,1:T(8,128)(2,1)} %fusion) | data formatting | bytes 16777216
Async XLA Ops:
  7.2 333.0 %all-gather.3.cloned.1.call-start = ((), (), s32[]{:S(2)}) async-start(), calls=%async_computation | async-start | bytes 16908288 | tf_op jit(solution)/shard_map/all_gather | solution.py:16
  7.9 407.7 %copy-start = (f32[256,512]{1,0:T(8,128)S(1)}, f32[256,512]{1,0:T(8,128)}, u32[]{:S(2)}) copy-start(f32[256,512]{1,0:T(8,128)} %param.7) | copy-start | bytes 1572868
  7.9 407.7 %copy-start.1 = (f32[256,512]{1,0:T(8,128)S(1)}, f32[256,512]{1,0:T(8,128)}, u32[]{:S(2)}) copy-start(f32[256,512]{1,0:T(8,128)} %param.6) | copy-start | bytes 1572868
  7.9 407.7 %all-reduce.2.cloned.1.call-start = ((), (), s32[]{:S(2)}) async-start(), calls=%async_computation.1 | async-start | bytes 4194304 | tf_op jit(solution)/shard_map/psum | solution.py:20
  355.9 82.3 %all-gather.5.cloned.1.call-start = ((), (), s32[]{:S(2)}) async-start(), calls=%async_computation.2 | async-start | bytes 1310720 | tf_op jit(solution)/shard_map/all_gather | solution.py:28
Sparse Core Ops, SparseCore 0:
  9.7 330.3 all-gather.2
  356.1 59.4 all-reduce.1
  418.1 20.1 all-gather.4
where the time goes:
time: 472 us; the launch traced here: 471 us
  waiting for transfers between devices  413 us (88%)
  matrix products  30.5 us (6%)
  between operations  13.8 us (3%)
  local copies, waits for them, and re-layouts  11.9 us (3%)
    all_gather x1, waiting for transfers between devices, local(): whole_basis = lax.all_gather(basis, ('dp', 'fsdp'), axis=0, tiled=True)  332 us
    psum x1, waiting for transfers between devices, local(): summed = lax.psum(partial_value, 'dp')  59.6 us
    all_gather x1, waiting for transfers between devices, local(): full_direction = lax.all_gather(direction, 'dp', axis=0, tiled=True)  20.3 us
    dot_general x1, matrix products, local(): lax.dot_general(whole_basis, local_grad, (((0,), (0,)), ((), ())), prefer...  15.8 us
    dot_general x1, matrix products, local(): jnp.dot(whole_basis, full_direction, preferred_element_type=jnp.float32)  14.7 us
    unnamed x5, local copies, waits for them, and re-layouts  11.9 us
  transfers between devices with their start and end apart: 3, of which 3 were waited for; matrix products, arithmetic and copies ran while one was open for 0% of the time, Pallas kernels for 0%

commit v1 on v0

v1 whole, which is shorter than its diff:
```python
import math

import jax
import jax.numpy as jnp
from jax import lax
from jax.experimental import pallas as pl
from jax.experimental.pallas import tpu as pltpu
from jax.sharding import PartitionSpec as P

first_fix = 1.0 - math.exp(1000.0 * math.log(0.9))
second_fix = 1.0 - math.exp(1000.0 * math.log(0.999))

BOTH = ("dp", "fsdp")
STREAMS = ((0, 384, "zyx"), (384, 768, "yxz"), (768, 1024, "xzy"))
ORDER = ((0, 1, 3, 2), (0, 3, 1, 2))


def pairs(partner):
    out = []
    for c in range(2):
        for z in range(4):
            for y in range(4):
                for x in range(4):
                    out.append((linear(c, z, y, x), linear(*partner(c, z, y, x))))
    return out


def linear(c, z, y, x):
    return (((z // 2) * 2 + c) * 2 + z % 2) * 16 + y * 4 + x


def exchange(value, axis, step):
    def partner(c, z, y, x):
        t = ORDER[c][1] if step == 0 else ORDER[1 - c][1]
        return c, z ^ t if axis == "z" else z, y ^ t if axis == "y" else y, x ^ t if axis == "x" else x

    return lax.ppermute(value, BOTH, pairs(partner))


def swap_core(value):
    return lax.ppermute(value, BOTH, pairs(lambda c, z, y, x: (1 - c, z, y, x)))


def swap_far(value):
    return lax.ppermute(value, BOTH, pairs(lambda c, z, y, x: (c, z ^ 2, y, x)))


def gather(shard, order):
    held = shard[None, None, None]
    for axis in order:
        for step in range(2):
            held = jnp.concatenate([held, exchange(held, axis, step)], axis="zyx".index(axis))
    return held


def place(core, block):
    return jnp.where(core == 0, ORDER[0][block], ORDER[1][block])


def row_of(core, of_core, z, y, x, index):
    a, b, c = index // 16, (index // 4) % 4, index % 4

    def off(p):
        one = jnp.where(of_core == 0, 1, 3)
        return jnp.where(p == 0, 0, jnp.where(p == 1, one, jnp.where(p == 2, 4 - one, 2)))

    zz, yy, xx = z ^ off(a), y ^ off(b), x ^ off(c)
    return (((zz // 2) * 2 + of_core) * 2 + zz % 2) * 1024 + yy * 256 + xx * 64


def split_kernel(where, grads, own, other, sems):
    core, z, y, x = where[0], where[1], where[2], where[3]

    def body(i, carry):
        for k, (out, of_core) in enumerate(((own, core), (other, 1 - core))):
            row = pl.multiple_of(row_of(core, of_core, z, y, x, i), 64)
            pltpu.make_async_copy(
                grads.at[pl.ds(row, 64)], out.at[pl.ds(pl.multiple_of(i * 64, 64), 64)], sems.at[k]
            ).start()
        return carry

    lax.fori_loop(0, 64, body, 0)
    pltpu.make_async_copy(own, own, sems.at[0]).wait()
    pltpu.make_async_copy(other, other, sems.at[1]).wait()


def split_grads(where, grads):
    half = jax.ShapeDtypeStruct((grads.shape[0] // 2, grads.shape[1]), grads.dtype)
    return pl.pallas_call(
        split_kernel,
        out_shape=(half, half),
        grid_spec=pltpu.PrefetchScalarGridSpec(
            num_scalar_prefetch=1,
            grid=(),
            in_specs=[pl.BlockSpec(memory_space=pl.ANY)],
            out_specs=[pl.BlockSpec(memory_space=pl.ANY)] * 2,
            scratch_shapes=[pltpu.SemaphoreType.DMA((2,))],
        ),
        name="split_grads",
    )(where, grads)


TILE = 512


def update_kernel(where, own, other, direction, out, result, sems):
    core, z, y, x = where[0], where[1], where[2], where[3]
    step = pl.program_id(0)
    half = pl.num_programs(0) // 2
    slot = step % 2

    def drain(k):
        pltpu.make_async_copy(result.at[k], result.at[k], sems.at[k]).wait()

    @pl.when(step >= 2)
    def _():
        drain(slot)

    def go(basis, of_core, base):
        result[slot] = jnp.dot(
            basis[...], direction[...], preferred_element_type=jnp.float32
        ).astype(jnp.bfloat16)
        for j in range(TILE // 64):
            row = pl.multiple_of(row_of(core, of_core, z, y, x, base * (TILE // 64) + j), 64)
            pltpu.make_async_copy(
                result.at[slot, pl.ds(j * 64, 64)], out.at[pl.ds(row, 64)], sems.at[slot]
            ).start()

    @pl.when(step < half)
    def _():
        go(own, core, step)

    @pl.when(step >= half)
    def _():
        go(other, 1 - core, step - half)

    @pl.when(step == 2 * half - 1)
    def _():
        drain(1 - slot)
        drain(slot)


def back_project(where, own, other, direction):
    rows, rank = own.shape
    columns = direction.shape[1]
    half = rows // TILE
    return pl.pallas_call(
        update_kernel,
        out_shape=jax.ShapeDtypeStruct((2 * rows, columns), jnp.bfloat16),
        grid_spec=pltpu.PrefetchScalarGridSpec(
            num_scalar_prefetch=1,
            grid=(2 * half,),
            in_specs=[
                pl.BlockSpec((TILE, rank), lambda i, w: (jnp.minimum(i, half - 1), 0)),
                pl.BlockSpec((TILE, rank), lambda i, w: (jnp.maximum(i - half, 0), 0)),
                pl.BlockSpec((rank, columns), lambda i, w: (0, 0)),
            ],
            out_specs=pl.BlockSpec(memory_space=pl.ANY),
            scratch_shapes=[
                pltpu.VMEM((2, TILE, columns), jnp.bfloat16),
                pltpu.SemaphoreType.DMA((2,)),
            ],
        ),
        compiler_params=pltpu.CompilerParams(vmem_limit_bytes=32 * 1024 * 1024),
        name="back_project",
    )(where, own, other, direction)


def local(grads, basis, first_moment, second_moment):
    dp, fsdp = lax.axis_index("dp"), lax.axis_index("fsdp")
    far, core = dp // 2, dp % 2
    z, y, x = far * 2 + fsdp // 16, (fsdp // 4) % 4, fsdp % 4
    where = jnp.stack([core, z, y, x]).astype(jnp.int32)

    mine, theirs = split_grads(where, grads[0])
    summed_grads = (mine.astype(jnp.float32) + swap_core(theirs).astype(jnp.float32)).astype(jnp.bfloat16)

    chunks = [gather(basis[:, low:high], order).reshape(-1, high - low) for low, high, order in STREAMS]
    partial = jnp.concatenate(
        [
            lax.dot_general(chunk, summed_grads, (((0,), (0,)), ((), ())), preferred_element_type=jnp.float32)
            for chunk in chunks
        ]
    )
    own_basis = jnp.concatenate(chunks, axis=1)
    other_basis = swap_core(own_basis)

    share, columns = first_moment.shape
    partial = partial.reshape(2, 2, share, columns)
    kept = lax.dynamic_index_in_dim(partial, core, 1, keepdims=False)
    sent = lax.dynamic_index_in_dim(partial, 1 - core, 1, keepdims=False)
    chip = kept + swap_core(sent)
    kept = lax.dynamic_index_in_dim(chip, far, 0, keepdims=False)
    sent = lax.dynamic_index_in_dim(chip, 1 - far, 0, keepdims=False)
    total = kept + swap_far(sent.astype(jnp.bfloat16)).astype(jnp.float32)

    projected = total * (1.0 / 4)
    new_first = 0.9 * first_moment + 0.1 * projected
    new_second = 0.999 * second_moment + 0.001 * projected * projected
    direction = (new_first / first_fix / (jnp.sqrt(new_second / second_fix) + 1e-08)).astype(jnp.bfloat16)

    received = swap_far(direction)
    pair = jnp.stack([jnp.where(far == 0, direction, received), jnp.where(far == 0, received, direction)])
    received = swap_core(pair)
    whole = jnp.stack([jnp.where(core == 0, pair, received), jnp.where(core == 0, received, pair)], axis=1)
    update = back_project(where, own_basis, other_basis, whole.reshape(4 * share, columns))
    return (update, new_first, new_second)


def solution(mesh):
    return jax.shard_map(
        local,
        mesh=mesh,
        in_specs=(P("dp", None, "fsdp"), P(("dp", "fsdp"), None), P("dp", "fsdp"), P("dp", "fsdp")),
        out_specs=(P(None, "fsdp"), P("dp", "fsdp"), P("dp", "fsdp")),
        check_vma=False,
    )
```

time: 472 us -> 396 us (0.84)
  waiting for transfers between devices: 413 us -> 44.6 us
  Pallas kernels: 0 us -> 276 us
  starting transfers between devices: 0.12 us -> 39.7 us
  matrix products: 30.5 us -> 13.7 us
  other arithmetic: 2.31 us -> 18 us
  between operations: 13.8 us -> 1.42 us
  local copies, waits for them, and re-layouts: 11.9 us -> 1.9 us
    all_gather x2 -> x0, waiting for transfers between devices: 352 us -> none  [the longest x1 332 us: local(): whole_basis = lax.all_gather(basis, ('dp', 'fsdp'), axis=0, tiled=True)]
    pallas_call x0 -> x2, Pallas kernels: none -> 276 us  [the longest x1 256 us: split_grads(): pl.pallas_call(split_kernel, out_shape=(half, half), grid_spec=pltpu.Pref...]
    psum x1 -> x0, waiting for transfers between devices: 59.6 us -> none  [local(): summed = lax.psum(partial_value, 'dp')]
    ppermute x0 -> x24, waiting for transfers between devices: none -> 44.6 us  [the longest x18 23.8 us: exchange(): return lax.ppermute(value, BOTH, pairs(partner))]
    ppermute x0 -> x24, starting transfers between devices: none -> 39.7 us  [the longest x18 19.9 us: exchange(): return lax.ppermute(value, BOTH, pairs(partner))]
    dot_general x2 -> x3, matrix products: 30.5 us -> 13.7 us  [local(): lax.dot_general(chunk, summed_grads, (((0,), (0,)), ((), ())), preferred_...]
    concatenate x0 -> x20, other arithmetic: none -> 13.2 us  [the longest x18 8.64 us: gather(): jnp.concatenate([held, exchange(held, axis, step)], axis='zyx'.index(axis))]
    unnamed x5 -> x54, local copies, waits for them, and re-layouts: 11.9 us -> 0.11 us
  transfers between devices with their start and end apart: 3 -> 24, of which waited for: 3 -> 13; matrix products, arithmetic and copies ran while one was open for 0% -> 8% of each run, Pallas kernels for 0% -> 65%
where the time goes in v1:
time: 396 us
  Pallas kernels  276 us (70%)
  waiting for transfers between devices  44.6 us (11%)
  starting transfers between devices  39.7 us (10%)
  other arithmetic  18 us (5%)
  matrix products  13.7 us (3%)
    pallas_call x1, Pallas kernels, split_grads(): pl.pallas_call(split_kernel, out_shape=(half, half), grid_spec=pltpu.Pref...  256 us
    ppermute x18, waiting for transfers between devices, exchange(): return lax.ppermute(value, BOTH, pairs(partner))  23.8 us
    pallas_call x1, Pallas kernels, back_project(): pl.pallas_call(update_kernel, out_shape=jax.ShapeDtypeStruct((2 * rows, c...  20.3 us
    ppermute x18, starting transfers between devices, exchange(): return lax.ppermute(value, BOTH, pairs(partner))  19.9 us
    ppermute x4, starting transfers between devices, swap_core(): return lax.ppermute(value, BOTH, pairs(lambda c, z, y, x: (1 - c, z, y, x)))  19.4 us
    ppermute x2, waiting for transfers between devices, swap_far(): return lax.ppermute(value, BOTH, pairs(lambda c, z, y, x: (c, z ^ 2, y, x)))  16.8 us
    dot_general x3, matrix products, local(): lax.dot_general(chunk, summed_grads, (((0,), (0,)), ((), ())), preferred_...  13.7 us
    concatenate x18, other arithmetic, gather(): jnp.concatenate([held, exchange(held, axis, step)], axis='zyx'.index(axis))  8.64 us
  transfers between devices with their start and end apart: 24, of which 13 were waited for; matrix products, arithmetic and copies ran while one was open for 8% of the time, Pallas kernels for 65%

profile of v1, /device:TPU:1, one launch (start us, length us, event | category | flops | bytes accessed | tf_op | source)
XLA Modules:
  0.0 395.6 jit_solution(2672576738431375572)
XLA Ops:
  1.5 4.7 %collective-permute-start = (bf16[1,1,1,64,384]{4,3,2,1,0:T(8,128)(2,1)S(1)}, bf16[1,1,1,64,384]{4,3,2,1,0:T(8,128)(2,1)S(1)}, u32[]{:S(2)}, u32[]{:S(2)}) collective-permute-start(bf16[1,1,1,64,384]{4,3,2,1,0:T(8,128)(2,1)S(1)} %get-tuple-element.14), channel_id=1, source_target_pairs={{0,16},{1,17},{2,18},{3,19},{4,20},{5,21},{6,22},{7,23},{8,24},{9,... | collective-permute-start | bytes 147464 | tf_op jit(solution)/shard_map/ppermute | solution.py:37
  6.2 2.7 collective-permute-start.6
  10.5 2.3 collective-permute-done.1
  14.8 2.5 collective-permute-start.12
  20.1 2.8 collective-permute-done.13
  23.0 2.8 collective-permute-start.14
  26.3 2.3 collective-permute-start.4
  28.7 4.1 %collective-permute-done.9 = bf16[1,4,2,64,384]{4,3,2,1,0:T(8,128)(2,1)S(1)} collective-permute-done((bf16[1,4,2,64,384]{4,3,2,1,0:T(8,128)(2,1)S(1)}, bf16[1,4,2,64,384]{4,3,2,1,0:T(8,128)(2,1)S(1)}, u32[]{:S(2)}, u32[]{:S(2)}) %collective-permute-start.9) | collective-permute-done | bytes 393248 | tf_op jit(solution)/shard_map/ppermute | solution.py:37
  33.0 2.6 collective-permute-done.15
  36.5 6.5 %collective-permute-done.4 = bf16[4,4,1,64,384]{4,3,2,1,0:T(8,128)(2,1)S(1)} collective-permute-done((bf16[4,4,1,64,384]{4,3,2,1,0:T(8,128)(2,1)S(1)}, bf16[4,4,1,64,384]{4,3,2,1,0:T(8,128)(2,1)S(1)}, u32[]{:S(2)}, u32[]{:S(2)}) %collective-permute-start.4) | collective-permute-done | bytes 786464 | tf_op jit(solution)/shard_map/ppermute | solution.py:37
  46.2 1.7 collective-permute-done.10
  50.1 255.9 %split_grads.1 = (bf16[4096,512]{1,0:T(8,128)(2,1)}, bf16[4096,512]{1,0:T(8,128)(2,1)}) custom-call(s32[4]{0:T(128)} %pad_add_fusion.where, bf16[8192,512]{1,0:T(8,128)(2,1)} %bitcast.46), custom_call_target="tpu_custom_call" | custom-call | tf_op jit(solution)/shard_map/split_grads/pallas_call | solution.py:89
  306.1 16.7 %collective-permute-start.19 = (bf16[4096,512]{1,0:T(8,128)(2,1)}, bf16[4096,512]{1,0:T(8,128)(2,1)}, u32[]{:S(2)}, u32[]{:S(2)}) collective-permute-start(bf16[4096,512]{1,0:T(8,128)(2,1)} %get-tuple-element.6), channel_id=1, source_target_pairs={{0,32},{1,33},{2,34},{3,35},{4,36},{5,37},{6,38},{7,39},{8,40},{9,... | collective-permute-start | bytes 12582920 | tf_op jit(solution)/shard_map/ppermute | solution.py:41
  324.2 2.5 pad_maximum_fusion.1
  328.4 4.3 %pad_maximum_fusion.own = bf16[4096,1024]{1,0:T(8,128)(2,1)} fusion(bf16[4096,256]{1,0:T(8,128)(2,1)S(1)} %bitcast.49, bf16[4096,384]{1,0:T(8,128)(2,1)S(1)} %bitcast.44, bf16[4096,384]{1,0:T(8,128)(2,1)S(1)} %bitcast.42), kind=kLoop, calls=%fused_computation | loop fusion | flops 25165824 | bytes 16777216 | tf_op jit(solution)/shard_map/concatenate | solution.py:185
  332.9 5.5 %fusion.1 = f32[256,512]{1,0:T(8,128)S(1)} fusion(bf16[4096,256]{1,0:T(8,128)(2,1)} %bitcast.50, bf16[4096,512]{1,0:T(8,128)(2,1)} %collective-permute-done.19, bf16[4096,512]{1,0:T(8,128)(2,1)} %get-tuple-element.5), kind=kOutput, calls=%fused_computation.39 | convolution fusion | flops 1082130432 | bytes 11010048 | tf_op jit(solution)/shard_map/dot_general | solution.py:181
  338.4 4.2 %fusion.3 = f32[384,512]{1,0:T(8,128)S(1)} fusion(bf16[4096,384]{1,0:T(8,128)(2,1)S(1)} %bitcast.43, bf16[4096,512]{1,0:T(8,128)(2,1)} %collective-permute-done.19, bf16[4096,512]{1,0:T(8,128)(2,1)S(1)} %copy-done.26), kind=kOutput, calls=%fused_computation.41 | convolution fusion | flops 1619001344 | bytes 12320768 | tf_op jit(solution)/shard_map/dot_general | solution.py:181
  342.6 4.0 %fusion.2 = f32[384,512]{1,0:T(8,128)S(1)} fusion(bf16[4096,384]{1,0:T(8,128)(2,1)S(1)} %bitcast.45, bf16[4096,512]{1,0:T(8,128)(2,1)} %collective-permute-done.19, bf16[4096,512]{1,0:T(8,128)(2,1)S(1)} %copy-done.26), kind=kOutput, calls=%fused_computation.40 | convolution fusion | flops 1619001344 | bytes 12320768 | tf_op jit(solution)/shard_map/dot_general | solution.py:181
  347.3 2.4 collective-permute-done.20
  351.3 9.0 %collective-permute-done.21 = bf16[256,512]{1,0:T(8,128)(2,1)S(1)} collective-permute-done((bf16[256,512]{1,0:T(8,128)(2,1)S(1)}, bf16[256,512]{1,0:T(8,128)(2,1)S(1)}, u32[]{:S(2)}, u32[]{:S(2)}) %collective-permute-start.21) | collective-permute-done | bytes 262176 | tf_op jit(solution)/shard_map/ppermute | solution.py:45
  360.4 2.5 divide_convert_fusion
  363.2 7.8 %collective-permute-done.22 = bf16[256,512]{1,0:T(8,128)(2,1)S(1)} collective-permute-done((bf16[256,512]{1,0:T(8,128)(2,1)S(1)}, bf16[256,512]{1,0:T(8,128)(2,1)S(1)}, u32[]{:S(2)}, u32[]{:S(2)}) %collective-permute-start.22) | collective-permute-done | bytes 262176 | tf_op jit(solution)/shard_map/ppermute | solution.py:45
  371.1 2.2 collective-permute-start.23
  375.1 20.3 %back_project.1 = bf16[8192,512]{1,0:T(8,128)(2,1)} custom-call(s32[4]{0:T(128)S(1)} %copy-done, bf16[4096,1024]{1,0:T(8,128)(2,1)} %pad_maximum_fusion.own, bf16[4096,1024]{1,0:T(8,128)(2,1)} %collective-permute-done.18.other, bf16[1024,512]{1,0:T(8,128)(2,1)S(1)} %bitcast.41), custom_call_target="tpu_custom_call" | custom-call | tf_op jit(solution)/shard_map/back_project/pallas_call | solution.py:147
  (115 shorter events, 21.9 us)
Async XLA Ops:
  1.5 7.4 %collective-permute-start = (bf16[1,1,1,64,384]{4,3,2,1,0:T(8,128)(2,1)S(1)}, bf16[1,1,1,64,384]{4,3,2,1,0:T(8,128)(2,1)S(1)}, u32[]{:S(2)}, u32[]{:S(2)}) collective-permute-start(bf16[1,1,1,64,384]{4,3,2,1,0:T(8,128)(2,1)S(1)} %get-tuple-element.14), channel_id=1, source_target_pairs={{0,16},{1,17},{2,18},{3,19},{4,20},{5,21},{6,22},{7,23},{8,24},{9,... | collective-permute-start | bytes 147464 | tf_op jit(solution)/shard_map/ppermute | solution.py:37
  6.2 4.2 %collective-permute-start.6 = (bf16[1,1,1,64,384]{4,3,2,1,0:T(8,128)(2,1)S(1)}, bf16[1,1,1,64,384]{4,3,2,1,0:T(8,128)(2,1)S(1)}, u32[]{:S(2)}, u32[]{:S(2)}) collective-permute-start(bf16[1,1,1,64,384]{4,3,2,1,0:T(8,128)(2,1)S(1)} %get-tuple-element.15), channel_id=1, source_target_pairs={{0,4},{1,5},{2,6},{3,7},{4,0},{5,1},{6,2},{7,3},{8,12},{9,13},{10,... | collective-permute-start | bytes 147464 | tf_op jit(solution)/shard_map/ppermute | solution.py:37
  8.9 3.8 collective-permute-start.1
  10.4 6.9 %collective-permute-start.7 = (bf16[1,2,1,64,384]{4,3,2,1,0:T(8,128)(2,1)S(1)}, bf16[1,2,1,64,384]{4,3,2,1,0:T(8,128)(2,1)S(1)}, u32[]{:S(2)}, u32[]{:S(2)}) collective-permute-start(bf16[1,2,1,64,384]{4,3,2,1,0:T(8,128)(2,1)S(1)} %pad_maximum_fusion.20), channel_id=1, source_target_pairs={{0,12},{1,13},{2,14},{3,15},{4,8},{5,9},{6,10},{7,11},{8,4},{9,5},... | collective-permute-start | bytes 294920 | tf_op jit(solution)/shard_map/ppermute | solution.py:37
  12.8 5.9 %collective-permute-start.2 = (bf16[4,1,1,64,384]{4,3,2,1,0:T(8,128)(2,1)S(1)}, bf16[4,1,1,64,384]{4,3,2,1,0:T(8,128)(2,1)S(1)}, u32[]{:S(2)}, u32[]{:S(2)}) collective-permute-start(bf16[4,1,1,64,384]{4,3,2,1,0:T(8,128)(2,1)S(1)} %pad_maximum_fusion.16), channel_id=1, source_target_pairs={{0,4},{1,5},{2,6},{3,7},{4,0},{5,1},{6,2},{7,3},{8,12},{9,13},{10,... | collective-permute-start | bytes 589832 | tf_op jit(solution)/shard_map/ppermute | solution.py:37
  14.8 4.0 %collective-permute-start.12 = (bf16[1,1,1,64,256]{4,3,2,1,0:T(8,128)(2,1)S(1)}, bf16[1,1,1,64,256]{4,3,2,1,0:T(8,128)(2,1)S(1)}, u32[]{:S(2)}, u32[]{:S(2)}) collective-permute-start(bf16[1,1,1,64,256]{4,3,2,1,0:T(8,128)(2,1)S(1)} %slice_bitcast_fusion.2), channel_id=1, source_target_pairs={{0,1},{1,0},{2,3},{3,2},{4,5},{5,4},{6,7},{7,6},{8,9},{9,8},{10,11... | collective-permute-start | bytes 98312 | tf_op jit(solution)/shard_map/ppermute | solution.py:37
  17.3 8.4 %collective-permute-start.8 = (bf16[1,4,1,64,384]{4,3,2,1,0:T(8,128)(2,1)S(1)}, bf16[1,4,1,64,384]{4,3,2,1,0:T(8,128)(2,1)S(1)}, u32[]{:S(2)}, u32[]{:S(2)}) collective-permute-start(bf16[1,4,1,64,384]{4,3,2,1,0:T(8,128)(2,1)S(1)} %pad_maximum_fusion.17), channel_id=1, source_target_pairs={{0,1},{1,0},{2,3},{3,2},{4,5},{5,4},{6,7},{7,6},{8,9},{9,8},{10,11... | collective-permute-start | bytes 589832 | tf_op jit(solution)/shard_map/ppermute | solution.py:37
  18.7 7.5 %collective-permute-start.3 = (bf16[4,2,1,64,384]{4,3,2,1,0:T(8,128)(2,1)S(1)}, bf16[4,2,1,64,384]{4,3,2,1,0:T(8,128)(2,1)S(1)}, u32[]{:S(2)}, u32[]{:S(2)}) collective-permute-start(bf16[4,2,1,64,384]{4,3,2,1,0:T(8,128)(2,1)S(1)} %pad_maximum_fusion.13), channel_id=1, source_target_pairs={{0,12},{1,13},{2,14},{3,15},{4,8},{5,9},{6,10},{7,11},{8,4},{9,5},... | collective-permute-start | bytes 1179656 | tf_op jit(solution)/shard_map/ppermute | solution.py:37
  18.8 4.1 %collective-permute-start.13 = (bf16[1,1,2,64,256]{4,3,2,1,0:T(8,128)(2,1)S(1)}, bf16[1,1,2,64,256]{4,3,2,1,0:T(8,128)(2,1)S(1)}, u32[]{:S(2)}, u32[]{:S(2)}) collective-permute-start(bf16[1,1,2,64,256]{4,3,2,1,0:T(8,128)(2,1)S(1)} %pad_maximum_fusion.21), channel_id=1, source_target_pairs={{0,3},{1,2},{2,1},{3,0},{4,7},{5,6},{6,5},{7,4},{8,11},{9,10},{10,... | collective-permute-start | bytes 196616 | tf_op jit(solution)/shard_map/ppermute | solution.py:37
  23.0 5.6 %collective-permute-start.14 = (bf16[1,1,4,64,256]{4,3,2,1,0:T(8,128)(2,1)S(1)}, bf16[1,1,4,64,256]{4,3,2,1,0:T(8,128)(2,1)S(1)}, u32[]{:S(2)}, u32[]{:S(2)}) collective-permute-start(bf16[1,1,4,64,256]{4,3,2,1,0:T(8,128)(2,1)S(1)} %pad_maximum_fusion.18), channel_id=1, source_target_pairs={{0,16},{1,17},{2,18},{3,19},{4,20},{5,21},{6,22},{7,23},{8,24},{9,... | collective-permute-start | bytes 393224 | tf_op jit(solution)/shard_map/ppermute | solution.py:37
  25.8 7.0 %collective-permute-start.9 = (bf16[1,4,2,64,384]{4,3,2,1,0:T(8,128)(2,1)S(1)}, bf16[1,4,2,64,384]{4,3,2,1,0:T(8,128)(2,1)S(1)}, u32[]{:S(2)}, u32[]{:S(2)}) collective-permute-start(bf16[1,4,2,64,384]{4,3,2,1,0:T(8,128)(2,1)S(1)} %pad_maximum_fusion.14), channel_id=1, source_target_pairs={{0,3},{1,2},{2,1},{3,0},{4,7},{5,6},{6,5},{7,4},{8,11},{9,10},{10,... | collective-permute-start | bytes 1179656 | tf_op jit(solution)/shard_map/ppermute | solution.py:37
  26.3 16.6 %collective-permute-start.4 = (bf16[4,4,1,64,384]{4,3,2,1,0:T(8,128)(2,1)S(1)}, bf16[4,4,1,64,384]{4,3,2,1,0:T(8,128)(2,1)S(1)}, u32[]{:S(2)}, u32[]{:S(2)}) collective-permute-start(bf16[4,4,1,64,384]{4,3,2,1,0:T(8,128)(2,1)S(1)} %pad_maximum_fusion.9), channel_id=1, source_target_pairs={{0,1},{1,0},{2,3},{3,2},{4,5},{5,4},{6,7},{7,6},{8,9},{9,8},{10,11... | collective-permute-start | bytes 2359304 | tf_op jit(solution)/shard_map/ppermute | solution.py:37
  28.6 7.0 %collective-permute-start.15 = (bf16[2,1,4,64,256]{4,3,2,1,0:T(8,128)(2,1)S(1)}, bf16[2,1,4,64,256]{4,3,2,1,0:T(8,128)(2,1)S(1)}, u32[]{:S(2)}, u32[]{:S(2)}) collective-permute-start(bf16[2,1,4,64,256]{4,3,2,1,0:T(8,128)(2,1)S(1)} %pad_maximum_fusion.15), channel_id=1, source_target_pairs={{0,80},{1,81},{2,82},{3,83},{4,84},{5,85},{6,86},{7,87},{8,88},{9,... | collective-permute-start | bytes 786440 | tf_op jit(solution)/shard_map/ppermute | solution.py:37
  32.9 14.9 %collective-permute-start.10 = (bf16[1,4,4,64,384]{4,3,2,1,0:T(8,128)(2,1)S(1)}, bf16[1,4,4,64,384]{4,3,2,1,0:T(8,128)(2,1)S(1)}, u32[]{:S(2)}, u32[]{:S(2)}) collective-permute-start(bf16[1,4,4,64,384]{4,3,2,1,0:T(8,128)(2,1)S(1)} %pad_maximum_fusion.10), channel_id=1, source_target_pairs={{0,16},{1,17},{2,18},{3,19},{4,20},{5,21},{6,22},{7,23},{8,24},{9,... | collective-permute-start | bytes 2359304 | tf_op jit(solution)/shard_map/ppermute | solution.py:37
  35.7 9.4 %collective-permute-start.16 = (bf16[4,1,4,64,256]{4,3,2,1,0:T(8,128)(2,1)S(1)}, bf16[4,1,4,64,256]{4,3,2,1,0:T(8,128)(2,1)S(1)}, u32[]{:S(2)}, u32[]{:S(2)}) collective-permute-start(bf16[4,1,4,64,256]{4,3,2,1,0:T(8,128)(2,1)S(1)} %pad_maximum_fusion.11), channel_id=1, source_target_pairs={{0,4},{1,5},{2,6},{3,7},{4,0},{5,1},{6,2},{7,3},{8,12},{9,13},{10,... | collective-permute-start | bytes 1572872 | tf_op jit(solution)/shard_map/ppermute | solution.py:37
  43.2 281.0 %collective-permute-start.5 = (bf16[4,4,2,64,384]{4,3,2,1,0:T(8,128)(2,1)S(1)}, bf16[4,4,2,64,384]{4,3,2,1,0:T(8,128)(2,1)}, u32[]{:S(2)}, u32[]{:S(2)}) collective-permute-start(bf16[4,4,2,64,384]{4,3,2,1,0:T(8,128)(2,1)S(1)} %pad_maximum_fusion.5), channel_id=1, source_target_pairs={{0,3},{1,2},{2,1},{3,0},{4,7},{5,6},{6,5},{7,4},{8,11},{9,10},{10,... | collective-permute-start | bytes 4718600 | tf_op jit(solution)/shard_map/ppermute | solution.py:37
  46.2 276.5 %collective-permute-start.17 = (bf16[4,2,4,64,256]{4,3,2,1,0:T(8,128)(2,1)}, bf16[4,2,4,64,256]{4,3,2,1,0:T(8,128)(2,1)}, u32[]{:S(2)}, u32[]{:S(2)}) collective-permute-start(bf16[4,2,4,64,256]{4,3,2,1,0:T(8,128)(2,1)} %pad_maximum_fusion.7), channel_id=1, source_target_pairs={{0,12},{1,13},{2,14},{3,15},{4,8},{5,9},{6,10},{7,11},{8,4},{9,5},... | collective-permute-start | bytes 3145736 | tf_op jit(solution)/shard_map/ppermute | solution.py:37
  49.4 277.3 %collective-permute-start.11 = (bf16[2,4,4,64,384]{4,3,2,1,0:T(8,128)(2,1)}, bf16[2,4,4,64,384]{4,3,2,1,0:T(8,128)(2,1)}, u32[]{:S(2)}, u32[]{:S(2)}) collective-permute-start(bf16[2,4,4,64,384]{4,3,2,1,0:T(8,128)(2,1)} %pad_maximum_fusion.6), channel_id=1, source_target_pairs={{0,80},{1,81},{2,82},{3,83},{4,84},{5,85},{6,86},{7,87},{8,88},{9,... | collective-permute-start | bytes 4718600 | tf_op jit(solution)/shard_map/ppermute | solution.py:37
  306.1 26.8 %collective-permute-start.19 = (bf16[4096,512]{1,0:T(8,128)(2,1)}, bf16[4096,512]{1,0:T(8,128)(2,1)}, u32[]{:S(2)}, u32[]{:S(2)}) collective-permute-start(bf16[4096,512]{1,0:T(8,128)(2,1)} %get-tuple-element.6), channel_id=1, source_target_pairs={{0,32},{1,33},{2,34},{3,35},{4,36},{5,37},{6,38},{7,39},{8,40},{9,... | collective-permute-start | bytes 12582920 | tf_op jit(solution)/shard_map/ppermute | solution.py:41
  332.7 42.4 %collective-permute-start.18 = (bf16[4096,1024]{1,0:T(8,128)(2,1)}, bf16[4096,1024]{1,0:T(8,128)(2,1)}, u32[]{:S(2)}, u32[]{:S(2)}) collective-permute-start(bf16[4096,1024]{1,0:T(8,128)(2,1)} %pad_maximum_fusion.own), channel_id=1, source_target_pairs={{0,32},{1,33},{2,34},{3,35},{4,36},{5,37},{6,38},{7,39},{8,40},{9,... | collective-permute-start | bytes 25165832 | tf_op jit(solution)/shard_map/ppermute | solution.py:41
  346.9 2.9 collective-permute-start.20
  351.2 9.1 %collective-permute-start.21 = (bf16[256,512]{1,0:T(8,128)(2,1)S(1)}, bf16[256,512]{1,0:T(8,128)(2,1)S(1)}, u32[]{:S(2)}, u32[]{:S(2)}) collective-permute-start(bf16[256,512]{1,0:T(8,128)(2,1)S(1)} %fusion), channel_id=1, source_target_pairs={{0,64},{1,65},{2,66},{3,67},{4,68},{5,69},{6,70},{7,71},{8,72},{9,... | collective-permute-start | bytes 786440 | tf_op jit(solution)/shard_map/ppermute | solution.py:45
  362.9 8.1 %collective-permute-start.22 = (bf16[256,512]{1,0:T(8,128)(2,1)S(1)}, bf16[256,512]{1,0:T(8,128)(2,1)S(1)}, u32[]{:S(2)}, u32[]{:S(2)}) collective-permute-start(bf16[256,512]{1,0:T(8,128)(2,1)S(1)} %get-tuple-element.7), channel_id=1, source_target_pairs={{0,64},{1,65},{2,66},{3,67},{4,68},{5,69},{6,70},{7,71},{8,72},{9,... | collective-permute-start | bytes 786440 | tf_op jit(solution)/shard_map/ppermute | solution.py:45
  371.1 3.7 collective-permute-start.23
  (27 other events, 416.1 us)

commit v2 on v0

v2 whole, which is shorter than its diff:
```python
import functools
import math

import jax
import jax.numpy as jnp
from jax import lax
from jax.experimental import pallas as pl
from jax.experimental.pallas import tpu as pltpu
from jax.sharding import PartitionSpec as P

first_fix = 1.0 - math.exp(1000.0 * math.log(0.9))
second_fix = 1.0 - math.exp(1000.0 * math.log(0.999))

BOTH = ("dp", "fsdp")
ORDER = ((0, 1, 3, 2), (0, 3, 1, 2))
STREAMS = ((0, 384, "x"), (384, 768, "y"), (768, 1024, "z"))
MIB = 1024 * 1024


def linear(c, z, y, x):
    return (((z // 2) * 2 + c) * 2 + z % 2) * 16 + y * 4 + x


def pairs(partner):
    return [
        (linear(c, z, y, x), linear(*partner(c, z, y, x)))
        for c in range(2)
        for z in range(4)
        for y in range(4)
        for x in range(4)
    ]


def exchange(value, axis, step):
    def partner(c, z, y, x):
        t = ORDER[c][1] if step == 0 else ORDER[1 - c][1]
        return c, z ^ t if axis == "z" else z, y ^ t if axis == "y" else y, x ^ t if axis == "x" else x

    return lax.ppermute(value, BOTH, pairs(partner))


def swap_core(value):
    return lax.ppermute(value, BOTH, pairs(lambda c, z, y, x: (1 - c, z, y, x)))


def swap_far(value):
    return lax.ppermute(value, BOTH, pairs(lambda c, z, y, x: (c, z ^ 2, y, x)))


def grow(held, axis, step):
    return jnp.concatenate([held, exchange(held, axis, step)], axis="zyx".index(axis))


def together(*values):
    return lax.optimization_barrier(values)


def offset(of_core, position):
    one = jnp.where(of_core == 0, 1, 3)
    return jnp.where(position == 0, 0, jnp.where(position == 1, one, jnp.where(position == 2, 4 - one, 2)))


def layer(of_core, z, position):
    zz = z ^ offset(of_core, position)
    return ((zz // 2) * 2 + of_core) * 2 + zz % 2


def sum_kernel(where, grads, theirs, out, mine, other, sems):
    core, z, y, x = where[0], where[1], where[2], where[3]

    def load(i):
        rows = pl.ds(pl.multiple_of(layer(core, z, i) * 1024, 1024), 1024)
        return [
            pltpu.make_async_copy(grads.at[rows], mine.at[i % 2], sems.at[0, i % 2]),
            pltpu.make_async_copy(theirs.at[rows], other.at[i % 2], sems.at[1, i % 2]),
        ]

    for i in range(2):
        for copy in load(i):
            copy.start()
    for i in range(4):
        for copy in load(i):
            copy.wait()
        for b in range(4):
            for c in range(4):
                rows = pl.ds(pl.multiple_of((y ^ offset(core, b)) * 256 + (x ^ offset(core, c)) * 64, 64), 64)
                both = mine[i % 2, rows].astype(jnp.float32) + other[i % 2, rows].astype(jnp.float32)
                out[i, b, c] = both.astype(jnp.bfloat16)
        if i < 2:
            for copy in load(i + 2):
                copy.start()


def sum_grads(where, grads, theirs):
    columns = grads.shape[1]
    far = pl.BlockSpec(memory_space=pltpu.HBM)
    return pl.pallas_call(
        sum_kernel,
        out_shape=jax.ShapeDtypeStruct((4, 4, 4, 64, columns), jnp.bfloat16),
        in_specs=[pl.BlockSpec(memory_space=pltpu.SMEM), far, far],
        out_specs=pl.BlockSpec(memory_space=pltpu.VMEM),
        scratch_shapes=[
            pltpu.VMEM((2, 1024, columns), jnp.bfloat16),
            pltpu.VMEM((2, 1024, columns), jnp.bfloat16),
            pltpu.SemaphoreType.DMA((2, 2)),
        ],
        compiler_params=pltpu.CompilerParams(vmem_limit_bytes=40 * MIB),
        cost_estimate=pl.CostEstimate(flops=4096 * columns, bytes_accessed=24576 * columns, transcendentals=0),
        name="sum_grads",
    )(where, grads, theirs)


def project_kernel(late, summed, *refs):
    pieces, refs = refs[:3], refs[3:]
    if late:
        where, before, partial, sent, one, two, three, sems, out_sem = refs
    else:
        partial, one, two, three, sems = refs
    scratch = (one, two, three)
    loads = [
        [pltpu.make_async_copy(p.at[a], v.at[a], sems.at[s, a]) for a in range(p.shape[0])]
        for s, (p, v) in enumerate(zip(pieces, scratch))
    ]
    first = 2 if late else 0
    order = [(s, a) for s in range(3) for a in range(scratch[s].shape[0])]
    for s, a in order:
        loads[s][a].start()
    for s, a in order:
        loads[s][a].wait()
        low, high, axis = STREAMS[s]
        if axis == "x":
            rows = summed[a, :, first : first + 2]
        elif axis == "y":
            rows = summed[a, first : first + 2]
        else:
            rows = summed[first + a]
        depth = scratch[s].shape[1] * scratch[s].shape[2] * 64
        product = lax.dot_general(
            scratch[s][a].reshape(depth, high - low),
            rows.reshape(depth, rows.shape[-1]),
            (((0,), (0,)), ((), ())),
            preferred_element_type=jnp.float32,
        )
        if a > 0:
            partial[low:high] += product
        elif late:
            partial[low:high] = before[low:high] + product
        else:
            partial[low:high] = product
    if late:
        share = sent.shape[1]
        for far in range(2):
            row = pl.multiple_of((far * 2 + 1 - where[0]) * share, share)
            pltpu.make_async_copy(partial.at[pl.ds(row, share)], sent.at[far], out_sem).start()
        pltpu.make_async_copy(sent, sent, out_sem).wait()


def project(summed, pieces, where=None, before=None):
    columns = summed.shape[-1]
    late = before is not None
    anywhere, inside = pl.BlockSpec(memory_space=pl.ANY), pl.BlockSpec(memory_space=pltpu.VMEM)
    result = jax.ShapeDtypeStruct((1024, columns), jnp.float32)
    return pl.pallas_call(
        functools.partial(project_kernel, late),
        out_shape=(result, jax.ShapeDtypeStruct((2, 256, columns), jnp.float32)) if late else result,
        in_specs=[inside] + [anywhere] * 3 + [pl.BlockSpec(memory_space=pltpu.SMEM), inside] * late,
        out_specs=(inside, anywhere) if late else inside,
        scratch_shapes=[pltpu.VMEM(piece.shape, jnp.bfloat16) for piece in pieces]
        + [pltpu.SemaphoreType.DMA((3, 4))]
        + [pltpu.SemaphoreType.DMA] * late,
        compiler_params=pltpu.CompilerParams(vmem_limit_bytes=32 * MIB),
        cost_estimate=pl.CostEstimate(
            flops=summed.size * 1024, bytes_accessed=2 * summed.size + 4 * MIB, transcendentals=0
        ),
        name="project_late" if late else "project",
    )(summed, *pieces, *([where, before] if late else []))


def chip_kernel(where, partial, received, kept, sent):
    core, far = where[0], where[1] // 2
    share = kept.shape[0]

    def total(f):
        return partial[pl.ds(pl.multiple_of((f * 2 + core) * share, share), share)] + received[f]

    sent[...] = total(1 - far).astype(jnp.bfloat16)
    kept[...] = total(far)


def add_cores(where, partial, received):
    columns = partial.shape[1]
    inside = pl.BlockSpec(memory_space=pltpu.VMEM)
    return pl.pallas_call(
        chip_kernel,
        out_shape=(
            jax.ShapeDtypeStruct((256, columns), jnp.float32),
            jax.ShapeDtypeStruct((256, columns), jnp.bfloat16),
        ),
        in_specs=[pl.BlockSpec(memory_space=pltpu.SMEM), inside, inside],
        out_specs=(inside, inside),
        compiler_params=pltpu.CompilerParams(vmem_limit_bytes=16 * MIB),
        name="add_cores",
    )(where, partial, received)


def adam(kept, received, first_moment, second_moment):
    projected = (kept + received.astype(jnp.float32)) * (1.0 / 4)
    new_first = 0.9 * first_moment + 0.1 * projected
    new_second = 0.999 * second_moment + 0.001 * projected * projected
    return new_first, new_second


def direction_kernel(kept, received, first_moment, second_moment, out):
    new_first, new_second = adam(kept[...], received[...], first_moment[...], second_moment[...])
    out[...] = (new_first / first_fix / (jnp.sqrt(new_second / second_fix) + 1e-08)).astype(jnp.bfloat16)


def direct(*operands):
    inside = pl.BlockSpec(memory_space=pltpu.VMEM)
    return pl.pallas_call(
        direction_kernel,
        out_shape=jax.ShapeDtypeStruct(operands[0].shape, jnp.bfloat16),
        in_specs=[inside] * 4,
        out_specs=inside,
        compiler_params=pltpu.CompilerParams(vmem_limit_bytes=16 * MIB),
        name="direction",
    )(*operands)


SLOTS = 3


def update_kernel(where, *refs):
    bases, quarters, refs = (refs[:6], refs[6:12]), refs[12:16], refs[16:]
    out, direction, block, result, quarter_sem, in_sems, out_sems = refs
    core, z, y, x = where[0], where[1], where[2], where[3]

    def load(t):
        side, a = t // 4, t % 4
        slot = t % SLOTS
        for s, (low, high, axis) in enumerate(STREAMS):
            held, got = bases[side][2 * s], bases[side][2 * s + 1]
            if axis == "x":
                jobs = [(held, a, slice(None), pl.ds(0, 2)), (got, a, slice(None), pl.ds(2, 2))]
            elif axis == "y":
                jobs = [(held, a, pl.ds(0, 2), slice(None)), (got, a, pl.ds(2, 2), slice(None))]
            else:
                jobs = [(held if a < 2 else got, a % 2, slice(None), slice(None))]
            for source, index, b, c in jobs:
                pltpu.make_async_copy(
                    source.at[index], block.at[slot, b, c, :, pl.ds(low, high - low)], in_sems.at[slot]
                ).start()

    def drain(turn):
        pltpu.make_async_copy(result.at[turn], result.at[turn], out_sems.at[turn]).wait()

    far, share = z // 2, quarters[0].shape[0]
    for k, quarter in enumerate(quarters):
        place = (far ^ (k // 2)) * 2 + (core ^ (k % 2))
        rows = pl.ds(pl.multiple_of(place * share, share), share)
        pltpu.make_async_copy(quarter, direction.at[rows], quarter_sem).start()
    for t in range(SLOTS):
        load(t)
    pltpu.make_async_copy(direction, direction, quarter_sem).wait()
    for t in range(8):
        side, a = t // 4, t % 4
        of_core = core if side == 0 else 1 - core
        slot, turn = t % SLOTS, t % 2
        pltpu.make_async_copy(block.at[slot], block.at[slot], in_sems.at[slot]).wait()
        if t >= 2:
            drain(turn)
        result[turn] = jnp.dot(
            block[slot].reshape(1024, block.shape[-1]), direction[...], preferred_element_type=jnp.float32
        ).astype(jnp.bfloat16)
        if t + SLOTS < 8:
            load(t + SLOTS)
        base = layer(of_core, z, a) * 1024
        for b in range(4):
            for c in range(4):
                row = pl.multiple_of(base + (y ^ offset(of_core, b)) * 256 + (x ^ offset(of_core, c)) * 64, 64)
                pltpu.make_async_copy(
                    result.at[turn, pl.ds((b * 4 + c) * 64, 64)], out.at[pl.ds(row, 64)], out_sems.at[turn]
                ).start()
    drain(0)
    drain(1)


def back_project(where, bases, quarters):
    share, columns = quarters[0].shape
    rank = 4 * share
    rows = 2 * 4096
    anywhere = pl.BlockSpec(memory_space=pl.ANY)
    return pl.pallas_call(
        update_kernel,
        out_shape=jax.ShapeDtypeStruct((rows, columns), jnp.bfloat16),
        in_specs=[pl.BlockSpec(memory_space=pltpu.SMEM)] + [anywhere] * 16,
        out_specs=anywhere,
        scratch_shapes=[
            pltpu.VMEM((rank, columns), jnp.bfloat16),
            pltpu.VMEM((SLOTS, 4, 4, 64, rank), jnp.bfloat16),
            pltpu.VMEM((2, 1024, columns), jnp.bfloat16),
            pltpu.SemaphoreType.DMA,
            pltpu.SemaphoreType.DMA((SLOTS,)),
            pltpu.SemaphoreType.DMA((2,)),
        ],
        compiler_params=pltpu.CompilerParams(vmem_limit_bytes=32 * MIB),
        cost_estimate=pl.CostEstimate(
            flops=2 * rows * rank * columns, bytes_accessed=2 * rows * (rank + columns), transcendentals=0
        ),
        name="back_project",
    )(where, *bases, *quarters)


def local(grads, basis, first_moment, second_moment):
    dp, fsdp = lax.axis_index("dp"), lax.axis_index("fsdp")
    far, core = dp // 2, dp % 2
    z, y, x = far * 2 + fsdp // 16, (fsdp // 4) % 4, fsdp % 4
    where = jnp.stack([core, z, y, x]).astype(jnp.int32)

    whole = grads[0]
    columns = whole.shape[1]
    theirs = swap_core(whole)
    held = grow(grow(basis[None, None, None], "x", 0), "y", 0)
    wide, narrow = held[..., :768], held[..., 768:]
    wide, narrow = together(grow(wide, "z", 0), grow(narrow, "x", 1))
    wide, narrow = together(grow(wide, "z", 1), grow(narrow, "y", 1))
    halves = together(grow(wide[..., :384], "y", 1), grow(wide[..., 384:], "x", 1), grow(narrow, "z", 0))
    got = [exchange(half, axis, 1) for half, (_, _, axis) in zip(halves, STREAMS)]
    summed = sum_grads(where, whole, theirs)
    partial, sent = project(summed, got, where, project(summed, halves))

    kept, sent = add_cores(where, partial, swap_core(sent))
    received = swap_far(sent)
    direction = direct(kept, received, first_moment, second_moment)
    new_first, new_second = adam(kept, received, first_moment, second_moment)

    bases = []
    for half, late in zip(halves, got):
        bases += [half, late]
    bases += [swap_core(piece) for piece in bases]
    distant = swap_far(direction)
    update = back_project(where, bases, (direction, swap_core(direction), distant, swap_core(distant)))
    return (update, new_first, new_second)


def solution(mesh):
    return jax.shard_map(
        local,
        mesh=mesh,
        in_specs=(P("dp", None, "fsdp"), P(("dp", "fsdp"), None), P("dp", "fsdp"), P("dp", "fsdp")),
        out_specs=(P(None, "fsdp"), P("dp", "fsdp"), P("dp", "fsdp")),
        check_vma=False,
    )
```

time: 472 us -> 129 us (0.27)
  waiting for transfers between devices: 413 us -> 53.4 us
  starting transfers between devices: 0.12 us -> 35.6 us
  matrix products: 30.5 us -> 0 us
  Pallas kernels: 0 us -> 30.2 us
  between operations: 13.8 us -> 0.94 us
  local copies, waits for them, and re-layouts: 11.9 us -> 3.71 us
    all_gather x2 -> x0, waiting for transfers between devices: 352 us -> none  [the longest x1 332 us: local(): whole_basis = lax.all_gather(basis, ('dp', 'fsdp'), axis=0, tiled=True)]
    psum x1 -> x0, waiting for transfers between devices: 59.6 us -> none  [local(): summed = lax.psum(partial_value, 'dp')]
    ppermute x0 -> x24, waiting for transfers between devices: none -> 53.4 us  [the longest x12 37.3 us: exchange(): return lax.ppermute(value, BOTH, pairs(partner))]
    ppermute x0 -> x24, starting transfers between devices: none -> 35.6 us  [the longest x12 15.1 us: exchange(): return lax.ppermute(value, BOTH, pairs(partner))]
    dot_general x2 -> x0, matrix products: 30.5 us -> none  [the longest x1 15.8 us: local(): lax.dot_general(whole_basis, local_grad, (((0,), (0,)), ((), ())), prefer...]
    pallas_call x0 -> x6, Pallas kernels: none -> 30.2 us  [the longest x1 14.8 us: back_project(): pl.pallas_call(update_kernel, out_shape=jax.ShapeDtypeStruct((rows, colum...]
    unnamed x5 -> x8, local copies, waits for them, and re-layouts: 11.9 us -> 3.4 us
  transfers between devices with their start and end apart: 3 -> 24, of which waited for: 3 -> 16; matrix products, arithmetic and copies ran while one was open for 0% -> 4% of each run, Pallas kernels for 0% -> 8%
where the time goes in v2:
time: 129 us
  waiting for transfers between devices  53.4 us (41%)
  starting transfers between devices  35.6 us (28%)
  Pallas kernels  30.2 us (23%)
  other arithmetic  4.89 us (4%)
  local copies, waits for them, and re-layouts  3.71 us (3%)
    ppermute x12, waiting for transfers between devices, exchange(): return lax.ppermute(value, BOTH, pairs(partner))  37.3 us
    ppermute x12, starting transfers between devices, exchange(): return lax.ppermute(value, BOTH, pairs(partner))  15.1 us
    pallas_call x1, Pallas kernels, back_project(): pl.pallas_call(update_kernel, out_shape=jax.ShapeDtypeStruct((rows, colum...  14.8 us
    ppermute x10, starting transfers between devices, swap_core(): return lax.ppermute(value, BOTH, pairs(lambda c, z, y, x: (1 - c, z, y, x)))  13 us
    ppermute x2, waiting for transfers between devices, swap_far(): return lax.ppermute(value, BOTH, pairs(lambda c, z, y, x: (c, z ^ 2, y, x)))  12.7 us
    pallas_call x2, Pallas kernels, project(): pl.pallas_call(functools.partial(project_kernel, late), out_shape=(result...  10.3 us
    ppermute x2, starting transfers between devices, swap_far(): return lax.ppermute(value, BOTH, pairs(lambda c, z, y, x: (c, z ^ 2, y, x)))  7.46 us
    pallas_call x1, Pallas kernels, sum_grads(): pl.pallas_call(sum_kernel, out_shape=jax.ShapeDtypeStruct((4, 4, 4, 64, c...  4.07 us
  transfers between devices with their start and end apart: 24, of which 16 were waited for; matrix products, arithmetic and copies ran while one was open for 4% of the time, Pallas kernels for 8%

profile of v2, /device:TPU:1, one launch (start us, length us, event | category | flops | bytes accessed | tf_op | source)
XLA Modules:
  0.0 128.7 jit_solution(4258326587938658542)
XLA Ops:
  2.1 2.6 %collective-permute-start = (bf16[1,1,1,64,1024]{4,3,2,1,0:T(8,128)(2,1)}, bf16[1,1,1,64,1024]{4,3,2,1,0:T(8,128)(2,1)S(1)}, u32[]{:S(2)}, u32[]{:S(2)}) collective-permute-start(bf16[1,1,1,64,1024]{4,3,2,1,0:T(8,128)(2,1)} %bitcast.8), channel_id=1, source_target_pairs={{0,1},{1,0},{2,3},{3,2},{4,5},{5,4},{6,7},{7,6},{8,9},{9,8},{10,11... | collective-permute-start | bytes 393224 | tf_op jit(solution)/shard_map/ppermute | solution.py:39
  4.7 2.7 %collective-permute-done = bf16[1,1,1,64,1024]{4,3,2,1,0:T(8,128)(2,1)S(1)} collective-permute-done((bf16[1,1,1,64,1024]{4,3,2,1,0:T(8,128)(2,1)}, bf16[1,1,1,64,1024]{4,3,2,1,0:T(8,128)(2,1)S(1)}, u32[]{:S(2)}, u32[]{:S(2)}) %collective-permute-start) | collective-permute-done | bytes 131104 | tf_op jit(solution)/shard_map/ppermute | solution.py:39
  8.3 2.9 %collective-permute-start.1 = (bf16[1,1,2,64,1024]{4,3,2,1,0:T(8,128)(2,1)S(1)}, bf16[1,1,2,64,1024]{4,3,2,1,0:T(8,128)(2,1)S(1)}, u32[]{:S(2)}, u32[]{:S(2)}) collective-permute-start(bf16[1,1,2,64,1024]{4,3,2,1,0:T(8,128)(2,1)S(1)} %pad_maximum_fusion.7), channel_id=1, source_target_pairs={{0,4},{1,5},{2,6},{3,7},{4,0},{5,1},{6,2},{7,3},{8,12},{9,13},{10,... | collective-permute-start | bytes 786440 | tf_op jit(solution)/shard_map/ppermute | solution.py:39
  11.2 3.8 %collective-permute-done.1 = bf16[1,1,2,64,1024]{4,3,2,1,0:T(8,128)(2,1)S(1)} collective-permute-done((bf16[1,1,2,64,1024]{4,3,2,1,0:T(8,128)(2,1)S(1)}, bf16[1,1,2,64,1024]{4,3,2,1,0:T(8,128)(2,1)S(1)}, u32[]{:S(2)}, u32[]{:S(2)}) %collective-permute-start.1) | collective-permute-done | bytes 262176 | tf_op jit(solution)/shard_map/ppermute | solution.py:39
  16.0 3.8 %collective-permute-start.2 = (bf16[1,2,2,64,768]{4,3,2,1,0:T(8,128)(2,1)S(1)}, bf16[1,2,2,64,768]{4,3,2,1,0:T(8,128)(2,1)S(1)}, u32[]{:S(2)}, u32[]{:S(2)}) collective-permute-start(bf16[1,2,2,64,768]{4,3,2,1,0:T(8,128)(2,1)S(1)} %slice.16), channel_id=1, source_target_pairs={{0,16},{1,17},{2,18},{3,19},{4,20},{5,21},{6,22},{7,23},{8,24},{9,... | collective-permute-start | bytes 1179656 | tf_op jit(solution)/shard_map/ppermute | solution.py:39
  20.2 3.6 %collective-permute-done.3 = bf16[1,2,2,64,256]{4,3,2,1,0:T(8,128)(2,1)S(1)} collective-permute-done((bf16[1,2,2,64,256]{4,3,2,1,0:T(8,128)(2,1)S(1)}, bf16[1,2,2,64,256]{4,3,2,1,0:T(8,128)(2,1)S(1)}, u32[]{:S(2)}, u32[]{:S(2)}) %collective-permute-start.3) | collective-permute-done | bytes 131104 | tf_op jit(solution)/shard_map/ppermute | solution.py:39
  25.6 5.2 %collective-permute-done.5 = bf16[1,2,4,64,256]{4,3,2,1,0:T(8,128)(2,1)S(1)} collective-permute-done((bf16[1,2,4,64,256]{4,3,2,1,0:T(8,128)(2,1)S(1)}, bf16[1,2,4,64,256]{4,3,2,1,0:T(8,128)(2,1)S(1)}, u32[]{:S(2)}, u32[]{:S(2)}) %collective-permute-start.5) | collective-permute-done | bytes 262176 | tf_op jit(solution)/shard_map/ppermute | solution.py:39
  30.8 5.5 %collective-permute-done.4 = bf16[2,2,2,64,768]{4,3,2,1,0:T(8,128)(2,1)S(1)} collective-permute-done((bf16[2,2,2,64,768]{4,3,2,1,0:T(8,128)(2,1)S(1)}, bf16[2,2,2,64,768]{4,3,2,1,0:T(8,128)(2,1)S(1)}, u32[]{:S(2)}, u32[]{:S(2)}) %collective-permute-start.4) | collective-permute-done | bytes 786464 | tf_op jit(solution)/shard_map/ppermute | solution.py:39
  37.1 2.7 %collective-permute-start.8 = (bf16[1,4,4,64,256]{4,3,2,1,0:T(8,128)(2,1)S(1)}, bf16[1,4,4,64,256]{4,3,2,1,0:T(8,128)(2,1)S(1)}, u32[]{:S(2)}, u32[]{:S(2)}) collective-permute-start(bf16[1,4,4,64,256]{4,3,2,1,0:T(8,128)(2,1)S(1)} %pad_maximum_fusion.6), channel_id=1, source_target_pairs={{0,16},{1,17},{2,18},{3,19},{4,20},{5,21},{6,22},{7,23},{8,24},{9,... | collective-permute-start | bytes 1572872 | tf_op jit(solution)/shard_map/ppermute | solution.py:39
  40.1 6.5 %collective-permute-done.8 = bf16[1,4,4,64,256]{4,3,2,1,0:T(8,128)(2,1)S(1)} collective-permute-done((bf16[1,4,4,64,256]{4,3,2,1,0:T(8,128)(2,1)S(1)}, bf16[1,4,4,64,256]{4,3,2,1,0:T(8,128)(2,1)S(1)}, u32[]{:S(2)}, u32[]{:S(2)}) %collective-permute-start.8) | collective-permute-done | bytes 524320 | tf_op jit(solution)/shard_map/ppermute | solution.py:39
  48.1 2.8 %collective-permute-done.6 = bf16[4,2,2,64,384]{4,3,2,1,0:T(8,128)(2,1)S(1)} collective-permute-done((bf16[4,2,2,64,384]{4,3,2,1,0:T(8,128)(2,1)S(1)}, bf16[4,2,2,64,384]{4,3,2,1,0:T(8,128)(2,1)S(1)}, u32[]{:S(2)}, u32[]{:S(2)}) %collective-permute-start.6) | collective-permute-done | bytes 786464 | tf_op jit(solution)/shard_map/ppermute | solution.py:39
  52.7 3.4 %copy-done = bf16[1,8192,512]{2,1,0:T(8,128)(2,1)S(1)} copy-done((bf16[1,8192,512]{2,1,0:T(8,128)(2,1)S(1)}, bf16[1,8192,512]{2,1,0:T(8,128)(2,1)}, u32[]{:S(2)}) %copy-start) | copy-done | bytes 8388632
  56.1 4.1 %sum_grads.1.summed = bf16[4,4,4,64,512]{4,3,2,1,0:T(8,128)(2,1)S(1)} custom-call(s32[4]{0:T(128)S(1)} %pad_add_fusion.where.refs_3_, bf16[8192,512]{1,0:T(8,128)(2,1)S(1)} %bitcast.7, bf16[8192,512]{1,0:T(8,128)(2,1)} %collective-permute-done.18.theirs), custom_call_target="tpu_custom_call" | custom-call | flops 2097152 | bytes 12582912 | tf_op jit(solution)/shard_map/sum_grads/pallas_call | solution.py:97
  60.2 5.0 %project.1.refs_4_ = f32[1024,512]{1,0:T(8,128)S(1)} custom-call(bf16[4,4,4,64,512]{4,3,2,1,0:T(8,128)(2,1)S(1)} %sum_grads.1.summed, bf16[4,4,2,64,384]{4,3,2,1,0:T(8,128)(2,1)S(1)} %pad_maximum_fusion.1.refs_0_, bf16[4,2,4,64,384]{4,3,2,1,0:T(8,128)(2,1)S(1)} %pad_maximum_fusion.2.refs_1_.refs_2_, bf16[2,4,4,64,256]{4,3,2,1,0:T(8,128)(2,1)} %pad_maximum_fusion.3.refs_2_.refs_4_), custom_call_target="tpu_custom_call" | custom-call | flops 2147483648 | bytes 8388608 | tf_op jit(solution)/shard_map/project/pallas_call | solution.py:163
  65.2 1.7 %collective-permute-done.11.refs_2_.refs_5_ = bf16[2,4,4,64,256]{4,3,2,1,0:T(8,128)(2,1)} collective-permute-done((bf16[2,4,4,64,256]{4,3,2,1,0:T(8,128)(2,1)}, bf16[2,4,4,64,256]{4,3,2,1,0:T(8,128)(2,1)}, u32[]{:S(2)}, u32[]{:S(2)}) %collective-permute-start.11) | collective-permute-done | bytes 1048608 | tf_op jit(solution)/shard_map/ppermute | solution.py:39
  66.9 3.9 %collective-permute-done.10.refs_1_.refs_3_ = bf16[4,2,4,64,384]{4,3,2,1,0:T(8,128)(2,1)} collective-permute-done((bf16[4,2,4,64,384]{4,3,2,1,0:T(8,128)(2,1)S(1)}, bf16[4,2,4,64,384]{4,3,2,1,0:T(8,128)(2,1)}, u32[]{:S(2)}, u32[]{:S(2)}) %collective-permute-start.10) | collective-permute-done | bytes 1572896 | tf_op jit(solution)/shard_map/ppermute | solution.py:39
  71.1 5.3 %project_late.1 = (f32[1024,512]{1,0:T(8,128)S(1)}, f32[2,256,512]{2,1,0:T(8,128)S(1)}) custom-call(bf16[4,4,4,64,512]{4,3,2,1,0:T(8,128)(2,1)S(1)} %sum_grads.1.summed, bf16[4,4,2,64,384]{4,3,2,1,0:T(8,128)(2,1)} %collective-permute-done.9.refs_0_.refs_1_, bf16[4,2,4,64,384]{4,3,2,1,0:T(8,128)(2,1)} %collective-permute-done.10.refs_1_.refs_3_, ...), custom_call_target="tpu_custom_call" | custom-call | flops 2147483648 | bytes 8388608 | tf_op jit(solution)/shard_map/project_late/pallas_call | solution.py:163
  76.4 8.3 %collective-permute-start.19 = (f32[2,256,512]{2,1,0:T(8,128)S(1)}, f32[2,256,512]{2,1,0:T(8,128)S(1)}, u32[]{:S(2)}, u32[]{:S(2)}) collective-permute-start(f32[2,256,512]{2,1,0:T(8,128)S(1)} %get-tuple-element.22), channel_id=1, source_target_pairs={{0,32},{1,33},{2,34},{3,35},{4,36},{5,37},{6,38},{7,39},{8,40},{9,... | collective-permute-start | bytes 3145736 | tf_op jit(solution)/shard_map/ppermute | solution.py:43
  85.8 1.8 %collective-permute-done.19.received = f32[2,256,512]{2,1,0:T(8,128)S(1)} collective-permute-done((f32[2,256,512]{2,1,0:T(8,128)S(1)}, f32[2,256,512]{2,1,0:T(8,128)S(1)}, u32[]{:S(2)}, u32[]{:S(2)}) %collective-permute-start.19) | collective-permute-done | bytes 1048608 | tf_op jit(solution)/shard_map/ppermute | solution.py:43
  90.1 4.4 %collective-permute-start.20 = (bf16[256,512]{1,0:T(8,128)(2,1)S(1)}, bf16[256,512]{1,0:T(8,128)(2,1)S(1)}, u32[]{:S(2)}, u32[]{:S(2)}) collective-permute-start(bf16[256,512]{1,0:T(8,128)(2,1)S(1)} %get-tuple-element.24), channel_id=1, source_target_pairs={{0,64},{1,65},{2,66},{3,67},{4,68},{5,69},{6,70},{7,71},{8,72},{9,... | collective-permute-start | bytes 786440 | tf_op jit(solution)/shard_map/ppermute | solution.py:47
  94.5 6.5 %collective-permute-done.20.received = bf16[256,512]{1,0:T(8,128)(2,1)S(1)} collective-permute-done((bf16[256,512]{1,0:T(8,128)(2,1)S(1)}, bf16[256,512]{1,0:T(8,128)(2,1)S(1)}, u32[]{:S(2)}, u32[]{:S(2)}) %collective-permute-start.20) | collective-permute-done | bytes 262176 | tf_op jit(solution)/shard_map/ppermute | solution.py:47
  102.2 3.0 %collective-permute-start.22 = (bf16[256,512]{1,0:T(8,128)(2,1)S(1)}, bf16[256,512]{1,0:T(8,128)(2,1)S(1)}, u32[]{:S(2)}, u32[]{:S(2)}) collective-permute-start(bf16[256,512]{1,0:T(8,128)(2,1)S(1)} %direction.1.refs_12_), channel_id=1, source_target_pairs={{0,64},{1,65},{2,66},{3,67},{4,68},{5,69},{6,70},{7,71},{8,72},{9,... | collective-permute-start | bytes 786440 | tf_op jit(solution)/shard_map/ppermute | solution.py:47
  105.5 6.2 %collective-permute-done.22.refs_14_ = bf16[256,512]{1,0:T(8,128)(2,1)S(1)} collective-permute-done((bf16[256,512]{1,0:T(8,128)(2,1)S(1)}, bf16[256,512]{1,0:T(8,128)(2,1)S(1)}, u32[]{:S(2)}, u32[]{:S(2)}) %collective-permute-start.22) | collective-permute-done | bytes 262176 | tf_op jit(solution)/shard_map/ppermute | solution.py:47
  113.7 14.8 %back_project.1 = bf16[8192,512]{1,0:T(8,128)(2,1)} custom-call(s32[4]{0:T(128)S(1)} %pad_add_fusion.where.refs_3_, bf16[4,4,2,64,384]{4,3,2,1,0:T(8,128)(2,1)S(1)} %pad_maximum_fusion.1.refs_0_, bf16[4,4,2,64,384]{4,3,2,1,0:T(8,128)(2,1)} %collective-permute-done.9.refs_0_.refs_1_, bf16[4,2,4,64,384]{4,3,2,1,0:T(8,128)(2,1)S(1)} %pad_maximum_fusion.2.refs_1_.refs_2_, ...), custom_call_target="tpu_custom_call" | custom-call | flops 8589934592 | bytes 25165824 | tf_op jit(solution)/shard_map/back_project/pallas_call | solution.py:293
  (52 shorter events, 17.3 us)
Async XLA Ops:
  0.6 52.1 %collective-permute-start.18 = (bf16[8192,512]{1,0:T(8,128)(2,1)}, bf16[8192,512]{1,0:T(8,128)(2,1)}, u32[]{:S(2)}, u32[]{:S(2)}) collective-permute-start(bf16[8192,512]{1,0:T(8,128)(2,1)} %bitcast.6), channel_id=1, source_target_pairs={{0,32},{1,33},{2,34},{3,35},{4,36},{5,37},{6,38},{7,39},{8,40},{9,... | collective-permute-start | bytes 25165832 | tf_op jit(solution)/shard_map/ppermute | solution.py:43
  2.1 5.2 %collective-permute-start = (bf16[1,1,1,64,1024]{4,3,2,1,0:T(8,128)(2,1)}, bf16[1,1,1,64,1024]{4,3,2,1,0:T(8,128)(2,1)S(1)}, u32[]{:S(2)}, u32[]{:S(2)}) collective-permute-start(bf16[1,1,1,64,1024]{4,3,2,1,0:T(8,128)(2,1)} %bitcast.8), channel_id=1, source_target_pairs={{0,1},{1,0},{2,3},{3,2},{4,5},{5,4},{6,7},{7,6},{8,9},{9,8},{10,11... | collective-permute-start | bytes 393224 | tf_op jit(solution)/shard_map/ppermute | solution.py:39
  8.3 6.7 %collective-permute-start.1 = (bf16[1,1,2,64,1024]{4,3,2,1,0:T(8,128)(2,1)S(1)}, bf16[1,1,2,64,1024]{4,3,2,1,0:T(8,128)(2,1)S(1)}, u32[]{:S(2)}, u32[]{:S(2)}) collective-permute-start(bf16[1,1,2,64,1024]{4,3,2,1,0:T(8,128)(2,1)S(1)} %pad_maximum_fusion.7), channel_id=1, source_target_pairs={{0,4},{1,5},{2,6},{3,7},{4,0},{5,1},{6,2},{7,3},{8,12},{9,13},{10,... | collective-permute-start | bytes 786440 | tf_op jit(solution)/shard_map/ppermute | solution.py:39
  16.0 9.0 %collective-permute-start.2 = (bf16[1,2,2,64,768]{4,3,2,1,0:T(8,128)(2,1)S(1)}, bf16[1,2,2,64,768]{4,3,2,1,0:T(8,128)(2,1)S(1)}, u32[]{:S(2)}, u32[]{:S(2)}) collective-permute-start(bf16[1,2,2,64,768]{4,3,2,1,0:T(8,128)(2,1)S(1)} %slice.16), channel_id=1, source_target_pairs={{0,16},{1,17},{2,18},{3,19},{4,20},{5,21},{6,22},{7,23},{8,24},{9,... | collective-permute-start | bytes 1179656 | tf_op jit(solution)/shard_map/ppermute | solution.py:39
  19.8 3.9 %collective-permute-start.3 = (bf16[1,2,2,64,256]{4,3,2,1,0:T(8,128)(2,1)S(1)}, bf16[1,2,2,64,256]{4,3,2,1,0:T(8,128)(2,1)S(1)}, u32[]{:S(2)}, u32[]{:S(2)}) collective-permute-start(bf16[1,2,2,64,256]{4,3,2,1,0:T(8,128)(2,1)S(1)} %pad_maximum_fusion.9), channel_id=1, source_target_pairs={{0,3},{1,2},{2,1},{3,0},{4,7},{5,6},{6,5},{7,4},{8,11},{9,10},{10,... | collective-permute-start | bytes 393224 | tf_op jit(solution)/shard_map/ppermute | solution.py:39
  25.1 11.2 %collective-permute-start.4 = (bf16[2,2,2,64,768]{4,3,2,1,0:T(8,128)(2,1)S(1)}, bf16[2,2,2,64,768]{4,3,2,1,0:T(8,128)(2,1)S(1)}, u32[]{:S(2)}, u32[]{:S(2)}) collective-permute-start(bf16[2,2,2,64,768]{4,3,2,1,0:T(8,128)(2,1)S(1)} %pad_maximum_fusion.4), channel_id=1, source_target_pairs={{0,80},{1,81},{2,82},{3,83},{4,84},{5,85},{6,86},{7,87},{8,88},{9,... | collective-permute-start | bytes 2359304 | tf_op jit(solution)/shard_map/ppermute | solution.py:39
  25.2 5.6 %collective-permute-start.5 = (bf16[1,2,4,64,256]{4,3,2,1,0:T(8,128)(2,1)S(1)}, bf16[1,2,4,64,256]{4,3,2,1,0:T(8,128)(2,1)S(1)}, u32[]{:S(2)}, u32[]{:S(2)}) collective-permute-start(bf16[1,2,4,64,256]{4,3,2,1,0:T(8,128)(2,1)S(1)} %pad_maximum_fusion.8), channel_id=1, source_target_pairs={{0,12},{1,13},{2,14},{3,15},{4,8},{5,9},{6,10},{7,11},{8,4},{9,5},... | collective-permute-start | bytes 786440 | tf_op jit(solution)/shard_map/ppermute | solution.py:39
  36.7 11.2 %collective-permute-start.7 = (bf16[4,2,2,64,384]{4,3,2,1,0:T(8,128)(2,1)S(1)}, bf16[4,2,2,64,384]{4,3,2,1,0:T(8,128)(2,1)S(1)}, u32[]{:S(2)}, u32[]{:S(2)}) collective-permute-start(bf16[4,2,2,64,384]{4,3,2,1,0:T(8,128)(2,1)S(1)} %get-tuple-element.25), channel_id=1, source_target_pairs={{0,3},{1,2},{2,1},{3,0},{4,7},{5,6},{6,5},{7,4},{8,11},{9,10},{10,... | collective-permute-start | bytes 2359304 | tf_op jit(solution)/shard_map/ppermute | solution.py:39
  37.1 9.5 %collective-permute-start.8 = (bf16[1,4,4,64,256]{4,3,2,1,0:T(8,128)(2,1)S(1)}, bf16[1,4,4,64,256]{4,3,2,1,0:T(8,128)(2,1)S(1)}, u32[]{:S(2)}, u32[]{:S(2)}) collective-permute-start(bf16[1,4,4,64,256]{4,3,2,1,0:T(8,128)(2,1)S(1)} %pad_maximum_fusion.6), channel_id=1, source_target_pairs={{0,16},{1,17},{2,18},{3,19},{4,20},{5,21},{6,22},{7,23},{8,24},{9,... | collective-permute-start | bytes 1572872 | tf_op jit(solution)/shard_map/ppermute | solution.py:39
  39.8 11.1 %collective-permute-start.6 = (bf16[4,2,2,64,384]{4,3,2,1,0:T(8,128)(2,1)S(1)}, bf16[4,2,2,64,384]{4,3,2,1,0:T(8,128)(2,1)S(1)}, u32[]{:S(2)}, u32[]{:S(2)}) collective-permute-start(bf16[4,2,2,64,384]{4,3,2,1,0:T(8,128)(2,1)S(1)} %get-tuple-element.26), channel_id=1, source_target_pairs={{0,12},{1,13},{2,14},{3,15},{4,8},{5,9},{6,10},{7,11},{8,4},{9,5},... | collective-permute-start | bytes 2359304 | tf_op jit(solution)/shard_map/ppermute | solution.py:39
  51.1 19.7 %collective-permute-start.10 = (bf16[4,2,4,64,384]{4,3,2,1,0:T(8,128)(2,1)S(1)}, bf16[4,2,4,64,384]{4,3,2,1,0:T(8,128)(2,1)}, u32[]{:S(2)}, u32[]{:S(2)}) collective-permute-start(bf16[4,2,4,64,384]{4,3,2,1,0:T(8,128)(2,1)S(1)} %pad_maximum_fusion.2.refs_1_.refs_2_), channel_id=1, source_target_pairs={{0,12},{1,13},{2,14},{3,15},{4,8},{5,9},{6,10},{7,11},{8,4},{9,5},... | collective-permute-start | bytes 4718600 | tf_op jit(solution)/shard_map/ppermute | solution.py:39
  51.5 19.7 %collective-permute-start.9 = (bf16[4,4,2,64,384]{4,3,2,1,0:T(8,128)(2,1)S(1)}, bf16[4,4,2,64,384]{4,3,2,1,0:T(8,128)(2,1)}, u32[]{:S(2)}, u32[]{:S(2)}) collective-permute-start(bf16[4,4,2,64,384]{4,3,2,1,0:T(8,128)(2,1)S(1)} %pad_maximum_fusion.1.refs_0_), channel_id=1, source_target_pairs={{0,3},{1,2},{2,1},{3,0},{4,7},{5,6},{6,5},{7,4},{8,11},{9,10},{10,... | collective-permute-start | bytes 4718600 | tf_op jit(solution)/shard_map/ppermute | solution.py:39
  52.6 14.3 %collective-permute-start.11 = (bf16[2,4,4,64,256]{4,3,2,1,0:T(8,128)(2,1)}, bf16[2,4,4,64,256]{4,3,2,1,0:T(8,128)(2,1)}, u32[]{:S(2)}, u32[]{:S(2)}) collective-permute-start(bf16[2,4,4,64,256]{4,3,2,1,0:T(8,128)(2,1)} %pad_maximum_fusion.3.refs_2_.refs_4_), channel_id=1, source_target_pairs={{0,80},{1,81},{2,82},{3,83},{4,84},{5,85},{6,86},{7,87},{8,88},{9,... | collective-permute-start | bytes 3145736 | tf_op jit(solution)/shard_map/ppermute | solution.py:39
  76.4 11.2 %collective-permute-start.19 = (f32[2,256,512]{2,1,0:T(8,128)S(1)}, f32[2,256,512]{2,1,0:T(8,128)S(1)}, u32[]{:S(2)}, u32[]{:S(2)}) collective-permute-start(f32[2,256,512]{2,1,0:T(8,128)S(1)} %get-tuple-element.22), channel_id=1, source_target_pairs={{0,32},{1,33},{2,34},{3,35},{4,36},{5,37},{6,38},{7,39},{8,40},{9,... | collective-permute-start | bytes 3145736 | tf_op jit(solution)/shard_map/ppermute | solution.py:43
  84.7 5.4 %collective-permute-start.16 = (bf16[2,4,4,64,256]{4,3,2,1,0:T(8,128)(2,1)}, bf16[2,4,4,64,256]{4,3,2,1,0:T(8,128)(2,1)S(1)}, u32[]{:S(2)}, u32[]{:S(2)}) collective-permute-start(bf16[2,4,4,64,256]{4,3,2,1,0:T(8,128)(2,1)} %pad_maximum_fusion.3.refs_2_.refs_4_), channel_id=1, source_target_pairs={{0,32},{1,33},{2,34},{3,35},{4,36},{5,37},{6,38},{7,39},{8,40},{9,... | collective-permute-start | bytes 3145736 | tf_op jit(solution)/shard_map/ppermute | solution.py:43
  84.8 17.3 %collective-permute-start.12 = (bf16[4,4,2,64,384]{4,3,2,1,0:T(8,128)(2,1)S(1)}, bf16[4,4,2,64,384]{4,3,2,1,0:T(8,128)(2,1)S(1)}, u32[]{:S(2)}, u32[]{:S(2)}) collective-permute-start(bf16[4,4,2,64,384]{4,3,2,1,0:T(8,128)(2,1)S(1)} %pad_maximum_fusion.1.refs_0_), channel_id=1, source_target_pairs={{0,32},{1,33},{2,34},{3,35},{4,36},{5,37},{6,38},{7,39},{8,40},{9,... | collective-permute-start | bytes 4718600 | tf_op jit(solution)/shard_map/ppermute | solution.py:43
  85.2 20.0 %collective-permute-start.14 = (bf16[4,2,4,64,384]{4,3,2,1,0:T(8,128)(2,1)S(1)}, bf16[4,2,4,64,384]{4,3,2,1,0:T(8,128)(2,1)S(1)}, u32[]{:S(2)}, u32[]{:S(2)}) collective-permute-start(bf16[4,2,4,64,384]{4,3,2,1,0:T(8,128)(2,1)S(1)} %pad_maximum_fusion.2.refs_1_.refs_2_), channel_id=1, source_target_pairs={{0,32},{1,33},{2,34},{3,35},{4,36},{5,37},{6,38},{7,39},{8,40},{9,... | collective-permute-start | bytes 4718600 | tf_op jit(solution)/shard_map/ppermute | solution.py:43
  85.3 28.3 %collective-permute-start.13 = (bf16[4,4,2,64,384]{4,3,2,1,0:T(8,128)(2,1)}, bf16[4,4,2,64,384]{4,3,2,1,0:T(8,128)(2,1)S(1)}, u32[]{:S(2)}, u32[]{:S(2)}) collective-permute-start(bf16[4,4,2,64,384]{4,3,2,1,0:T(8,128)(2,1)} %collective-permute-done.9.refs_0_.refs_1_), channel_id=1, source_target_pairs={{0,32},{1,33},{2,34},{3,35},{4,36},{5,37},{6,38},{7,39},{8,40},{9,... | collective-permute-start | bytes 4718600 | tf_op jit(solution)/shard_map/ppermute | solution.py:43
  87.6 26.1 %collective-permute-start.15 = (bf16[4,2,4,64,384]{4,3,2,1,0:T(8,128)(2,1)}, bf16[4,2,4,64,384]{4,3,2,1,0:T(8,128)(2,1)S(1)}, u32[]{:S(2)}, u32[]{:S(2)}) collective-permute-start(bf16[4,2,4,64,384]{4,3,2,1,0:T(8,128)(2,1)} %collective-permute-done.10.refs_1_.refs_3_), channel_id=1, source_target_pairs={{0,32},{1,33},{2,34},{3,35},{4,36},{5,37},{6,38},{7,39},{8,40},{9,... | collective-permute-start | bytes 4718600 | tf_op jit(solution)/shard_map/ppermute | solution.py:43
  90.1 11.0 %collective-permute-start.20 = (bf16[256,512]{1,0:T(8,128)(2,1)S(1)}, bf16[256,512]{1,0:T(8,128)(2,1)S(1)}, u32[]{:S(2)}, u32[]{:S(2)}) collective-permute-start(bf16[256,512]{1,0:T(8,128)(2,1)S(1)} %get-tuple-element.24), channel_id=1, source_target_pairs={{0,64},{1,65},{2,66},{3,67},{4,68},{5,69},{6,70},{7,71},{8,72},{9,... | collective-permute-start | bytes 786440 | tf_op jit(solution)/shard_map/ppermute | solution.py:47
  101.1 12.6 %collective-permute-start.17 = (bf16[2,4,4,64,256]{4,3,2,1,0:T(8,128)(2,1)}, bf16[2,4,4,64,256]{4,3,2,1,0:T(8,128)(2,1)S(1)}, u32[]{:S(2)}, u32[]{:S(2)}) collective-permute-start(bf16[2,4,4,64,256]{4,3,2,1,0:T(8,128)(2,1)} %collective-permute-done.11.refs_2_.refs_5_), channel_id=1, source_target_pairs={{0,32},{1,33},{2,34},{3,35},{4,36},{5,37},{6,38},{7,39},{8,40},{9,... | collective-permute-start | bytes 3145736 | tf_op jit(solution)/shard_map/ppermute | solution.py:43
  102.2 9.5 %collective-permute-start.22 = (bf16[256,512]{1,0:T(8,128)(2,1)S(1)}, bf16[256,512]{1,0:T(8,128)(2,1)S(1)}, u32[]{:S(2)}, u32[]{:S(2)}) collective-permute-start(bf16[256,512]{1,0:T(8,128)(2,1)S(1)} %direction.1.refs_12_), channel_id=1, source_target_pairs={{0,64},{1,65},{2,66},{3,67},{4,68},{5,69},{6,70},{7,71},{8,72},{9,... | collective-permute-start | bytes 786440 | tf_op jit(solution)/shard_map/ppermute | solution.py:47
  105.2 8.5 %collective-permute-start.21 = (bf16[256,512]{1,0:T(8,128)(2,1)S(1)}, bf16[256,512]{1,0:T(8,128)(2,1)S(1)}, u32[]{:S(2)}, u32[]{:S(2)}) collective-permute-start(bf16[256,512]{1,0:T(8,128)(2,1)S(1)} %direction.1.refs_12_), channel_id=1, source_target_pairs={{0,32},{1,33},{2,34},{3,35},{4,36},{5,37},{6,38},{7,39},{8,40},{9,... | collective-permute-start | bytes 786440 | tf_op jit(solution)/shard_map/ppermute | solution.py:43
  111.7 2.0 %collective-permute-start.23 = (bf16[256,512]{1,0:T(8,128)(2,1)S(1)}, bf16[256,512]{1,0:T(8,128)(2,1)S(1)}, u32[]{:S(2)}, u32[]{:S(2)}) collective-permute-start(bf16[256,512]{1,0:T(8,128)(2,1)S(1)} %collective-permute-done.22.refs_14_), channel_id=1, source_target_pairs={{0,32},{1,33},{2,34},{3,35},{4,36},{5,37},{6,38},{7,39},{8,40},{9,... | collective-permute-start | bytes 786440 | tf_op jit(solution)/shard_map/ppermute | solution.py:43
  (4 other events, 50.2 us)

commit v3 on v2

--- a/solution.py
+++ b/solution.py
@@ -12,8 +12,8 @@
 second_fix = 1.0 - math.exp(1000.0 * math.log(0.999))
 
 BOTH = ("dp", "fsdp")
-ORDER = ((0, 1, 3, 2), (0, 3, 1, 2))
-STREAMS = ((0, 384, "x"), (384, 768, "y"), (768, 1024, "z"))
+ORDER = ((0, 3, 1, 2), (0, 1, 3, 2))
+STREAMS = ((0, 384, "yzx"), (384, 768, "zxy"), (768, 1024, "xyz"))
 MIB = 1024 * 1024
 
 
@@ -31,10 +31,10 @@
     ]
 
 
-def exchange(value, axis, step):
+def exchange(value, axes, step):
     def partner(c, z, y, x):
         t = ORDER[c][1] if step == 0 else ORDER[1 - c][1]
-        return c, z ^ t if axis == "z" else z, y ^ t if axis == "y" else y, x ^ t if axis == "x" else x
+        return c, z ^ t if "z" in axes else z, y ^ t if "y" in axes else y, x ^ t if "x" in axes else x
 
     return lax.ppermute(value, BOTH, pairs(partner))
 
@@ -47,8 +47,40 @@
     return lax.ppermute(value, BOTH, pairs(lambda c, z, y, x: (c, z ^ 2, y, x)))
 
 
-def grow(held, axis, step):
-    return jnp.concatenate([held, exchange(held, axis, step)], axis="zyx".index(axis))
+def cube(shard):
+    x, y, xy = together(*[exchange(shard, axes, 0) for axes in ("x", "y", "xy")])
+    square = jnp.stack([shard, x, y, xy])
+    return x, jnp.concatenate([square, exchange(square, "z", 0)]).reshape(2, 2, 2, *shard.shape)
+
+
+def grow(held, axis):
+    return jnp.concatenate([held, exchange(held, axis, 1)], axis="zyx".index(axis))
+
+
+def corner(axes, quarter):
+    out = []
+    for axis in "zyx":
+        late = quarter % 2 if axis == axes[1] else quarter // 2
+        out.append(slice(0, 4) if axis == axes[0] else slice(2 * late, 2 * late + 2))
+    return tuple(out)
+
+
+def bring_kernel(source, out, sem):
+    copy = pltpu.make_async_copy(source, out, sem)
+    copy.start()
+    copy.wait()
+
+
+def bring(value):
+    return pl.pallas_call(
+        bring_kernel,
+        out_shape=jax.ShapeDtypeStruct(value.shape, value.dtype),
+        in_specs=[pl.BlockSpec(memory_space=pl.ANY)],
+        out_specs=pl.BlockSpec(memory_space=pltpu.VMEM),
+        scratch_shapes=[pltpu.SemaphoreType.DMA],
+        compiler_params=pltpu.CompilerParams(vmem_limit_bytes=4 * MIB),
+        name="bring",
+    )(value)
 
 
 def together(*values):
@@ -56,7 +88,7 @@
 
 
 def offset(of_core, position):
-    one = jnp.where(of_core == 0, 1, 3)
+    one = jnp.where(of_core == 0, 3, 1)
     return jnp.where(position == 0, 0, jnp.where(position == 1, one, jnp.where(position == 2, 4 - one, 2)))
 
 
@@ -111,37 +143,26 @@
 
 
 def project_kernel(late, summed, *refs):
-    pieces, refs = refs[:3], refs[3:]
+    pieces, refs = refs[:6], refs[6:]
     if late:
-        where, before, partial, sent, one, two, three, sems, out_sem = refs
+        where, before, partial, sent, *scratch, sems, out_sem = refs
     else:
-        partial, one, two, three, sems = refs
-    scratch = (one, two, three)
-    loads = [
-        [pltpu.make_async_copy(p.at[a], v.at[a], sems.at[s, a]) for a in range(p.shape[0])]
-        for s, (p, v) in enumerate(zip(pieces, scratch))
-    ]
-    first = 2 if late else 0
-    order = [(s, a) for s in range(3) for a in range(scratch[s].shape[0])]
-    for s, a in order:
-        loads[s][a].start()
-    for s, a in order:
-        loads[s][a].wait()
-        low, high, axis = STREAMS[s]
-        if axis == "x":
-            rows = summed[a, :, first : first + 2]
-        elif axis == "y":
-            rows = summed[a, first : first + 2]
-        else:
-            rows = summed[first + a]
-        depth = scratch[s].shape[1] * scratch[s].shape[2] * 64
+        partial, *scratch, sems = refs
+    loads = [pltpu.make_async_copy(p, v, sems.at[k]) for k, (p, v) in enumerate(zip(pieces, scratch))]
+    for load in loads:
+        load.start()
+    for k, load in enumerate(loads):
+        load.wait()
+        low, high, axes = STREAMS[k // 2]
+        z, y, x = corner(axes, 2 * late + k % 2)
+        rows = summed[z, y, x]
         product = lax.dot_general(
-            scratch[s][a].reshape(depth, high - low),
-            rows.reshape(depth, rows.shape[-1]),
+            scratch[k][...].reshape(1024, high - low),
+            rows.reshape(1024, rows.shape[-1]),
             (((0,), (0,)), ((), ())),
             preferred_element_type=jnp.float32,
         )
-        if a > 0:
+        if k % 2:
             partial[low:high] += product
         elif late:
             partial[low:high] = before[low:high] + product
@@ -163,10 +184,10 @@
     return pl.pallas_call(
         functools.partial(project_kernel, late),
         out_shape=(result, jax.ShapeDtypeStruct((2, 256, columns), jnp.float32)) if late else result,
-        in_specs=[inside] + [anywhere] * 3 + [pl.BlockSpec(memory_space=pltpu.SMEM), inside] * late,
+        in_specs=[inside] + [anywhere] * 6 + [pl.BlockSpec(memory_space=pltpu.SMEM), inside] * late,
         out_specs=(inside, anywhere) if late else inside,
         scratch_shapes=[pltpu.VMEM(piece.shape, jnp.bfloat16) for piece in pieces]
-        + [pltpu.SemaphoreType.DMA((3, 4))]
+        + [pltpu.SemaphoreType.DMA((6,))]
         + [pltpu.SemaphoreType.DMA] * late,
         compiler_params=pltpu.CompilerParams(vmem_limit_bytes=32 * MIB),
         cost_estimate=pl.CostEstimate(
@@ -231,37 +252,32 @@
 
 
 def update_kernel(where, *refs):
-    bases, quarters, refs = (refs[:6], refs[6:12]), refs[12:16], refs[16:]
-    out, direction, block, result, quarter_sem, in_sems, out_sems = refs
+    bases, quarters, refs = (refs[:12], refs[12:24]), refs[24:28], refs[28:]
+    out, direction, block, result, in_sems, out_sems = refs
     core, z, y, x = where[0], where[1], where[2], where[3]
 
     def load(t):
         side, a = t // 4, t % 4
         slot = t % SLOTS
-        for s, (low, high, axis) in enumerate(STREAMS):
-            held, got = bases[side][2 * s], bases[side][2 * s + 1]
-            if axis == "x":
-                jobs = [(held, a, slice(None), pl.ds(0, 2)), (got, a, slice(None), pl.ds(2, 2))]
-            elif axis == "y":
-                jobs = [(held, a, pl.ds(0, 2), slice(None)), (got, a, pl.ds(2, 2), slice(None))]
-            else:
-                jobs = [(held if a < 2 else got, a % 2, slice(None), slice(None))]
-            for source, index, b, c in jobs:
+        for k, piece in enumerate(bases[side]):
+            low, high, axes = STREAMS[k // 4]
+            layers, b, c = corner(axes, k % 4)
+            if layers.start <= a < layers.stop:
                 pltpu.make_async_copy(
-                    source.at[index], block.at[slot, b, c, :, pl.ds(low, high - low)], in_sems.at[slot]
+                    piece.at[a - layers.start],
+                    block.at[slot, pl.ds(b.start, b.stop - b.start), pl.ds(c.start, c.stop - c.start), :, pl.ds(low, high - low)],
+                    in_sems.at[slot],
                 ).start()
 
     def drain(turn):
         pltpu.make_async_copy(result.at[turn], result.at[turn], out_sems.at[turn]).wait()
 
+    for t in range(SLOTS):
+        load(t)
     far, share = z // 2, quarters[0].shape[0]
     for k, quarter in enumerate(quarters):
         place = (far ^ (k // 2)) * 2 + (core ^ (k % 2))
-        rows = pl.ds(pl.multiple_of(place * share, share), share)
-        pltpu.make_async_copy(quarter, direction.at[rows], quarter_sem).start()
-    for t in range(SLOTS):
-        load(t)
-    pltpu.make_async_copy(direction, direction, quarter_sem).wait()
+        direction[pl.ds(pl.multiple_of(place * share, share), share)] = quarter[...]
     for t in range(8):
         side, a = t // 4, t % 4
         of_core = core if side == 0 else 1 - core
@@ -289,17 +305,16 @@
     share, columns = quarters[0].shape
     rank = 4 * share
     rows = 2 * 4096
-    anywhere = pl.BlockSpec(memory_space=pl.ANY)
+    anywhere, inside = pl.BlockSpec(memory_space=pl.ANY), pl.BlockSpec(memory_space=pltpu.VMEM)
     return pl.pallas_call(
         update_kernel,
         out_shape=jax.ShapeDtypeStruct((rows, columns), jnp.bfloat16),
-        in_specs=[pl.BlockSpec(memory_space=pltpu.SMEM)] + [anywhere] * 16,
+        in_specs=[pl.BlockSpec(memory_space=pltpu.SMEM)] + [anywhere] * 24 + [inside] * 4,
         out_specs=anywhere,
         scratch_shapes=[
             pltpu.VMEM((rank, columns), jnp.bfloat16),
             pltpu.VMEM((SLOTS, 4, 4, 64, rank), jnp.bfloat16),
             pltpu.VMEM((2, 1024, columns), jnp.bfloat16),
-            pltpu.SemaphoreType.DMA,
             pltpu.SemaphoreType.DMA((SLOTS,)),
             pltpu.SemaphoreType.DMA((2,)),
         ],
@@ -319,27 +334,36 @@
 
     whole = grads[0]
     columns = whole.shape[1]
+    shard = bring(basis)
+    first, held = cube(shard)
+    first, whole = together(first, whole)
     theirs = swap_core(whole)
-    held = grow(grow(basis[None, None, None], "x", 0), "y", 0)
-    wide, narrow = held[..., :768], held[..., 768:]
-    wide, narrow = together(grow(wide, "z", 0), grow(narrow, "x", 1))
-    wide, narrow = together(grow(wide, "z", 1), grow(narrow, "y", 1))
-    halves = together(grow(wide[..., :384], "y", 1), grow(wide[..., 384:], "x", 1), grow(narrow, "z", 0))
-    got = [exchange(half, axis, 1) for half, (_, _, axis) in zip(halves, STREAMS)]
+    (held,) = together(held)
+    halves = [held[..., low:high] for low, high, _ in STREAMS]
+    *halves, theirs = together(*[grow(half, axes[0]) for half, (_, _, axes) in zip(halves, STREAMS)], theirs)
+    second = [exchange(half, axes[1], 1) for half, (_, _, axes) in zip(halves, STREAMS)]
+    third = [exchange(half, axes[2], 1) for half, (_, _, axes) in zip(halves, STREAMS)]
+    fourth = [exchange(got, axes[2], 1) for got, (_, _, axes) in zip(second, STREAMS)]
+    early = [piece for pair in zip(halves, second) for piece in pair]
+    late = [piece for pair in zip(third, fourth) for piece in pair]
     summed = sum_grads(where, whole, theirs)
-    partial, sent = project(summed, got, where, project(summed, halves))
+    *ready, summed = together(*early, summed)
+    swapped = [swap_core(piece) for piece in ready]
+    partial, sent = project(summed, late, where, project(summed, early))
 
     kept, sent = add_cores(where, partial, swap_core(sent))
-    received = swap_far(sent)
+    received, *waiting = together(swap_far(sent), *late)
     direction = direct(kept, received, first_moment, second_moment)
     new_first, new_second = adam(kept, received, first_moment, second_moment)
 
-    bases = []
-    for half, late in zip(halves, got):
-        bases += [half, late]
-    bases += [swap_core(piece) for piece in bases]
+    waiting = [swap_core(piece) for piece in waiting]
+
+    def arranged(first, last):
+        return [piece for k in range(3) for piece in (*first[2 * k : 2 * k + 2], *last[2 * k : 2 * k + 2])]
+
+    own, other = arranged(early, late), arranged(swapped, waiting)
     distant = swap_far(direction)
-    update = back_project(where, bases, (direction, swap_core(direction), distant, swap_core(distant)))
+    update = back_project(where, own + other, (direction, swap_core(direction), distant, swap_core(distant)))
     return (update, new_first, new_second)
 
 

time: 129 us -> 119 us (0.922)
  waiting for transfers between devices: 53.4 us -> 41.9 us
  starting transfers between devices: 35.6 us -> 40.8 us
  other arithmetic: 4.89 us -> 1.57 us
  Pallas kernels: 30.2 us -> 28.1 us
  local copies, waits for them, and re-layouts: 3.71 us -> 5.33 us
    ppermute x12 -> x16, waiting for transfers between devices: 37.3 us -> 25.9 us  [exchange(): return lax.ppermute(value, BOTH, pairs(partner))]
    ppermute x12 -> x16, starting transfers between devices: 15.1 us -> 23 us  [exchange(): return lax.ppermute(value, BOTH, pairs(partner))]
    concatenate x9 -> x3, other arithmetic: 3.62 us -> 0.23 us  [grow(): jnp.concatenate([held, exchange(held, axis, 1)], axis='zyx'.index(axis))]
    ppermute x2, starting transfers between devices: 7.46 us -> 4.76 us  [swap_far(): return lax.ppermute(value, BOTH, pairs(lambda c, z, y, x: (c, z ^ 2, y, x)))]
    pallas_call x2, Pallas kernels: 10.3 us -> 8.3 us  [project(): pl.pallas_call(functools.partial(project_kernel, late), out_shape=(result...]
    unnamed x8 -> x18, local copies, waits for them, and re-layouts: 3.4 us -> 5.14 us
    ppermute x10 -> x16, waiting for transfers between devices: 3.33 us -> 4.08 us  [swap_core(): return lax.ppermute(value, BOTH, pairs(lambda c, z, y, x: (1 - c, z, y, x)))]
    ppermute x10 -> x16, starting transfers between devices: 13 us -> 13.1 us  [swap_core(): return lax.ppermute(value, BOTH, pairs(lambda c, z, y, x: (1 - c, z, y, x)))]
  transfers between devices with their start and end apart: 24 -> 34, of which waited for: 16 -> 15; matrix products, arithmetic and copies ran while one was open for 4% -> 2% of each run, Pallas kernels for 8% -> 7%
where the time goes in v3:
time: 119 us
  waiting for transfers between devices  41.9 us (35%)
  starting transfers between devices  40.8 us (34%)
  Pallas kernels  28.1 us (24%)
  local copies, waits for them, and re-layouts  5.33 us (4%)
  other arithmetic  1.57 us (1%)
    ppermute x16, waiting for transfers between devices, exchange(): return lax.ppermute(value, BOTH, pairs(partner))  25.9 us
    ppermute x16, starting transfers between devices, exchange(): return lax.ppermute(value, BOTH, pairs(partner))  23 us
    pallas_call x1, Pallas kernels, back_project(): pl.pallas_call(update_kernel, out_shape=jax.ShapeDtypeStruct((rows, colum...  14.6 us
    ppermute x16, starting transfers between devices, swap_core(): return lax.ppermute(value, BOTH, pairs(lambda c, z, y, x: (1 - c, z, y, x)))  13.1 us
    ppermute x2, waiting for transfers between devices, swap_far(): return lax.ppermute(value, BOTH, pairs(lambda c, z, y, x: (c, z ^ 2, y, x)))  11.9 us
    pallas_call x2, Pallas kernels, project(): pl.pallas_call(functools.partial(project_kernel, late), out_shape=(result...  8.3 us
    unnamed x18, local copies, waits for them, and re-layouts  5.14 us
    ppermute x2, starting transfers between devices, swap_far(): return lax.ppermute(value, BOTH, pairs(lambda c, z, y, x: (c, z ^ 2, y, x)))  4.76 us
  transfers between devices with their start and end apart: 34, of which 15 were waited for; matrix products, arithmetic and copies ran while one was open for 2% of the time, Pallas kernels for 7%

profile of v3, /device:TPU:1, one launch (start us, length us, event | category | flops | bytes accessed | tf_op | source)
XLA Modules:
  0.0 118.8 jit_solution(6055416116252915628)
XLA Ops:
  1.7 2.1 %collective-permute-start = (bf16[64,1024]{1,0:T(8,128)(2,1)S(1)}, bf16[64,1024]{1,0:T(8,128)(2,1)S(1)}, u32[]{:S(2)}, u32[]{:S(2)}) collective-permute-start(bf16[64,1024]{1,0:T(8,128)(2,1)S(1)} %bring.1), channel_id=1, source_target_pairs={{0,3},{1,2},{2,1},{3,0},{4,7},{5,6},{6,5},{7,4},{8,11},{9,10},{10,... | collective-permute-start | bytes 393224 | tf_op jit(solution)/shard_map/ppermute | solution.py:39
  6.2 2.3 %collective-permute-done.1 = bf16[64,1024]{1,0:T(8,128)(2,1)S(1)} collective-permute-done((bf16[64,1024]{1,0:T(8,128)(2,1)S(1)}, bf16[64,1024]{1,0:T(8,128)(2,1)S(1)}, u32[]{:S(2)}, u32[]{:S(2)}) %collective-permute-start.1) | collective-permute-done | bytes 131104 | tf_op jit(solution)/shard_map/ppermute | solution.py:39
  9.8 7.5 %collective-permute-start.7 = (bf16[8192,512]{1,0:T(8,128)(2,1)}, bf16[8192,512]{1,0:T(8,128)(2,1)S(1)}, u32[]{:S(2)}, u32[]{:S(2)}) collective-permute-start(bf16[8192,512]{1,0:T(8,128)(2,1)} %bitcast.14), channel_id=1, source_target_pairs={{0,32},{1,33},{2,34},{3,35},{4,36},{5,37},{6,38},{7,39},{8,40},{9,... | collective-permute-start | bytes 25165832 | tf_op jit(solution)/shard_map/ppermute | solution.py:43
  17.4 1.7 %collective-permute-start.3 = (bf16[4,64,1024]{2,1,0:T(8,128)(2,1)S(1)}, bf16[4,64,1024]{2,1,0:T(8,128)(2,1)S(1)}, u32[]{:S(2)}, u32[]{:S(2)}) collective-permute-start(bf16[4,64,1024]{2,1,0:T(8,128)(2,1)S(1)} %pad_maximum_fusion.2), channel_id=1, source_target_pairs={{0,80},{1,81},{2,82},{3,83},{4,84},{5,85},{6,86},{7,87},{8,88},{9,... | collective-permute-start | bytes 1572872 | tf_op jit(solution)/shard_map/ppermute | solution.py:39
  19.2 6.8 %collective-permute-done.3 = bf16[4,64,1024]{2,1,0:T(8,128)(2,1)S(1)} collective-permute-done((bf16[4,64,1024]{2,1,0:T(8,128)(2,1)S(1)}, bf16[4,64,1024]{2,1,0:T(8,128)(2,1)S(1)}, u32[]{:S(2)}, u32[]{:S(2)}) %collective-permute-start.3) | collective-permute-done | bytes 524320 | tf_op jit(solution)/shard_map/ppermute | solution.py:39
  26.6 3.6 %collective-permute-start.5 = (bf16[2,2,2,64,384]{4,3,2,1,0:T(8,128)(2,1)S(1)}, bf16[2,2,2,64,384]{4,3,2,1,0:T(8,128)(2,1)S(1)}, u32[]{:S(2)}, u32[]{:S(2)}) collective-permute-start(bf16[2,2,2,64,384]{4,3,2,1,0:T(8,128)(2,1)S(1)} %get-tuple-element.55), channel_id=1, source_target_pairs={{0,16},{1,17},{2,18},{3,19},{4,20},{5,21},{6,22},{7,23},{8,24},{9,... | collective-permute-start | bytes 1179656 | tf_op jit(solution)/shard_map/ppermute | solution.py:39
  30.2 2.7 %collective-permute-done.6 = bf16[2,2,2,64,256]{4,3,2,1,0:T(8,128)(2,1)S(1)} collective-permute-done((bf16[2,2,2,64,256]{4,3,2,1,0:T(8,128)(2,1)S(1)}, bf16[2,2,2,64,256]{4,3,2,1,0:T(8,128)(2,1)S(1)}, u32[]{:S(2)}, u32[]{:S(2)}) %collective-permute-start.6) | collective-permute-done | bytes 262176 | tf_op jit(solution)/shard_map/ppermute | solution.py:39
  35.4 2.8 %collective-permute-start.8 = (bf16[2,4,2,64,384]{4,3,2,1,0:T(8,128)(2,1)S(1)}, bf16[2,4,2,64,384]{4,3,2,1,0:T(8,128)(2,1)S(1)}, u32[]{:S(2)}, u32[]{:S(2)}) collective-permute-start(bf16[2,4,2,64,384]{4,3,2,1,0:T(8,128)(2,1)S(1)} %pad_maximum_fusion.refs_0_), channel_id=1, source_target_pairs={{0,16},{1,17},{2,18},{3,19},{4,20},{5,21},{6,22},{7,23},{8,24},{9,... | collective-permute-start | bytes 2359304 | tf_op jit(solution)/shard_map/ppermute | solution.py:39
  38.2 2.5 %collective-permute-start.11 = (bf16[4,2,2,64,384]{4,3,2,1,0:T(8,128)(2,1)S(1)}, bf16[4,2,2,64,384]{4,3,2,1,0:T(8,128)(2,1)}, u32[]{:S(2)}, u32[]{:S(2)}) collective-permute-start(bf16[4,2,2,64,384]{4,3,2,1,0:T(8,128)(2,1)S(1)} %pad_maximum_fusion.1.refs_2_.refs_4_), channel_id=1, source_target_pairs={{0,1},{1,0},{2,3},{3,2},{4,5},{5,4},{6,7},{7,6},{8,9},{9,8},{10,11... | collective-permute-start | bytes 2359304 | tf_op jit(solution)/shard_map/ppermute | solution.py:39
  40.7 2.7 %collective-permute-start.14 = (bf16[2,2,4,64,256]{4,3,2,1,0:T(8,128)(2,1)S(1)}, bf16[2,2,4,64,256]{4,3,2,1,0:T(8,128)(2,1)S(1)}, u32[]{:S(2)}, u32[]{:S(2)}) collective-permute-start(bf16[2,2,4,64,256]{4,3,2,1,0:T(8,128)(2,1)S(1)} %pad_maximum_fusion.3.refs_4_.refs_8_), channel_id=1, source_target_pairs={{0,4},{1,5},{2,6},{3,7},{4,0},{5,1},{6,2},{7,3},{8,12},{9,13},{10,... | collective-permute-start | bytes 1572872 | tf_op jit(solution)/shard_map/ppermute | solution.py:39
  43.6 6.3 %collective-permute-done.14.refs_5_.refs_9_ = bf16[2,2,4,64,256]{4,3,2,1,0:T(8,128)(2,1)S(1)} collective-permute-done((bf16[2,2,4,64,256]{4,3,2,1,0:T(8,128)(2,1)S(1)}, bf16[2,2,4,64,256]{4,3,2,1,0:T(8,128)(2,1)S(1)}, u32[]{:S(2)}, u32[]{:S(2)}) %collective-permute-start.14) | collective-permute-done | bytes 524320 | tf_op jit(solution)/shard_map/ppermute | solution.py:39
  49.9 2.7 %collective-permute-start.12 = (bf16[4,2,2,64,384]{4,3,2,1,0:T(8,128)(2,1)S(1)}, bf16[4,2,2,64,384]{4,3,2,1,0:T(8,128)(2,1)}, u32[]{:S(2)}, u32[]{:S(2)}) collective-permute-start(bf16[4,2,2,64,384]{4,3,2,1,0:T(8,128)(2,1)S(1)} %pad_maximum_fusion.1.refs_2_.refs_4_), channel_id=1, source_target_pairs={{0,4},{1,5},{2,6},{3,7},{4,0},{5,1},{6,2},{7,3},{8,12},{9,13},{10,... | collective-permute-start | bytes 2359304 | tf_op jit(solution)/shard_map/ppermute | solution.py:39
  54.0 2.7 %collective-permute-start.16 = (bf16[2,2,4,64,256]{4,3,2,1,0:T(8,128)(2,1)S(1)}, bf16[2,2,4,64,256]{4,3,2,1,0:T(8,128)(2,1)}, u32[]{:S(2)}, u32[]{:S(2)}) collective-permute-start(bf16[2,2,4,64,256]{4,3,2,1,0:T(8,128)(2,1)S(1)} %collective-permute-done.14.refs_5_.refs_9_), channel_id=1, source_target_pairs={{0,16},{1,17},{2,18},{3,19},{4,20},{5,21},{6,22},{7,23},{8,24},{9,... | collective-permute-start | bytes 1572872 | tf_op jit(solution)/shard_map/ppermute | solution.py:39
  56.7 3.4 %copy-done = bf16[1,8192,512]{2,1,0:T(8,128)(2,1)S(1)} copy-done((bf16[1,8192,512]{2,1,0:T(8,128)(2,1)S(1)}, bf16[1,8192,512]{2,1,0:T(8,128)(2,1)}, u32[]{:S(2)}) %copy-start) | copy-done | bytes 8388632
  60.1 4.1 %sum_grads.1.summed = bf16[4,4,4,64,512]{4,3,2,1,0:T(8,128)(2,1)S(1)} custom-call(s32[4]{0:T(128)S(1)} %pad_add_fusion.where.refs_6_, bf16[8192,512]{1,0:T(8,128)(2,1)S(1)} %bitcast.15, bf16[8192,512]{1,0:T(8,128)(2,1)} %copy-done.6), custom_call_target="tpu_custom_call" | custom-call | flops 2097152 | bytes 12582912 | tf_op jit(solution)/shard_map/sum_grads/pallas_call | solution.py:129
  64.2 3.3 %project.1.refs_7_ = f32[1024,512]{1,0:T(8,128)S(1)} custom-call(bf16[4,4,4,64,512]{4,3,2,1,0:T(8,128)(2,1)S(1)} %sum_grads.1.summed, bf16[2,4,2,64,384]{4,3,2,1,0:T(8,128)(2,1)S(1)} %pad_maximum_fusion.refs_0_, bf16[2,4,2,64,384]{4,3,2,1,0:T(8,128)(2,1)S(1)} %collective-permute-done.8.refs_1_, ...), custom_call_target="tpu_custom_call" | custom-call | flops 2147483648 | bytes 8388608 | tf_op jit(solution)/shard_map/project/pallas_call | solution.py:184
  67.6 2.9 %collective-permute-done.13.refs_3_.refs_7_ = bf16[4,2,2,64,384]{4,3,2,1,0:T(8,128)(2,1)} collective-permute-done((bf16[4,2,2,64,384]{4,3,2,1,0:T(8,128)(2,1)}, bf16[4,2,2,64,384]{4,3,2,1,0:T(8,128)(2,1)}, u32[]{:S(2)}, u32[]{:S(2)}) %collective-permute-start.13) | collective-permute-done | bytes 786464 | tf_op jit(solution)/shard_map/ppermute | solution.py:39
  70.5 5.0 %project_late.1 = (f32[1024,512]{1,0:T(8,128)S(1)}, f32[2,256,512]{2,1,0:T(8,128)S(1)}) custom-call(bf16[4,4,4,64,512]{4,3,2,1,0:T(8,128)(2,1)S(1)} %sum_grads.1.summed, bf16[2,4,2,64,384]{4,3,2,1,0:T(8,128)(2,1)} %collective-permute-done.9.refs_0_.refs_2_, bf16[2,4,2,64,384]{4,3,2,1,0:T(8,128)(2,1)} %collective-permute-done.10.refs_1_.refs_3_, ...), custom_call_target="tpu_custom_call" | custom-call | flops 2147483648 | bytes 8388608 | tf_op jit(solution)/shard_map/project_late/pallas_call | solution.py:184
  76.1 2.1 %collective-permute-done.19.received = f32[2,256,512]{2,1,0:T(8,128)S(1)} collective-permute-done((f32[2,256,512]{2,1,0:T(8,128)S(1)}, f32[2,256,512]{2,1,0:T(8,128)S(1)}, u32[]{:S(2)}, u32[]{:S(2)}) %collective-permute-start.19) | collective-permute-done | bytes 1048608 | tf_op jit(solution)/shard_map/ppermute | solution.py:43
  78.9 2.4 %collective-permute-start.20 = (bf16[256,512]{1,0:T(8,128)(2,1)S(1)}, bf16[256,512]{1,0:T(8,128)(2,1)S(1)}, u32[]{:S(2)}, u32[]{:S(2)}) collective-permute-start(bf16[256,512]{1,0:T(8,128)(2,1)S(1)} %get-tuple-element.42), channel_id=1, source_target_pairs={{0,64},{1,65},{2,66},{3,67},{4,68},{5,69},{6,70},{7,71},{8,72},{9,... | collective-permute-start | bytes 786440 | tf_op jit(solution)/shard_map/ppermute | solution.py:47
  82.5 5.8 %collective-permute-done.20.received = bf16[256,512]{1,0:T(8,128)(2,1)S(1)} collective-permute-done((bf16[256,512]{1,0:T(8,128)(2,1)S(1)}, bf16[256,512]{1,0:T(8,128)(2,1)S(1)}, u32[]{:S(2)}, u32[]{:S(2)}) %collective-permute-start.20) | collective-permute-done | bytes 262176 | tf_op jit(solution)/shard_map/ppermute | solution.py:47
  90.2 2.3 %collective-permute-start.32 = (bf16[256,512]{1,0:T(8,128)(2,1)S(1)}, bf16[256,512]{1,0:T(8,128)(2,1)S(1)}, u32[]{:S(2)}, u32[]{:S(2)}) collective-permute-start(bf16[256,512]{1,0:T(8,128)(2,1)S(1)} %direction.1.refs_24_), channel_id=1, source_target_pairs={{0,64},{1,65},{2,66},{3,67},{4,68},{5,69},{6,70},{7,71},{8,72},{9,... | collective-permute-start | bytes 786440 | tf_op jit(solution)/shard_map/ppermute | solution.py:47
  93.4 6.1 %collective-permute-done.32.refs_26_ = bf16[256,512]{1,0:T(8,128)(2,1)S(1)} collective-permute-done((bf16[256,512]{1,0:T(8,128)(2,1)S(1)}, bf16[256,512]{1,0:T(8,128)(2,1)S(1)}, u32[]{:S(2)}, u32[]{:S(2)}) %collective-permute-start.32) | collective-permute-done | bytes 262176 | tf_op jit(solution)/shard_map/ppermute | solution.py:47
  104.1 14.6 %back_project.1 = bf16[8192,512]{1,0:T(8,128)(2,1)} custom-call(s32[4]{0:T(128)S(1)} %pad_add_fusion.where.refs_6_, bf16[2,4,2,64,384]{4,3,2,1,0:T(8,128)(2,1)S(1)} %pad_maximum_fusion.refs_0_, bf16[2,4,2,64,384]{4,3,2,1,0:T(8,128)(2,1)S(1)} %collective-permute-done.8.refs_1_, bf16[2,4,2,64,384]{4,3,2,1,0:T(8,128)(2,1)} %collective-permute-done.9.refs_0_.refs_2_, ...), custom_call_target="tpu_custom_call" | custom-call | flops 8589934592 | bytes 25165824 | tf_op jit(solution)/shard_map/back_project/pallas_call | solution.py:309
  (78 shorter events, 19.6 us)
Async XLA Ops:
  9.8 25.6 %collective-permute-start.7 = (bf16[8192,512]{1,0:T(8,128)(2,1)}, bf16[8192,512]{1,0:T(8,128)(2,1)S(1)}, u32[]{:S(2)}, u32[]{:S(2)}) collective-permute-start(bf16[8192,512]{1,0:T(8,128)(2,1)} %bitcast.14), channel_id=1, source_target_pairs={{0,32},{1,33},{2,34},{3,35},{4,36},{5,37},{6,38},{7,39},{8,40},{9,... | collective-permute-start | bytes 25165832 | tf_op jit(solution)/shard_map/ppermute | solution.py:43
  17.4 8.6 %collective-permute-start.3 = (bf16[4,64,1024]{2,1,0:T(8,128)(2,1)S(1)}, bf16[4,64,1024]{2,1,0:T(8,128)(2,1)S(1)}, u32[]{:S(2)}, u32[]{:S(2)}) collective-permute-start(bf16[4,64,1024]{2,1,0:T(8,128)(2,1)S(1)} %pad_maximum_fusion.2), channel_id=1, source_target_pairs={{0,80},{1,81},{2,82},{3,83},{4,84},{5,85},{6,86},{7,87},{8,88},{9,... | collective-permute-start | bytes 1572872 | tf_op jit(solution)/shard_map/ppermute | solution.py:39
  26.2 7.9 %collective-permute-start.4 = (bf16[2,2,2,64,384]{4,3,2,1,0:T(8,128)(2,1)S(1)}, bf16[2,2,2,64,384]{4,3,2,1,0:T(8,128)(2,1)S(1)}, u32[]{:S(2)}, u32[]{:S(2)}) collective-permute-start(bf16[2,2,2,64,384]{4,3,2,1,0:T(8,128)(2,1)S(1)} %get-tuple-element.56), channel_id=1, source_target_pairs={{0,4},{1,5},{2,6},{3,7},{4,0},{5,1},{6,2},{7,3},{8,12},{9,13},{10,... | collective-permute-start | bytes 1179656 | tf_op jit(solution)/shard_map/ppermute | solution.py:39
  26.6 8.7 %collective-permute-start.5 = (bf16[2,2,2,64,384]{4,3,2,1,0:T(8,128)(2,1)S(1)}, bf16[2,2,2,64,384]{4,3,2,1,0:T(8,128)(2,1)S(1)}, u32[]{:S(2)}, u32[]{:S(2)}) collective-permute-start(bf16[2,2,2,64,384]{4,3,2,1,0:T(8,128)(2,1)S(1)} %get-tuple-element.55), channel_id=1, source_target_pairs={{0,16},{1,17},{2,18},{3,19},{4,20},{5,21},{6,22},{7,23},{8,24},{9,... | collective-permute-start | bytes 1179656 | tf_op jit(solution)/shard_map/ppermute | solution.py:39
  35.4 17.1 %collective-permute-start.8 = (bf16[2,4,2,64,384]{4,3,2,1,0:T(8,128)(2,1)S(1)}, bf16[2,4,2,64,384]{4,3,2,1,0:T(8,128)(2,1)S(1)}, u32[]{:S(2)}, u32[]{:S(2)}) collective-permute-start(bf16[2,4,2,64,384]{4,3,2,1,0:T(8,128)(2,1)S(1)} %pad_maximum_fusion.refs_0_), channel_id=1, source_target_pairs={{0,16},{1,17},{2,18},{3,19},{4,20},{5,21},{6,22},{7,23},{8,24},{9,... | collective-permute-start | bytes 2359304 | tf_op jit(solution)/shard_map/ppermute | solution.py:39
  38.2 14.6 %collective-permute-start.11 = (bf16[4,2,2,64,384]{4,3,2,1,0:T(8,128)(2,1)S(1)}, bf16[4,2,2,64,384]{4,3,2,1,0:T(8,128)(2,1)}, u32[]{:S(2)}, u32[]{:S(2)}) collective-permute-start(bf16[4,2,2,64,384]{4,3,2,1,0:T(8,128)(2,1)S(1)} %pad_maximum_fusion.1.refs_2_.refs_4_), channel_id=1, source_target_pairs={{0,1},{1,0},{2,3},{3,2},{4,5},{5,4},{6,7},{7,6},{8,9},{9,8},{10,11... | collective-permute-start | bytes 2359304 | tf_op jit(solution)/shard_map/ppermute | solution.py:39
  40.7 9.2 %collective-permute-start.14 = (bf16[2,2,4,64,256]{4,3,2,1,0:T(8,128)(2,1)S(1)}, bf16[2,2,4,64,256]{4,3,2,1,0:T(8,128)(2,1)S(1)}, u32[]{:S(2)}, u32[]{:S(2)}) collective-permute-start(bf16[2,2,4,64,256]{4,3,2,1,0:T(8,128)(2,1)S(1)} %pad_maximum_fusion.3.refs_4_.refs_8_), channel_id=1, source_target_pairs={{0,4},{1,5},{2,6},{3,7},{4,0},{5,1},{6,2},{7,3},{8,12},{9,13},{10,... | collective-permute-start | bytes 1572872 | tf_op jit(solution)/shard_map/ppermute | solution.py:39
  43.3 9.9 %collective-permute-start.15 = (bf16[2,2,4,64,256]{4,3,2,1,0:T(8,128)(2,1)S(1)}, bf16[2,2,4,64,256]{4,3,2,1,0:T(8,128)(2,1)S(1)}, u32[]{:S(2)}, u32[]{:S(2)}) collective-permute-start(bf16[2,2,4,64,256]{4,3,2,1,0:T(8,128)(2,1)S(1)} %pad_maximum_fusion.3.refs_4_.refs_8_), channel_id=1, source_target_pairs={{0,16},{1,17},{2,18},{3,19},{4,20},{5,21},{6,22},{7,23},{8,24},{9,... | collective-permute-start | bytes 1572872 | tf_op jit(solution)/shard_map/ppermute | solution.py:39
  43.4 24.1 %collective-permute-start.9 = (bf16[2,4,2,64,384]{4,3,2,1,0:T(8,128)(2,1)S(1)}, bf16[2,4,2,64,384]{4,3,2,1,0:T(8,128)(2,1)}, u32[]{:S(2)}, u32[]{:S(2)}) collective-permute-start(bf16[2,4,2,64,384]{4,3,2,1,0:T(8,128)(2,1)S(1)} %pad_maximum_fusion.refs_0_), channel_id=1, source_target_pairs={{0,1},{1,0},{2,3},{3,2},{4,5},{5,4},{6,7},{7,6},{8,9},{9,8},{10,11... | collective-permute-start | bytes 2359304 | tf_op jit(solution)/shard_map/ppermute | solution.py:39
  49.9 17.7 %collective-permute-start.12 = (bf16[4,2,2,64,384]{4,3,2,1,0:T(8,128)(2,1)S(1)}, bf16[4,2,2,64,384]{4,3,2,1,0:T(8,128)(2,1)}, u32[]{:S(2)}, u32[]{:S(2)}) collective-permute-start(bf16[4,2,2,64,384]{4,3,2,1,0:T(8,128)(2,1)S(1)} %pad_maximum_fusion.1.refs_2_.refs_4_), channel_id=1, source_target_pairs={{0,4},{1,5},{2,6},{3,7},{4,0},{5,1},{6,2},{7,3},{8,12},{9,13},{10,... | collective-permute-start | bytes 2359304 | tf_op jit(solution)/shard_map/ppermute | solution.py:39
  52.6 15.0 %collective-permute-start.10 = (bf16[2,4,2,64,384]{4,3,2,1,0:T(8,128)(2,1)S(1)}, bf16[2,4,2,64,384]{4,3,2,1,0:T(8,128)(2,1)}, u32[]{:S(2)}, u32[]{:S(2)}) collective-permute-start(bf16[2,4,2,64,384]{4,3,2,1,0:T(8,128)(2,1)S(1)} %collective-permute-done.8.refs_1_), channel_id=1, source_target_pairs={{0,1},{1,0},{2,3},{3,2},{4,5},{5,4},{6,7},{7,6},{8,9},{9,8},{10,11... | collective-permute-start | bytes 2359304 | tf_op jit(solution)/shard_map/ppermute | solution.py:39
  52.8 17.7 %collective-permute-start.13 = (bf16[4,2,2,64,384]{4,3,2,1,0:T(8,128)(2,1)}, bf16[4,2,2,64,384]{4,3,2,1,0:T(8,128)(2,1)}, u32[]{:S(2)}, u32[]{:S(2)}) collective-permute-start(bf16[4,2,2,64,384]{4,3,2,1,0:T(8,128)(2,1)} %collective-permute-done.11.refs_3_.refs_5_), channel_id=1, source_target_pairs={{0,4},{1,5},{2,6},{3,7},{4,0},{5,1},{6,2},{7,3},{8,12},{9,13},{10,... | collective-permute-start | bytes 2359304 | tf_op jit(solution)/shard_map/ppermute | solution.py:39
  54.0 13.6 %collective-permute-start.16 = (bf16[2,2,4,64,256]{4,3,2,1,0:T(8,128)(2,1)S(1)}, bf16[2,2,4,64,256]{4,3,2,1,0:T(8,128)(2,1)}, u32[]{:S(2)}, u32[]{:S(2)}) collective-permute-start(bf16[2,2,4,64,256]{4,3,2,1,0:T(8,128)(2,1)S(1)} %collective-permute-done.14.refs_5_.refs_9_), channel_id=1, source_target_pairs={{0,16},{1,17},{2,18},{3,19},{4,20},{5,21},{6,22},{7,23},{8,24},{9,... | collective-permute-start | bytes 1572872 | tf_op jit(solution)/shard_map/ppermute | solution.py:39
  75.6 6.9 %collective-permute-start.27 = (bf16[2,2,4,64,256]{4,3,2,1,0:T(8,128)(2,1)S(1)}, bf16[2,2,4,64,256]{4,3,2,1,0:T(8,128)(2,1)S(1)}, u32[]{:S(2)}, u32[]{:S(2)}) collective-permute-start(bf16[2,2,4,64,256]{4,3,2,1,0:T(8,128)(2,1)S(1)} %pad_maximum_fusion.3.refs_4_.refs_8_), channel_id=1, source_target_pairs={{0,32},{1,33},{2,34},{3,35},{4,36},{5,37},{6,38},{7,39},{8,40},{9,... | collective-permute-start | bytes 1572872 | tf_op jit(solution)/shard_map/ppermute | solution.py:43
  78.9 9.4 %collective-permute-start.20 = (bf16[256,512]{1,0:T(8,128)(2,1)S(1)}, bf16[256,512]{1,0:T(8,128)(2,1)S(1)}, u32[]{:S(2)}, u32[]{:S(2)}) collective-permute-start(bf16[256,512]{1,0:T(8,128)(2,1)S(1)} %get-tuple-element.42), channel_id=1, source_target_pairs={{0,64},{1,65},{2,66},{3,67},{4,68},{5,69},{6,70},{7,71},{8,72},{9,... | collective-permute-start | bytes 786440 | tf_op jit(solution)/shard_map/ppermute | solution.py:47
  81.3 8.3 %collective-permute-start.17 = (bf16[2,4,2,64,384]{4,3,2,1,0:T(8,128)(2,1)S(1)}, bf16[2,4,2,64,384]{4,3,2,1,0:T(8,128)(2,1)S(1)}, u32[]{:S(2)}, u32[]{:S(2)}) collective-permute-start(bf16[2,4,2,64,384]{4,3,2,1,0:T(8,128)(2,1)S(1)} %pad_maximum_fusion.refs_0_), channel_id=1, source_target_pairs={{0,32},{1,33},{2,34},{3,35},{4,36},{5,37},{6,38},{7,39},{8,40},{9,... | collective-permute-start | bytes 2359304 | tf_op jit(solution)/shard_map/ppermute | solution.py:43
  82.0 8.2 %collective-permute-start.18 = (bf16[2,4,2,64,384]{4,3,2,1,0:T(8,128)(2,1)S(1)}, bf16[2,4,2,64,384]{4,3,2,1,0:T(8,128)(2,1)S(1)}, u32[]{:S(2)}, u32[]{:S(2)}) collective-permute-start(bf16[2,4,2,64,384]{4,3,2,1,0:T(8,128)(2,1)S(1)} %collective-permute-done.8.refs_1_), channel_id=1, source_target_pairs={{0,32},{1,33},{2,34},{3,35},{4,36},{5,37},{6,38},{7,39},{8,40},{9,... | collective-permute-start | bytes 2359304 | tf_op jit(solution)/shard_map/ppermute | solution.py:43
  82.0 7.2 %collective-permute-start.28 = (bf16[2,2,4,64,256]{4,3,2,1,0:T(8,128)(2,1)S(1)}, bf16[2,2,4,64,256]{4,3,2,1,0:T(8,128)(2,1)S(1)}, u32[]{:S(2)}, u32[]{:S(2)}) collective-permute-start(bf16[2,2,4,64,256]{4,3,2,1,0:T(8,128)(2,1)S(1)} %collective-permute-done.14.refs_5_.refs_9_), channel_id=1, source_target_pairs={{0,32},{1,33},{2,34},{3,35},{4,36},{5,37},{6,38},{7,39},{8,40},{9,... | collective-permute-start | bytes 1572872 | tf_op jit(solution)/shard_map/ppermute | solution.py:43
  82.5 10.1 %collective-permute-start.23 = (bf16[4,2,2,64,384]{4,3,2,1,0:T(8,128)(2,1)S(1)}, bf16[4,2,2,64,384]{4,3,2,1,0:T(8,128)(2,1)S(1)}, u32[]{:S(2)}, u32[]{:S(2)}) collective-permute-start(bf16[4,2,2,64,384]{4,3,2,1,0:T(8,128)(2,1)S(1)} %pad_maximum_fusion.1.refs_2_.refs_4_), channel_id=1, source_target_pairs={{0,32},{1,33},{2,34},{3,35},{4,36},{5,37},{6,38},{7,39},{8,40},{9,... | collective-permute-start | bytes 2359304 | tf_op jit(solution)/shard_map/ppermute | solution.py:43
  89.2 11.2 %collective-permute-start.29 = (bf16[2,2,4,64,256]{4,3,2,1,0:T(8,128)(2,1)S(1)}, bf16[2,2,4,64,256]{4,3,2,1,0:T(8,128)(2,1)S(1)}, u32[]{:S(2)}, u32[]{:S(2)}) collective-permute-start(bf16[2,2,4,64,256]{4,3,2,1,0:T(8,128)(2,1)S(1)} %copy-done.4), channel_id=1, source_target_pairs={{0,32},{1,33},{2,34},{3,35},{4,36},{5,37},{6,38},{7,39},{8,40},{9,... | collective-permute-start | bytes 1572872 | tf_op jit(solution)/shard_map/ppermute | solution.py:43
  90.2 9.4 %collective-permute-start.32 = (bf16[256,512]{1,0:T(8,128)(2,1)S(1)}, bf16[256,512]{1,0:T(8,128)(2,1)S(1)}, u32[]{:S(2)}, u32[]{:S(2)}) collective-permute-start(bf16[256,512]{1,0:T(8,128)(2,1)S(1)} %direction.1.refs_24_), channel_id=1, source_target_pairs={{0,64},{1,65},{2,66},{3,67},{4,68},{5,69},{6,70},{7,71},{8,72},{9,... | collective-permute-start | bytes 786440 | tf_op jit(solution)/shard_map/ppermute | solution.py:47
  92.6 7.9 %collective-permute-start.30 = (bf16[2,2,4,64,256]{4,3,2,1,0:T(8,128)(2,1)}, bf16[2,2,4,64,256]{4,3,2,1,0:T(8,128)(2,1)S(1)}, u32[]{:S(2)}, u32[]{:S(2)}) collective-permute-start(bf16[2,2,4,64,256]{4,3,2,1,0:T(8,128)(2,1)} %collective-permute-done.16.refs_5_.refs_11_), channel_id=1, source_target_pairs={{0,32},{1,33},{2,34},{3,35},{4,36},{5,37},{6,38},{7,39},{8,40},{9,... | collective-permute-start | bytes 1572872 | tf_op jit(solution)/shard_map/ppermute | solution.py:43
  92.9 10.2 %collective-permute-start.21 = (bf16[2,4,2,64,384]{4,3,2,1,0:T(8,128)(2,1)}, bf16[2,4,2,64,384]{4,3,2,1,0:T(8,128)(2,1)S(1)}, u32[]{:S(2)}, u32[]{:S(2)}) collective-permute-start(bf16[2,4,2,64,384]{4,3,2,1,0:T(8,128)(2,1)} %collective-permute-done.9.refs_0_.refs_2_), channel_id=1, source_target_pairs={{0,32},{1,33},{2,34},{3,35},{4,36},{5,37},{6,38},{7,39},{8,40},{9,... | collective-permute-start | bytes 2359304 | tf_op jit(solution)/shard_map/ppermute | solution.py:43
  93.1 10.0 %collective-permute-start.22 = (bf16[2,4,2,64,384]{4,3,2,1,0:T(8,128)(2,1)}, bf16[2,4,2,64,384]{4,3,2,1,0:T(8,128)(2,1)S(1)}, u32[]{:S(2)}, u32[]{:S(2)}) collective-permute-start(bf16[2,4,2,64,384]{4,3,2,1,0:T(8,128)(2,1)} %collective-permute-done.10.refs_1_.refs_3_), channel_id=1, source_target_pairs={{0,32},{1,33},{2,34},{3,35},{4,36},{5,37},{6,38},{7,39},{8,40},{9,... | collective-permute-start | bytes 2359304 | tf_op jit(solution)/shard_map/ppermute | solution.py:43
  (17 other events, 113.5 us)

commit v4 on v3

--- a/solution.py
+++ b/solution.py
@@ -33,8 +33,8 @@
 
 def exchange(value, axes, step):
     def partner(c, z, y, x):
-        t = ORDER[c][1] if step == 0 else ORDER[1 - c][1]
-        return c, z ^ t if "z" in axes else z, y ^ t if "y" in axes else y, x ^ t if "x" in axes else x
+        t, u = (ORDER[c][1], ORDER[1 - c][1]) if step == 0 else (ORDER[1 - c][1], ORDER[c][1])
+        return c, z ^ u if "z" in axes else z, y ^ t if "y" in axes else y, x ^ t if "x" in axes else x
 
     return lax.ppermute(value, BOTH, pairs(partner))
 
@@ -45,24 +45,6 @@
 
 def swap_far(value):
     return lax.ppermute(value, BOTH, pairs(lambda c, z, y, x: (c, z ^ 2, y, x)))
-
-
-def cube(shard):
-    x, y, xy = together(*[exchange(shard, axes, 0) for axes in ("x", "y", "xy")])
-    square = jnp.stack([shard, x, y, xy])
-    return x, jnp.concatenate([square, exchange(square, "z", 0)]).reshape(2, 2, 2, *shard.shape)
-
-
-def grow(held, axis):
-    return jnp.concatenate([held, exchange(held, axis, 1)], axis="zyx".index(axis))
-
-
-def corner(axes, quarter):
-    out = []
-    for axis in "zyx":
-        late = quarter % 2 if axis == axes[1] else quarter // 2
-        out.append(slice(0, 4) if axis == axes[0] else slice(2 * late, 2 * late + 2))
-    return tuple(out)
 
 
 def bring_kernel(source, out, sem):
@@ -83,6 +65,24 @@
     )(value)
 
 
+def cube(shard):
+    x, y, xy, z = together(*[exchange(shard, axes, 0) for axes in ("x", "y", "xy", "z")])
+    xz, yz, xyz = exchange(jnp.stack([x, y, xy]), "z", 0)
+    return jnp.stack([bring(shard), x, y, xy, z, xz, yz, xyz]).reshape(2, 2, 2, *shard.shape)
+
+
+def join(first, second, axis):
+    return jnp.concatenate([first, second], axis="zyx".index(axis))
+
+
+def corner(axes, quarter):
+    out = []
+    for axis in "zyx":
+        late = quarter % 2 if axis == axes[1] else quarter // 2
+        out.append(slice(0, 4) if axis == axes[0] else slice(2 * late, 2 * late + 2))
+    return tuple(out)
+
+
 def together(*values):
     return lax.optimization_barrier(values)
 
@@ -93,7 +93,7 @@
 
 
 def layer(of_core, z, position):
-    zz = z ^ offset(of_core, position)
+    zz = z ^ offset(1 - of_core, position)
     return ((zz // 2) * 2 + of_core) * 2 + zz % 2
 
 
@@ -145,14 +145,16 @@
 def project_kernel(late, summed, *refs):
     pieces, refs = refs[:6], refs[6:]
     if late:
-        where, before, partial, sent, *scratch, sems, out_sem = refs
+        where, before, partial, sent, *refs = refs
     else:
-        partial, *scratch, sems = refs
+        partial, *refs = refs
+    packed, scratch, (sems, pack_sem, out_sem) = refs[:3], refs[3:9], refs[9:]
     loads = [pltpu.make_async_copy(p, v, sems.at[k]) for k, (p, v) in enumerate(zip(pieces, scratch))]
     for load in loads:
         load.start()
     for k, load in enumerate(loads):
         load.wait()
+        pltpu.make_async_copy(scratch[k], packed[k // 2].at[k % 2], pack_sem).start()
         low, high, axes = STREAMS[k // 2]
         z, y, x = corner(axes, 2 * late + k % 2)
         rows = summed[z, y, x]
@@ -174,21 +176,25 @@
             row = pl.multiple_of((far * 2 + 1 - where[0]) * share, share)
             pltpu.make_async_copy(partial.at[pl.ds(row, share)], sent.at[far], out_sem).start()
         pltpu.make_async_copy(sent, sent, out_sem).wait()
+    for out in packed:
+        pltpu.make_async_copy(out, out, pack_sem).wait()
 
 
 def project(summed, pieces, where=None, before=None):
     columns = summed.shape[-1]
     late = before is not None
     anywhere, inside = pl.BlockSpec(memory_space=pl.ANY), pl.BlockSpec(memory_space=pltpu.VMEM)
-    result = jax.ShapeDtypeStruct((1024, columns), jnp.float32)
+    result = [jax.ShapeDtypeStruct((1024, columns), jnp.float32)]
+    if late:
+        result.append(jax.ShapeDtypeStruct((2, 256, columns), jnp.float32))
+    packed = [jax.ShapeDtypeStruct((2, *piece.shape), piece.dtype) for piece in pieces[::2]]
     return pl.pallas_call(
         functools.partial(project_kernel, late),
-        out_shape=(result, jax.ShapeDtypeStruct((2, 256, columns), jnp.float32)) if late else result,
+        out_shape=result + packed,
         in_specs=[inside] + [anywhere] * 6 + [pl.BlockSpec(memory_space=pltpu.SMEM), inside] * late,
-        out_specs=(inside, anywhere) if late else inside,
+        out_specs=[inside] + [anywhere] * (len(result) + 2),
         scratch_shapes=[pltpu.VMEM(piece.shape, jnp.bfloat16) for piece in pieces]
-        + [pltpu.SemaphoreType.DMA((6,))]
-        + [pltpu.SemaphoreType.DMA] * late,
+        + [pltpu.SemaphoreType.DMA((6,)), pltpu.SemaphoreType.DMA, pltpu.SemaphoreType.DMA],
         compiler_params=pltpu.CompilerParams(vmem_limit_bytes=32 * MIB),
         cost_estimate=pl.CostEstimate(
             flops=summed.size * 1024, bytes_accessed=2 * summed.size + 4 * MIB, transcendentals=0
@@ -252,7 +258,8 @@
 
 
 def update_kernel(where, *refs):
-    bases, quarters, refs = (refs[:12], refs[12:24]), refs[24:28], refs[28:]
+    own, other, quarters, refs = refs[:12], refs[12:18], refs[18:22], refs[22:]
+    bases = own, [other[2 * (k // 4) + (k % 4) // 2].at[k % 2] for k in range(12)]
     out, direction, block, result, in_sems, out_sems = refs
     core, z, y, x = where[0], where[1], where[2], where[3]
 
@@ -285,13 +292,18 @@
         pltpu.make_async_copy(block.at[slot], block.at[slot], in_sems.at[slot]).wait()
         if t >= 2:
             drain(turn)
-        result[turn] = jnp.dot(
-            block[slot].reshape(1024, block.shape[-1]), direction[...], preferred_element_type=jnp.float32
-        ).astype(jnp.bfloat16)
-        if t + SLOTS < 8:
-            load(t + SLOTS)
         base = layer(of_core, z, a) * 1024
+        parts = 1 if t < 7 else 2
         for b in range(4):
+            if b % (4 // parts) == 0:
+                size = 1024 // parts
+                result[turn, b * 256 : b * 256 + size] = jnp.dot(
+                    block[slot, b : b + 4 // parts].reshape(size, block.shape[-1]),
+                    direction[...],
+                    preferred_element_type=jnp.float32,
+                ).astype(jnp.bfloat16)
+            if b == 0 and t + SLOTS < 8:
+                load(t + SLOTS)
             for c in range(4):
                 row = pl.multiple_of(base + (y ^ offset(of_core, b)) * 256 + (x ^ offset(of_core, c)) * 64, 64)
                 pltpu.make_async_copy(
@@ -309,7 +321,7 @@
     return pl.pallas_call(
         update_kernel,
         out_shape=jax.ShapeDtypeStruct((rows, columns), jnp.bfloat16),
-        in_specs=[pl.BlockSpec(memory_space=pltpu.SMEM)] + [anywhere] * 24 + [inside] * 4,
+        in_specs=[pl.BlockSpec(memory_space=pltpu.SMEM)] + [anywhere] * 18 + [inside] * 4,
         out_specs=anywhere,
         scratch_shapes=[
             pltpu.VMEM((rank, columns), jnp.bfloat16),
@@ -334,36 +346,34 @@
 
     whole = grads[0]
     columns = whole.shape[1]
-    shard = bring(basis)
-    first, held = cube(shard)
-    first, whole = together(first, whole)
     theirs = swap_core(whole)
-    (held,) = together(held)
-    halves = [held[..., low:high] for low, high, _ in STREAMS]
-    *halves, theirs = together(*[grow(half, axes[0]) for half, (_, _, axes) in zip(halves, STREAMS)], theirs)
-    second = [exchange(half, axes[1], 1) for half, (_, _, axes) in zip(halves, STREAMS)]
+    held, theirs = together(cube(basis), theirs)
+    eighths = [held[..., low:high] for low, high, _ in STREAMS]
+    got = [exchange(eighth, axes[0], 1) for eighth, (_, _, axes) in zip(eighths, STREAMS)]
+    ahead = [exchange(eighth, axes[1], 1) for eighth, (_, _, axes) in zip(eighths, STREAMS)]
+    got = together(*got)
+    halves = [join(eighth, other, axes[0]) for eighth, other, (_, _, axes) in zip(eighths, got, STREAMS)]
+    behind = [exchange(other, axes[1], 1) for other, (_, _, axes) in zip(got, STREAMS)]
     third = [exchange(half, axes[2], 1) for half, (_, _, axes) in zip(halves, STREAMS)]
+    second = [join(first, last, axes[0]) for first, last, (_, _, axes) in zip(ahead, behind, STREAMS)]
     fourth = [exchange(got, axes[2], 1) for got, (_, _, axes) in zip(second, STREAMS)]
     early = [piece for pair in zip(halves, second) for piece in pair]
     late = [piece for pair in zip(third, fourth) for piece in pair]
     summed = sum_grads(where, whole, theirs)
-    *ready, summed = together(*early, summed)
-    swapped = [swap_core(piece) for piece in ready]
-    partial, sent = project(summed, late, where, project(summed, early))
+    partial, *packed = project(summed, early)
+    partial, sent, *more = project(summed, late, where, partial)
 
     kept, sent = add_cores(where, partial, swap_core(sent))
-    received, *waiting = together(swap_far(sent), *late)
+    kept, *more = together(kept, *more)
+    received = swap_far(sent)
     direction = direct(kept, received, first_moment, second_moment)
     new_first, new_second = adam(kept, received, first_moment, second_moment)
 
-    waiting = [swap_core(piece) for piece in waiting]
-
-    def arranged(first, last):
-        return [piece for k in range(3) for piece in (*first[2 * k : 2 * k + 2], *last[2 * k : 2 * k + 2])]
-
-    own, other = arranged(early, late), arranged(swapped, waiting)
     distant = swap_far(direction)
-    update = back_project(where, own + other, (direction, swap_core(direction), distant, swap_core(distant)))
+    near = swap_core(direction)
+    own = [piece for k in range(3) for piece in (*early[2 * k : 2 * k + 2], *late[2 * k : 2 * k + 2])]
+    other = [swap_core(value) for pair in zip(packed, more) for value in pair]
+    update = back_project(where, own + other, (direction, near, distant, swap_core(distant)))
     return (update, new_first, new_second)
 
 

time: 119 us -> 114 us (0.958)
  waiting for transfers between devices: 41.9 us -> 32.7 us
  starting transfers between devices: 40.8 us -> 43.3 us
  local copies, waits for them, and re-layouts: 5.33 us -> 7.09 us
    ppermute x16 -> x20, waiting for transfers between devices: 25.9 us -> 13.4 us  [exchange(): return lax.ppermute(value, BOTH, pairs(partner))]
    ppermute x16 -> x20, starting transfers between devices: 23 us -> 31.3 us  [exchange(): return lax.ppermute(value, BOTH, pairs(partner))]
    ppermute x2, waiting for transfers between devices: 11.9 us -> 17.3 us  [swap_far(): return lax.ppermute(value, BOTH, pairs(lambda c, z, y, x: (c, z ^ 2, y, x)))]
    ppermute x2, starting transfers between devices: 4.76 us -> 0.93 us  [swap_far(): return lax.ppermute(value, BOTH, pairs(lambda c, z, y, x: (c, z ^ 2, y, x)))]
    ppermute x16 -> x10, waiting for transfers between devices: 4.08 us -> 1.95 us  [swap_core(): return lax.ppermute(value, BOTH, pairs(lambda c, z, y, x: (1 - c, z, y, x)))]
    ppermute x16 -> x10, starting transfers between devices: 13.1 us -> 11.2 us  [swap_core(): return lax.ppermute(value, BOTH, pairs(lambda c, z, y, x: (1 - c, z, y, x)))]
    unnamed x18 -> x20, local copies, waits for them, and re-layouts: 5.14 us -> 6.03 us
  transfers between devices with their start and end apart: 34 -> 32, of which waited for: 15 -> 13; matrix products, arithmetic and copies ran while one was open for 2% -> 3% of each run, Pallas kernels for 7% -> 8%
where the time goes in v4:
time: 114 us
  starting transfers between devices  43.3 us (38%)
  waiting for transfers between devices  32.7 us (29%)
  Pallas kernels  28.4 us (25%)
  local copies, waits for them, and re-layouts  7.09 us (6%)
  other arithmetic  1.54 us (1%)
    ppermute x20, starting transfers between devices, exchange(): return lax.ppermute(value, BOTH, pairs(partner))  31.3 us
    ppermute x2, waiting for transfers between devices, swap_far(): return lax.ppermute(value, BOTH, pairs(lambda c, z, y, x: (c, z ^ 2, y, x)))  17.3 us
    pallas_call x1, Pallas kernels, back_project(): pl.pallas_call(update_kernel, out_shape=jax.ShapeDtypeStruct((rows, colum...  14.4 us
    ppermute x20, waiting for transfers between devices, exchange(): return lax.ppermute(value, BOTH, pairs(partner))  13.4 us
    ppermute x10, starting transfers between devices, swap_core(): return lax.ppermute(value, BOTH, pairs(lambda c, z, y, x: (1 - c, z, y, x)))  11.2 us
    pallas_call x2, Pallas kernels, project(): pl.pallas_call(functools.partial(project_kernel, late), out_shape=result...  8.77 us
    unnamed x20, local copies, waits for them, and re-layouts  6.03 us
    pallas_call x1, Pallas kernels, sum_grads(): pl.pallas_call(sum_kernel, out_shape=jax.ShapeDtypeStruct((4, 4, 4, 64, c...  4.07 us
  transfers between devices with their start and end apart: 32, of which 13 were waited for; matrix products, arithmetic and copies ran while one was open for 3% of the time, Pallas kernels for 8%

profile of v4, /device:TPU:1, one launch (start us, length us, event | category | flops | bytes accessed | tf_op | source)
XLA Modules:
  0.0 114.2 jit_solution(1504457685342343861)
XLA Ops:
  0.6 1.5 %collective-permute-start.5 = (bf16[8192,512]{1,0:T(8,128)(2,1)}, bf16[8192,512]{1,0:T(8,128)(2,1)}, u32[]{:S(2)}, u32[]{:S(2)}) collective-permute-start(bf16[8192,512]{1,0:T(8,128)(2,1)} %bitcast.16), channel_id=1, source_target_pairs={{0,32},{1,33},{2,34},{3,35},{4,36},{5,37},{6,38},{7,39},{8,40},{9,... | collective-permute-start | bytes 25165832 | tf_op jit(solution)/shard_map/ppermute | solution.py:43
  3.4 1.3 %collective-permute-start.1 = (bf16[64,1024]{1,0:T(8,128)(2,1)}, bf16[64,1024]{1,0:T(8,128)(2,1)S(1)}, u32[]{:S(2)}, u32[]{:S(2)}) collective-permute-start(bf16[64,1024]{1,0:T(8,128)(2,1)} %source.1), channel_id=1, source_target_pairs={{0,12},{1,13},{2,14},{3,15},{4,8},{5,9},{6,10},{7,11},{8,4},{9,5},... | collective-permute-start | bytes 393224 | tf_op jit(solution)/shard_map/ppermute | solution.py:39
  4.8 3.8 %collective-permute-start.3 = (bf16[64,1024]{1,0:T(8,128)(2,1)}, bf16[64,1024]{1,0:T(8,128)(2,1)S(1)}, u32[]{:S(2)}, u32[]{:S(2)}) collective-permute-start(bf16[64,1024]{1,0:T(8,128)(2,1)} %source.1), channel_id=1, source_target_pairs={{0,16},{1,17},{2,18},{3,19},{4,20},{5,21},{6,22},{7,23},{8,24},{9,... | collective-permute-start | bytes 393224 | tf_op jit(solution)/shard_map/ppermute | solution.py:39
  11.3 3.0 %collective-permute-start.4 = (bf16[3,64,1024]{2,1,0:T(8,128)(2,1)S(1)}, bf16[3,64,1024]{2,1,0:T(8,128)(2,1)S(1)}, u32[]{:S(2)}, u32[]{:S(2)}) collective-permute-start(bf16[3,64,1024]{2,1,0:T(8,128)(2,1)S(1)} %pad_maximum_fusion.3), channel_id=1, source_target_pairs={{0,16},{1,17},{2,18},{3,19},{4,20},{5,21},{6,22},{7,23},{8,24},{9,... | collective-permute-start | bytes 1179656 | tf_op jit(solution)/shard_map/ppermute | solution.py:39
  14.4 5.1 %collective-permute-done.4 = bf16[3,64,1024]{2,1,0:T(8,128)(2,1)S(1)} collective-permute-done((bf16[3,64,1024]{2,1,0:T(8,128)(2,1)S(1)}, bf16[3,64,1024]{2,1,0:T(8,128)(2,1)S(1)}, u32[]{:S(2)}, u32[]{:S(2)}) %collective-permute-start.4) | collective-permute-done | bytes 393248 | tf_op jit(solution)/shard_map/ppermute | solution.py:39
  19.6 2.8 %collective-permute-start.6 = (bf16[2,2,2,64,384]{4,3,2,1,0:T(8,128)(2,1)S(1)}, bf16[2,2,2,64,384]{4,3,2,1,0:T(8,128)(2,1)S(1)}, u32[]{:S(2)}, u32[]{:S(2)}) collective-permute-start(bf16[2,2,2,64,384]{4,3,2,1,0:T(8,128)(2,1)S(1)} %get-tuple-element.52), channel_id=1, source_target_pairs={{0,4},{1,5},{2,6},{3,7},{4,0},{5,1},{6,2},{7,3},{8,12},{9,13},{10,... | collective-permute-start | bytes 1179656 | tf_op jit(solution)/shard_map/ppermute | solution.py:39
  22.5 2.6 %collective-permute-start.8 = (bf16[2,2,2,64,256]{4,3,2,1,0:T(8,128)(2,1)S(1)}, bf16[2,2,2,64,256]{4,3,2,1,0:T(8,128)(2,1)S(1)}, u32[]{:S(2)}, u32[]{:S(2)}) collective-permute-start(bf16[2,2,2,64,256]{4,3,2,1,0:T(8,128)(2,1)S(1)} %slice.12), channel_id=1, source_target_pairs={{0,1},{1,0},{2,3},{3,2},{4,5},{5,4},{6,7},{7,6},{8,9},{9,8},{10,11... | collective-permute-start | bytes 786440 | tf_op jit(solution)/shard_map/ppermute | solution.py:39
  25.0 1.5 %collective-permute-start.9 = (bf16[2,2,2,64,384]{4,3,2,1,0:T(8,128)(2,1)S(1)}, bf16[2,2,2,64,384]{4,3,2,1,0:T(8,128)(2,1)S(1)}, u32[]{:S(2)}, u32[]{:S(2)}) collective-permute-start(bf16[2,2,2,64,384]{4,3,2,1,0:T(8,128)(2,1)S(1)} %get-tuple-element.52), channel_id=1, source_target_pairs={{0,80},{1,81},{2,82},{3,83},{4,84},{5,85},{6,86},{7,87},{8,88},{9,... | collective-permute-start | bytes 1179656 | tf_op jit(solution)/shard_map/ppermute | solution.py:39
  26.7 2.3 %collective-permute-done.8 = bf16[2,2,2,64,256]{4,3,2,1,0:T(8,128)(2,1)S(1)} collective-permute-done((bf16[2,2,2,64,256]{4,3,2,1,0:T(8,128)(2,1)S(1)}, bf16[2,2,2,64,256]{4,3,2,1,0:T(8,128)(2,1)S(1)}, u32[]{:S(2)}, u32[]{:S(2)}) %collective-permute-start.8) | collective-permute-done | bytes 262176 | tf_op jit(solution)/shard_map/ppermute | solution.py:39
  30.8 2.7 %collective-permute-start.18 = (bf16[2,2,2,64,256]{4,3,2,1,0:T(8,128)(2,1)S(1)}, bf16[2,2,2,64,256]{4,3,2,1,0:T(8,128)(2,1)S(1)}, u32[]{:S(2)}, u32[]{:S(2)}) collective-permute-start(bf16[2,2,2,64,256]{4,3,2,1,0:T(8,128)(2,1)S(1)} %collective-permute-done.8), channel_id=1, source_target_pairs={{0,4},{1,5},{2,6},{3,7},{4,0},{5,1},{6,2},{7,3},{8,12},{9,13},{10,... | collective-permute-start | bytes 786440 | tf_op jit(solution)/shard_map/ppermute | solution.py:39
  33.6 2.5 %collective-permute-start.14 = (bf16[2,2,2,64,384]{4,3,2,1,0:T(8,128)(2,1)S(1)}, bf16[2,2,2,64,384]{4,3,2,1,0:T(8,128)(2,1)S(1)}, u32[]{:S(2)}, u32[]{:S(2)}) collective-permute-start(bf16[2,2,2,64,384]{4,3,2,1,0:T(8,128)(2,1)S(1)} %collective-permute-done.7), channel_id=1, source_target_pairs={{0,1},{1,0},{2,3},{3,2},{4,5},{5,4},{6,7},{7,6},{8,9},{9,8},{10,11... | collective-permute-start | bytes 1179656 | tf_op jit(solution)/shard_map/ppermute | solution.py:39
  37.8 2.5 %collective-permute-start.11 = (bf16[2,4,2,64,384]{4,3,2,1,0:T(8,128)(2,1)S(1)}, bf16[2,4,2,64,384]{4,3,2,1,0:T(8,128)(2,1)}, u32[]{:S(2)}, u32[]{:S(2)}) collective-permute-start(bf16[2,4,2,64,384]{4,3,2,1,0:T(8,128)(2,1)S(1)} %pad_maximum_fusion.refs_0_), channel_id=1, source_target_pairs={{0,1},{1,0},{2,3},{3,2},{4,5},{5,4},{6,7},{7,6},{8,9},{9,8},{10,11... | collective-permute-start | bytes 2359304 | tf_op jit(solution)/shard_map/ppermute | solution.py:39
  42.5 2.6 %collective-permute-start.12 = (bf16[2,4,2,64,384]{4,3,2,1,0:T(8,128)(2,1)S(1)}, bf16[2,4,2,64,384]{4,3,2,1,0:T(8,128)(2,1)}, u32[]{:S(2)}, u32[]{:S(2)}) collective-permute-start(bf16[2,4,2,64,384]{4,3,2,1,0:T(8,128)(2,1)S(1)} %constant_dynamic-update-slice_fusion.4.refs_1_), channel_id=1, source_target_pairs={{0,1},{1,0},{2,3},{3,2},{4,5},{5,4},{6,7},{7,6},{8,9},{9,8},{10,11... | collective-permute-start | bytes 2359304 | tf_op jit(solution)/shard_map/ppermute | solution.py:39
  45.1 2.6 %collective-permute-start.16 = (bf16[4,2,2,64,384]{4,3,2,1,0:T(8,128)(2,1)}, bf16[4,2,2,64,384]{4,3,2,1,0:T(8,128)(2,1)}, u32[]{:S(2)}, u32[]{:S(2)}) collective-permute-start(bf16[4,2,2,64,384]{4,3,2,1,0:T(8,128)(2,1)} %constant_dynamic-update-slice_fusion.6.refs_3_.refs_5_), channel_id=1, source_target_pairs={{0,4},{1,5},{2,6},{3,7},{4,0},{5,1},{6,2},{7,3},{8,12},{9,13},{10,... | collective-permute-start | bytes 2359304 | tf_op jit(solution)/shard_map/ppermute | solution.py:39
  48.6 3.4 %copy-done = bf16[1,8192,512]{2,1,0:T(8,128)(2,1)S(1)} copy-done((bf16[1,8192,512]{2,1,0:T(8,128)(2,1)S(1)}, bf16[1,8192,512]{2,1,0:T(8,128)(2,1)}, u32[]{:S(2)}) %copy-start) | copy-done | bytes 8388632
  52.0 4.1 %sum_grads.1.summed = bf16[4,4,4,64,512]{4,3,2,1,0:T(8,128)(2,1)S(1)} custom-call(s32[4]{0:T(128)S(1)} %pad_add_fusion.where.refs_6_, bf16[8192,512]{1,0:T(8,128)(2,1)S(1)} %bitcast.17, bf16[8192,512]{1,0:T(8,128)(2,1)} %collective-permute-done.5.theirs), custom_call_target="tpu_custom_call" | custom-call | flops 2097152 | bytes 12582912 | tf_op jit(solution)/shard_map/sum_grads/pallas_call | solution.py:129
  56.1 3.6 %project.1 = (f32[1024,512]{1,0:T(8,128)S(1)}, bf16[2,2,4,2,64,384]{5,4,3,2,1,0:T(8,128)(2,1)S(1)}, bf16[2,4,2,2,64,384]{5,4,3,2,1,0:T(8,128)(2,1)S(1)}, bf16[2,2,2,4,64,256]{5,4,3,2,1,0:T(8,128)(2,1)S(1)}) custom-call(bf16[4,4,4,64,512]{4,3,2,1,0:T(8,128)(2,1)S(1)} %sum_grads.1.summed, bf16[2,4,2,64,384]{4,3,2,1,0:T(8,128)(2,1)S(1)} %pad_maximum_fusion.refs_0_, ...), custom_call_target="tpu_custom_call" | custom-call | flops 2147483648 | bytes 8388608 | tf_op jit(solution)/shard_map/project/pallas_call | solution.py:191
  59.7 2.5 %collective-permute-done.16.refs_3_.refs_7_ = bf16[4,2,2,64,384]{4,3,2,1,0:T(8,128)(2,1)} collective-permute-done((bf16[4,2,2,64,384]{4,3,2,1,0:T(8,128)(2,1)}, bf16[4,2,2,64,384]{4,3,2,1,0:T(8,128)(2,1)}, u32[]{:S(2)}, u32[]{:S(2)}) %collective-permute-start.16) | collective-permute-done | bytes 786464 | tf_op jit(solution)/shard_map/ppermute | solution.py:39
  62.3 5.2 %project_late.1 = (f32[1024,512]{1,0:T(8,128)S(1)}, f32[2,256,512]{2,1,0:T(8,128)S(1)}, bf16[2,2,4,2,64,384]{5,4,3,2,1,0:T(8,128)(2,1)S(1)}, bf16[2,4,2,2,64,384...) custom-call(bf16[4,4,4,64,512]{4,3,2,1,0:T(8,128)(2,1)S(1)} %sum_grads.1.summed, ...), custom_call_target="tpu_custom_call" | custom-call | flops 2147483648 | bytes 8388608 | tf_op jit(solution)/shard_map/project_late/pallas_call | solution.py:191
  67.4 6.2 %collective-permute-start.22 = (f32[2,256,512]{2,1,0:T(8,128)S(1)}, f32[2,256,512]{2,1,0:T(8,128)S(1)}, u32[]{:S(2)}, u32[]{:S(2)}) collective-permute-start(f32[2,256,512]{2,1,0:T(8,128)S(1)} %get-tuple-element.39), channel_id=1, source_target_pairs={{0,32},{1,33},{2,34},{3,35},{4,36},{5,37},{6,38},{7,39},{8,40},{9,... | collective-permute-start | bytes 3145736 | tf_op jit(solution)/shard_map/ppermute | solution.py:43
  74.2 1.7 %collective-permute-done.22.received = f32[2,256,512]{2,1,0:T(8,128)S(1)} collective-permute-done((f32[2,256,512]{2,1,0:T(8,128)S(1)}, f32[2,256,512]{2,1,0:T(8,128)S(1)}, u32[]{:S(2)}, u32[]{:S(2)}) %collective-permute-start.22) | collective-permute-done | bytes 1048608 | tf_op jit(solution)/shard_map/ppermute | solution.py:43
  77.8 8.6 %collective-permute-done.28.received = bf16[256,512]{1,0:T(8,128)(2,1)S(1)} collective-permute-done((bf16[256,512]{1,0:T(8,128)(2,1)S(1)}, bf16[256,512]{1,0:T(8,128)(2,1)S(1)}, u32[]{:S(2)}, u32[]{:S(2)}) %collective-permute-start.28) | collective-permute-done | bytes 262176 | tf_op jit(solution)/shard_map/ppermute | solution.py:47
  88.8 8.7 %collective-permute-done.30.refs_20_ = bf16[256,512]{1,0:T(8,128)(2,1)S(1)} collective-permute-done((bf16[256,512]{1,0:T(8,128)(2,1)S(1)}, bf16[256,512]{1,0:T(8,128)(2,1)S(1)}, u32[]{:S(2)}, u32[]{:S(2)}) %collective-permute-start.30) | collective-permute-done | bytes 262176 | tf_op jit(solution)/shard_map/ppermute | solution.py:47
  99.6 14.4 %back_project.1 = bf16[8192,512]{1,0:T(8,128)(2,1)} custom-call(s32[4]{0:T(128)S(1)} %pad_add_fusion.where.refs_6_, bf16[2,4,2,64,384]{4,3,2,1,0:T(8,128)(2,1)S(1)} %pad_maximum_fusion.refs_0_, bf16[2,4,2,64,384]{4,3,2,1,0:T(8,128)(2,1)S(1)} %constant_dynamic-update-slice_fusion.4.refs_1_, ...), custom_call_target="tpu_custom_call" | custom-call | flops 8589934592 | bytes 25165824 | tf_op jit(solution)/shard_map/back_project/pallas_call | solution.py:321
  (79 shorter events, 18.1 us)
Async XLA Ops:
  0.6 18.9 %collective-permute-start.5 = (bf16[8192,512]{1,0:T(8,128)(2,1)}, bf16[8192,512]{1,0:T(8,128)(2,1)}, u32[]{:S(2)}, u32[]{:S(2)}) collective-permute-start(bf16[8192,512]{1,0:T(8,128)(2,1)} %bitcast.16), channel_id=1, source_target_pairs={{0,32},{1,33},{2,34},{3,35},{4,36},{5,37},{6,38},{7,39},{8,40},{9,... | collective-permute-start | bytes 25165832 | tf_op jit(solution)/shard_map/ppermute | solution.py:43
  11.3 8.2 %collective-permute-start.4 = (bf16[3,64,1024]{2,1,0:T(8,128)(2,1)S(1)}, bf16[3,64,1024]{2,1,0:T(8,128)(2,1)S(1)}, u32[]{:S(2)}, u32[]{:S(2)}) collective-permute-start(bf16[3,64,1024]{2,1,0:T(8,128)(2,1)S(1)} %pad_maximum_fusion.3), channel_id=1, source_target_pairs={{0,16},{1,17},{2,18},{3,19},{4,20},{5,21},{6,22},{7,23},{8,24},{9,... | collective-permute-start | bytes 1179656 | tf_op jit(solution)/shard_map/ppermute | solution.py:39
  19.6 9.5 %collective-permute-start.6 = (bf16[2,2,2,64,384]{4,3,2,1,0:T(8,128)(2,1)S(1)}, bf16[2,2,2,64,384]{4,3,2,1,0:T(8,128)(2,1)S(1)}, u32[]{:S(2)}, u32[]{:S(2)}) collective-permute-start(bf16[2,2,2,64,384]{4,3,2,1,0:T(8,128)(2,1)S(1)} %get-tuple-element.52), channel_id=1, source_target_pairs={{0,4},{1,5},{2,6},{3,7},{4,0},{5,1},{6,2},{7,3},{8,12},{9,13},{10,... | collective-permute-start | bytes 1179656 | tf_op jit(solution)/shard_map/ppermute | solution.py:39
  25.0 8.5 %collective-permute-start.9 = (bf16[2,2,2,64,384]{4,3,2,1,0:T(8,128)(2,1)S(1)}, bf16[2,2,2,64,384]{4,3,2,1,0:T(8,128)(2,1)S(1)}, u32[]{:S(2)}, u32[]{:S(2)}) collective-permute-start(bf16[2,2,2,64,384]{4,3,2,1,0:T(8,128)(2,1)S(1)} %get-tuple-element.52), channel_id=1, source_target_pairs={{0,80},{1,81},{2,82},{3,83},{4,84},{5,85},{6,86},{7,87},{8,88},{9,... | collective-permute-start | bytes 1179656 | tf_op jit(solution)/shard_map/ppermute | solution.py:39
  26.5 9.7 %collective-permute-start.13 = (bf16[2,2,2,64,384]{4,3,2,1,0:T(8,128)(2,1)S(1)}, bf16[2,2,2,64,384]{4,3,2,1,0:T(8,128)(2,1)S(1)}, u32[]{:S(2)}, u32[]{:S(2)}) collective-permute-start(bf16[2,2,2,64,384]{4,3,2,1,0:T(8,128)(2,1)S(1)} %get-tuple-element.51), channel_id=1, source_target_pairs={{0,1},{1,0},{2,3},{3,2},{4,5},{5,4},{6,7},{7,6},{8,9},{9,8},{10,11... | collective-permute-start | bytes 1179656 | tf_op jit(solution)/shard_map/ppermute | solution.py:39
  29.0 13.5 %collective-permute-start.17 = (bf16[2,2,2,64,256]{4,3,2,1,0:T(8,128)(2,1)S(1)}, bf16[2,2,2,64,256]{4,3,2,1,0:T(8,128)(2,1)S(1)}, u32[]{:S(2)}, u32[]{:S(2)}) collective-permute-start(bf16[2,2,2,64,256]{4,3,2,1,0:T(8,128)(2,1)S(1)} %slice.12), channel_id=1, source_target_pairs={{0,4},{1,5},{2,6},{3,7},{4,0},{5,1},{6,2},{7,3},{8,12},{9,13},{10,... | collective-permute-start | bytes 786440 | tf_op jit(solution)/shard_map/ppermute | solution.py:39
  29.4 8.3 %collective-permute-start.10 = (bf16[2,2,2,64,384]{4,3,2,1,0:T(8,128)(2,1)S(1)}, bf16[2,2,2,64,384]{4,3,2,1,0:T(8,128)(2,1)S(1)}, u32[]{:S(2)}, u32[]{:S(2)}) collective-permute-start(bf16[2,2,2,64,384]{4,3,2,1,0:T(8,128)(2,1)S(1)} %collective-permute-done.6), channel_id=1, source_target_pairs={{0,80},{1,81},{2,82},{3,83},{4,84},{5,85},{6,86},{7,87},{8,88},{9,... | collective-permute-start | bytes 1179656 | tf_op jit(solution)/shard_map/ppermute | solution.py:39
  30.8 14.3 %collective-permute-start.18 = (bf16[2,2,2,64,256]{4,3,2,1,0:T(8,128)(2,1)S(1)}, bf16[2,2,2,64,256]{4,3,2,1,0:T(8,128)(2,1)S(1)}, u32[]{:S(2)}, u32[]{:S(2)}) collective-permute-start(bf16[2,2,2,64,256]{4,3,2,1,0:T(8,128)(2,1)S(1)} %collective-permute-done.8), channel_id=1, source_target_pairs={{0,4},{1,5},{2,6},{3,7},{4,0},{5,1},{6,2},{7,3},{8,12},{9,13},{10,... | collective-permute-start | bytes 786440 | tf_op jit(solution)/shard_map/ppermute | solution.py:39
  33.6 7.8 %collective-permute-start.14 = (bf16[2,2,2,64,384]{4,3,2,1,0:T(8,128)(2,1)S(1)}, bf16[2,2,2,64,384]{4,3,2,1,0:T(8,128)(2,1)S(1)}, u32[]{:S(2)}, u32[]{:S(2)}) collective-permute-start(bf16[2,2,2,64,384]{4,3,2,1,0:T(8,128)(2,1)S(1)} %collective-permute-done.7), channel_id=1, source_target_pairs={{0,1},{1,0},{2,3},{3,2},{4,5},{5,4},{6,7},{7,6},{8,9},{9,8},{10,11... | collective-permute-start | bytes 1179656 | tf_op jit(solution)/shard_map/ppermute | solution.py:39
  36.2 11.5 %collective-permute-start.19 = (bf16[2,2,4,64,256]{4,3,2,1,0:T(8,128)(2,1)S(1)}, bf16[2,2,4,64,256]{4,3,2,1,0:T(8,128)(2,1)S(1)}, u32[]{:S(2)}, u32[]{:S(2)}) collective-permute-start(bf16[2,2,4,64,256]{4,3,2,1,0:T(8,128)(2,1)S(1)} %pad_maximum_fusion.2.refs_4_.refs_8_), channel_id=1, source_target_pairs={{0,80},{1,81},{2,82},{3,83},{4,84},{5,85},{6,86},{7,87},{8,88},{9,... | collective-permute-start | bytes 1572872 | tf_op jit(solution)/shard_map/ppermute | solution.py:39
  37.8 21.9 %collective-permute-start.11 = (bf16[2,4,2,64,384]{4,3,2,1,0:T(8,128)(2,1)S(1)}, bf16[2,4,2,64,384]{4,3,2,1,0:T(8,128)(2,1)}, u32[]{:S(2)}, u32[]{:S(2)}) collective-permute-start(bf16[2,4,2,64,384]{4,3,2,1,0:T(8,128)(2,1)S(1)} %pad_maximum_fusion.refs_0_), channel_id=1, source_target_pairs={{0,1},{1,0},{2,3},{3,2},{4,5},{5,4},{6,7},{7,6},{8,9},{9,8},{10,11... | collective-permute-start | bytes 2359304 | tf_op jit(solution)/shard_map/ppermute | solution.py:39
  41.4 18.3 %collective-permute-start.15 = (bf16[4,2,2,64,384]{4,3,2,1,0:T(8,128)(2,1)S(1)}, bf16[4,2,2,64,384]{4,3,2,1,0:T(8,128)(2,1)}, u32[]{:S(2)}, u32[]{:S(2)}) collective-permute-start(bf16[4,2,2,64,384]{4,3,2,1,0:T(8,128)(2,1)S(1)} %pad_maximum_fusion.1.refs_2_.refs_4_), channel_id=1, source_target_pairs={{0,4},{1,5},{2,6},{3,7},{4,0},{5,1},{6,2},{7,3},{8,12},{9,13},{10,... | collective-permute-start | bytes 2359304 | tf_op jit(solution)/shard_map/ppermute | solution.py:39
  42.5 17.2 %collective-permute-start.12 = (bf16[2,4,2,64,384]{4,3,2,1,0:T(8,128)(2,1)S(1)}, bf16[2,4,2,64,384]{4,3,2,1,0:T(8,128)(2,1)}, u32[]{:S(2)}, u32[]{:S(2)}) collective-permute-start(bf16[2,4,2,64,384]{4,3,2,1,0:T(8,128)(2,1)S(1)} %constant_dynamic-update-slice_fusion.4.refs_1_), channel_id=1, source_target_pairs={{0,1},{1,0},{2,3},{3,2},{4,5},{5,4},{6,7},{7,6},{8,9},{9,8},{10,11... | collective-permute-start | bytes 2359304 | tf_op jit(solution)/shard_map/ppermute | solution.py:39
  45.1 17.2 %collective-permute-start.16 = (bf16[4,2,2,64,384]{4,3,2,1,0:T(8,128)(2,1)}, bf16[4,2,2,64,384]{4,3,2,1,0:T(8,128)(2,1)}, u32[]{:S(2)}, u32[]{:S(2)}) collective-permute-start(bf16[4,2,2,64,384]{4,3,2,1,0:T(8,128)(2,1)} %constant_dynamic-update-slice_fusion.6.refs_3_.refs_5_), channel_id=1, source_target_pairs={{0,4},{1,5},{2,6},{3,7},{4,0},{5,1},{6,2},{7,3},{8,12},{9,13},{10,... | collective-permute-start | bytes 2359304 | tf_op jit(solution)/shard_map/ppermute | solution.py:39
  48.5 11.2 %collective-permute-start.20 = (bf16[2,2,4,64,256]{4,3,2,1,0:T(8,128)(2,1)S(1)}, bf16[2,2,4,64,256]{4,3,2,1,0:T(8,128)(2,1)}, u32[]{:S(2)}, u32[]{:S(2)}) collective-permute-start(bf16[2,2,4,64,256]{4,3,2,1,0:T(8,128)(2,1)S(1)} %constant_dynamic-update-slice_fusion.8.refs_5_.refs_9_), channel_id=1, source_target_pairs={{0,80},{1,81},{2,82},{3,83},{4,84},{5,85},{6,86},{7,87},{8,88},{9,... | collective-permute-start | bytes 1572872 | tf_op jit(solution)/shard_map/ppermute | solution.py:39
  67.4 8.5 %collective-permute-start.22 = (f32[2,256,512]{2,1,0:T(8,128)S(1)}, f32[2,256,512]{2,1,0:T(8,128)S(1)}, u32[]{:S(2)}, u32[]{:S(2)}) collective-permute-start(f32[2,256,512]{2,1,0:T(8,128)S(1)} %get-tuple-element.39), channel_id=1, source_target_pairs={{0,32},{1,33},{2,34},{3,35},{4,36},{5,37},{6,38},{7,39},{8,40},{9,... | collective-permute-start | bytes 3145736 | tf_op jit(solution)/shard_map/ppermute | solution.py:43
  73.7 14.3 %collective-permute-start.21 = (bf16[2,2,4,2,64,384]{5,4,3,2,1,0:T(8,128)(2,1)S(1)}, bf16[2,2,4,2,64,384]{5,4,3,2,1,0:T(8,128)(2,1)S(1)}, u32[]{:S(2)}, u32[]{:S(2)}) collective-permute-start(bf16[2,2,4,2,64,384]{5,4,3,2,1,0:T(8,128)(2,1)S(1)} %get-tuple-element.36), channel_id=1, source_target_pairs={{0,32},{1,33},{2,34},{3,35},{4,36},{5,37},{6,38},{7,39},{8,40},{9,... | collective-permute-start | bytes 4718600 | tf_op jit(solution)/shard_map/ppermute | solution.py:43
  74.1 14.4 %collective-permute-start.24 = (bf16[2,4,2,2,64,384]{5,4,3,2,1,0:T(8,128)(2,1)S(1)}, bf16[2,4,2,2,64,384]{5,4,3,2,1,0:T(8,128)(2,1)S(1)}, u32[]{:S(2)}, u32[]{:S(2)}) collective-permute-start(bf16[2,4,2,2,64,384]{5,4,3,2,1,0:T(8,128)(2,1)S(1)} %get-tuple-element.45), channel_id=1, source_target_pairs={{0,32},{1,33},{2,34},{3,35},{4,36},{5,37},{6,38},{7,39},{8,40},{9,... | collective-permute-start | bytes 4718600 | tf_op jit(solution)/shard_map/ppermute | solution.py:43
  76.6 23.0 %collective-permute-start.23 = (bf16[2,2,4,2,64,384]{5,4,3,2,1,0:T(8,128)(2,1)S(1)}, bf16[2,2,4,2,64,384]{5,4,3,2,1,0:T(8,128)(2,1)S(1)}, u32[]{:S(2)}, u32[]{:S(2)}) collective-permute-start(bf16[2,2,4,2,64,384]{5,4,3,2,1,0:T(8,128)(2,1)S(1)} %get-tuple-element.44), channel_id=1, source_target_pairs={{0,32},{1,33},{2,34},{3,35},{4,36},{5,37},{6,38},{7,39},{8,40},{9,... | collective-permute-start | bytes 4718600 | tf_op jit(solution)/shard_map/ppermute | solution.py:43
  77.0 22.5 %collective-permute-start.25 = (bf16[2,4,2,2,64,384]{5,4,3,2,1,0:T(8,128)(2,1)S(1)}, bf16[2,4,2,2,64,384]{5,4,3,2,1,0:T(8,128)(2,1)S(1)}, u32[]{:S(2)}, u32[]{:S(2)}) collective-permute-start(bf16[2,4,2,2,64,384]{5,4,3,2,1,0:T(8,128)(2,1)S(1)} %get-tuple-element.46), channel_id=1, source_target_pairs={{0,32},{1,33},{2,34},{3,35},{4,36},{5,37},{6,38},{7,39},{8,40},{9,... | collective-permute-start | bytes 4718600 | tf_op jit(solution)/shard_map/ppermute | solution.py:43
  77.4 9.0 %collective-permute-start.28 = (bf16[256,512]{1,0:T(8,128)(2,1)S(1)}, bf16[256,512]{1,0:T(8,128)(2,1)S(1)}, u32[]{:S(2)}, u32[]{:S(2)}) collective-permute-start(bf16[256,512]{1,0:T(8,128)(2,1)S(1)} %get-tuple-element.50), channel_id=1, source_target_pairs={{0,64},{1,65},{2,66},{3,67},{4,68},{5,69},{6,70},{7,71},{8,72},{9,... | collective-permute-start | bytes 786440 | tf_op jit(solution)/shard_map/ppermute | solution.py:47
  86.4 13.1 %collective-permute-start.27 = (bf16[2,2,2,4,64,256]{5,4,3,2,1,0:T(8,128)(2,1)S(1)}, bf16[2,2,2,4,64,256]{5,4,3,2,1,0:T(8,128)(2,1)S(1)}, u32[]{:S(2)}, u32[]{:S(2)}) collective-permute-start(bf16[2,2,2,4,64,256]{5,4,3,2,1,0:T(8,128)(2,1)S(1)} %get-tuple-element.48), channel_id=1, source_target_pairs={{0,32},{1,33},{2,34},{3,35},{4,36},{5,37},{6,38},{7,39},{8,40},{9,... | collective-permute-start | bytes 3145736 | tf_op jit(solution)/shard_map/ppermute | solution.py:43
  88.0 9.5 %collective-permute-start.30 = (bf16[256,512]{1,0:T(8,128)(2,1)S(1)}, bf16[256,512]{1,0:T(8,128)(2,1)S(1)}, u32[]{:S(2)}, u32[]{:S(2)}) collective-permute-start(bf16[256,512]{1,0:T(8,128)(2,1)S(1)} %direction.1.refs_18_), channel_id=1, source_target_pairs={{0,64},{1,65},{2,66},{3,67},{4,68},{5,69},{6,70},{7,71},{8,72},{9,... | collective-permute-start | bytes 786440 | tf_op jit(solution)/shard_map/ppermute | solution.py:47
  88.6 11.0 %collective-permute-start.29 = (bf16[256,512]{1,0:T(8,128)(2,1)S(1)}, bf16[256,512]{1,0:T(8,128)(2,1)S(1)}, u32[]{:S(2)}, u32[]{:S(2)}) collective-permute-start(bf16[256,512]{1,0:T(8,128)(2,1)S(1)} %direction.1.refs_18_), channel_id=1, source_target_pairs={{0,32},{1,33},{2,34},{3,35},{4,36},{5,37},{6,38},{7,39},{8,40},{9,... | collective-permute-start | bytes 786440 | tf_op jit(solution)/shard_map/ppermute | solution.py:43
  (14 other events, 79.6 us)

commit v5 on v4

--- a/solution.py
+++ b/solution.py
@@ -139,7 +139,7 @@
         compiler_params=pltpu.CompilerParams(vmem_limit_bytes=40 * MIB),
         cost_estimate=pl.CostEstimate(flops=4096 * columns, bytes_accessed=24576 * columns, transcendentals=0),
         name="sum_grads",
-    )(where, grads, theirs)
+    )(where, *[pltpu.with_memory_space_constraint(value, pltpu.HBM) for value in (grads, theirs)])
 
 
 def project_kernel(late, summed, *refs):
@@ -350,12 +350,13 @@
     held, theirs = together(cube(basis), theirs)
     eighths = [held[..., low:high] for low, high, _ in STREAMS]
     got = [exchange(eighth, axes[0], 1) for eighth, (_, _, axes) in zip(eighths, STREAMS)]
-    ahead = [exchange(eighth, axes[1], 1) for eighth, (_, _, axes) in zip(eighths, STREAMS)]
+    ahead = [exchange(eighth, axes[1], 1) for eighth, (_, _, axes) in zip(eighths[:2], STREAMS)]
     got = together(*got)
     halves = [join(eighth, other, axes[0]) for eighth, other, (_, _, axes) in zip(eighths, got, STREAMS)]
-    behind = [exchange(other, axes[1], 1) for other, (_, _, axes) in zip(got, STREAMS)]
+    behind = [exchange(other, axes[1], 1) for other, (_, _, axes) in zip(got[:2], STREAMS)]
     third = [exchange(half, axes[2], 1) for half, (_, _, axes) in zip(halves, STREAMS)]
     second = [join(first, last, axes[0]) for first, last, (_, _, axes) in zip(ahead, behind, STREAMS)]
+    second.append(exchange(halves[2], STREAMS[2][2][1], 1))
     fourth = [exchange(got, axes[2], 1) for got, (_, _, axes) in zip(second, STREAMS)]
     early = [piece for pair in zip(halves, second) for piece in pair]
     late = [piece for pair in zip(third, fourth) for piece in pair]

time: 114 us -> 112 us (0.982)
  waiting for transfers between devices: 32.7 us -> 38.1 us
  starting transfers between devices: 43.3 us -> 38 us
  local copies, waits for them, and re-layouts: 7.09 us -> 3.69 us
    ppermute x20 -> x19, starting transfers between devices: 31.3 us -> 25.8 us  [exchange(): return lax.ppermute(value, BOTH, pairs(partner))]
    ppermute x20 -> x19, waiting for transfers between devices: 13.4 us -> 18 us  [exchange(): return lax.ppermute(value, BOTH, pairs(partner))]
    unnamed x20 -> x17, local copies, waits for them, and re-layouts: 6.03 us -> 2.64 us
  transfers between devices with their start and end apart: 32 -> 31, of which waited for: 13 -> 13; matrix products, arithmetic and copies ran while one was open for 3% -> 3% of each run, Pallas kernels for 8% -> 9%
where the time goes in v5:
time: 112 us
  waiting for transfers between devices  38.1 us (34%)
  starting transfers between devices  38 us (34%)
  Pallas kernels  29.1 us (26%)
  local copies, waits for them, and re-layouts  3.69 us (3%)
  other arithmetic  1.54 us (1%)
    ppermute x19, starting transfers between devices, exchange(): return lax.ppermute(value, BOTH, pairs(partner))  25.8 us
    ppermute x2, waiting for transfers between devices, swap_far(): return lax.ppermute(value, BOTH, pairs(lambda c, z, y, x: (c, z ^ 2, y, x)))  18.2 us
    ppermute x19, waiting for transfers between devices, exchange(): return lax.ppermute(value, BOTH, pairs(partner))  18 us
    pallas_call x1, Pallas kernels, back_project(): pl.pallas_call(update_kernel, out_shape=jax.ShapeDtypeStruct((rows, colum...  14.4 us
    ppermute x10, starting transfers between devices, swap_core(): return lax.ppermute(value, BOTH, pairs(lambda c, z, y, x: (1 - c, z, y, x)))  12.1 us
    pallas_call x2, Pallas kernels, project(): pl.pallas_call(functools.partial(project_kernel, late), out_shape=result...  8.77 us
    pallas_call x1, Pallas kernels, sum_grads(): pl.pallas_call(sum_kernel, out_shape=jax.ShapeDtypeStruct((4, 4, 4, 64, c...  4.79 us
    unnamed x17, local copies, waits for them, and re-layouts  2.64 us
  transfers between devices with their start and end apart: 31, of which 13 were waited for; matrix products, arithmetic and copies ran while one was open for 3% of the time, Pallas kernels for 9%

profile of v5, /device:TPU:1, one launch (start us, length us, event | category | flops | bytes accessed | tf_op | source)
XLA Modules:
  0.0 111.5 jit_solution(1193062906372644989)
XLA Ops:
  0.6 1.5 %collective-permute-start.5 = (bf16[8192,512]{1,0:T(8,128)(2,1)}, bf16[8192,512]{1,0:T(8,128)(2,1)}, u32[]{:S(2)}, u32[]{:S(2)}) collective-permute-start(bf16[8192,512]{1,0:T(8,128)(2,1)} %bitcast.16), channel_id=1, source_target_pairs={{0,32},{1,33},{2,34},{3,35},{4,36},{5,37},{6,38},{7,39},{8,40},{9,... | collective-permute-start | bytes 25165832 | tf_op jit(solution)/shard_map/ppermute | solution.py:43
  2.1 1.3 %collective-permute-start = (bf16[64,1024]{1,0:T(8,128)(2,1)}, bf16[64,1024]{1,0:T(8,128)(2,1)S(1)}, u32[]{:S(2)}, u32[]{:S(2)}) collective-permute-start(bf16[64,1024]{1,0:T(8,128)(2,1)} %source.1), channel_id=1, source_target_pairs={{0,3},{1,2},{2,1},{3,0},{4,7},{5,6},{6,5},{7,4},{8,11},{9,10},{10,... | collective-permute-start | bytes 393224 | tf_op jit(solution)/shard_map/ppermute | solution.py:39
  3.4 1.3 %collective-permute-start.1 = (bf16[64,1024]{1,0:T(8,128)(2,1)}, bf16[64,1024]{1,0:T(8,128)(2,1)S(1)}, u32[]{:S(2)}, u32[]{:S(2)}) collective-permute-start(bf16[64,1024]{1,0:T(8,128)(2,1)} %source.1), channel_id=1, source_target_pairs={{0,12},{1,13},{2,14},{3,15},{4,8},{5,9},{6,10},{7,11},{8,4},{9,5},... | collective-permute-start | bytes 393224 | tf_op jit(solution)/shard_map/ppermute | solution.py:39
  4.8 3.8 %collective-permute-start.3 = (bf16[64,1024]{1,0:T(8,128)(2,1)}, bf16[64,1024]{1,0:T(8,128)(2,1)S(1)}, u32[]{:S(2)}, u32[]{:S(2)}) collective-permute-start(bf16[64,1024]{1,0:T(8,128)(2,1)} %source.1), channel_id=1, source_target_pairs={{0,16},{1,17},{2,18},{3,19},{4,20},{5,21},{6,22},{7,23},{8,24},{9,... | collective-permute-start | bytes 393224 | tf_op jit(solution)/shard_map/ppermute | solution.py:39
  9.9 1.3 %collective-permute-done.3 = bf16[64,1024]{1,0:T(8,128)(2,1)S(1)} collective-permute-done((bf16[64,1024]{1,0:T(8,128)(2,1)}, bf16[64,1024]{1,0:T(8,128)(2,1)S(1)}, u32[]{:S(2)}, u32[]{:S(2)}) %collective-permute-start.3) | collective-permute-done | bytes 131104 | tf_op jit(solution)/shard_map/ppermute | solution.py:39
  11.3 3.0 %collective-permute-start.4 = (bf16[3,64,1024]{2,1,0:T(8,128)(2,1)S(1)}, bf16[3,64,1024]{2,1,0:T(8,128)(2,1)S(1)}, u32[]{:S(2)}, u32[]{:S(2)}) collective-permute-start(bf16[3,64,1024]{2,1,0:T(8,128)(2,1)S(1)} %pad_maximum_fusion.3), channel_id=1, source_target_pairs={{0,16},{1,17},{2,18},{3,19},{4,20},{5,21},{6,22},{7,23},{8,24},{9,... | collective-permute-start | bytes 1179656 | tf_op jit(solution)/shard_map/ppermute | solution.py:39
  14.4 5.1 %collective-permute-done.4 = bf16[3,64,1024]{2,1,0:T(8,128)(2,1)S(1)} collective-permute-done((bf16[3,64,1024]{2,1,0:T(8,128)(2,1)S(1)}, bf16[3,64,1024]{2,1,0:T(8,128)(2,1)S(1)}, u32[]{:S(2)}, u32[]{:S(2)}) %collective-permute-start.4) | collective-permute-done | bytes 393248 | tf_op jit(solution)/shard_map/ppermute | solution.py:39
  19.6 2.8 %collective-permute-start.6 = (bf16[2,2,2,64,384]{4,3,2,1,0:T(8,128)(2,1)S(1)}, bf16[2,2,2,64,384]{4,3,2,1,0:T(8,128)(2,1)S(1)}, u32[]{:S(2)}, u32[]{:S(2)}) collective-permute-start(bf16[2,2,2,64,384]{4,3,2,1,0:T(8,128)(2,1)S(1)} %get-tuple-element.52), channel_id=1, source_target_pairs={{0,4},{1,5},{2,6},{3,7},{4,0},{5,1},{6,2},{7,3},{8,12},{9,13},{10,... | collective-permute-start | bytes 1179656 | tf_op jit(solution)/shard_map/ppermute | solution.py:39
  22.5 2.6 %collective-permute-start.8 = (bf16[2,2,2,64,256]{4,3,2,1,0:T(8,128)(2,1)S(1)}, bf16[2,2,2,64,256]{4,3,2,1,0:T(8,128)(2,1)S(1)}, u32[]{:S(2)}, u32[]{:S(2)}) collective-permute-start(bf16[2,2,2,64,256]{4,3,2,1,0:T(8,128)(2,1)S(1)} %slice.12), channel_id=1, source_target_pairs={{0,1},{1,0},{2,3},{3,2},{4,5},{5,4},{6,7},{7,6},{8,9},{9,8},{10,11... | collective-permute-start | bytes 786440 | tf_op jit(solution)/shard_map/ppermute | solution.py:39
  25.0 1.5 %collective-permute-start.9 = (bf16[2,2,2,64,384]{4,3,2,1,0:T(8,128)(2,1)S(1)}, bf16[2,2,2,64,384]{4,3,2,1,0:T(8,128)(2,1)S(1)}, u32[]{:S(2)}, u32[]{:S(2)}) collective-permute-start(bf16[2,2,2,64,384]{4,3,2,1,0:T(8,128)(2,1)S(1)} %get-tuple-element.52), channel_id=1, source_target_pairs={{0,80},{1,81},{2,82},{3,83},{4,84},{5,85},{6,86},{7,87},{8,88},{9,... | collective-permute-start | bytes 1179656 | tf_op jit(solution)/shard_map/ppermute | solution.py:39
  26.7 2.3 %collective-permute-done.8 = bf16[2,2,2,64,256]{4,3,2,1,0:T(8,128)(2,1)S(1)} collective-permute-done((bf16[2,2,2,64,256]{4,3,2,1,0:T(8,128)(2,1)S(1)}, bf16[2,2,2,64,256]{4,3,2,1,0:T(8,128)(2,1)S(1)}, u32[]{:S(2)}, u32[]{:S(2)}) %collective-permute-start.8) | collective-permute-done | bytes 262176 | tf_op jit(solution)/shard_map/ppermute | solution.py:39
  30.9 1.4 %collective-permute-start.18 = (bf16[2,2,4,64,256]{4,3,2,1,0:T(8,128)(2,1)S(1)}, bf16[2,2,4,64,256]{4,3,2,1,0:T(8,128)(2,1)S(1)}, u32[]{:S(2)}, u32[]{:S(2)}) collective-permute-start(bf16[2,2,4,64,256]{4,3,2,1,0:T(8,128)(2,1)S(1)} %pad_maximum_fusion.2.refs_4_.refs_8_), channel_id=1, source_target_pairs={{0,80},{1,81},{2,82},{3,83},{4,84},{5,85},{6,86},{7,87},{8,88},{9,... | collective-permute-start | bytes 1572872 | tf_op jit(solution)/shard_map/ppermute | solution.py:39
  33.6 2.5 %collective-permute-start.14 = (bf16[2,2,2,64,384]{4,3,2,1,0:T(8,128)(2,1)S(1)}, bf16[2,2,2,64,384]{4,3,2,1,0:T(8,128)(2,1)S(1)}, u32[]{:S(2)}, u32[]{:S(2)}) collective-permute-start(bf16[2,2,2,64,384]{4,3,2,1,0:T(8,128)(2,1)S(1)} %collective-permute-done.7), channel_id=1, source_target_pairs={{0,1},{1,0},{2,3},{3,2},{4,5},{5,4},{6,7},{7,6},{8,9},{9,8},{10,11... | collective-permute-start | bytes 1179656 | tf_op jit(solution)/shard_map/ppermute | solution.py:39
  37.9 3.8 %collective-permute-done.14 = bf16[2,2,2,64,384]{4,3,2,1,0:T(8,128)(2,1)S(1)} collective-permute-done((bf16[2,2,2,64,384]{4,3,2,1,0:T(8,128)(2,1)S(1)}, bf16[2,2,2,64,384]{4,3,2,1,0:T(8,128)(2,1)S(1)}, u32[]{:S(2)}, u32[]{:S(2)}) %collective-permute-start.14) | collective-permute-done | bytes 393248 | tf_op jit(solution)/shard_map/ppermute | solution.py:39
  41.7 2.5 %collective-permute-start.12 = (bf16[2,4,2,64,384]{4,3,2,1,0:T(8,128)(2,1)S(1)}, bf16[2,4,2,64,384]{4,3,2,1,0:T(8,128)(2,1)}, u32[]{:S(2)}, u32[]{:S(2)}) collective-permute-start(bf16[2,4,2,64,384]{4,3,2,1,0:T(8,128)(2,1)S(1)} %constant_dynamic-update-slice_fusion.4.refs_1_), channel_id=1, source_target_pairs={{0,1},{1,0},{2,3},{3,2},{4,5},{5,4},{6,7},{7,6},{8,9},{9,8},{10,11... | collective-permute-start | bytes 2359304 | tf_op jit(solution)/shard_map/ppermute | solution.py:39
  46.9 4.8 %sum_grads.1.summed = bf16[4,4,4,64,512]{4,3,2,1,0:T(8,128)(2,1)S(1)} custom-call(s32[4]{0:T(128)S(1)} %pad_add_fusion.where.refs_6_, bf16[8192,512]{1,0:T(8,128)(2,1)} %bitcast.17, bf16[8192,512]{1,0:T(8,128)(2,1)} %collective-permute-done.5.theirs), custom_call_target="tpu_custom_call" | custom-call | flops 2097152 | bytes 12582912 | tf_op jit(solution)/shard_map/sum_grads/pallas_call | solution.py:129
  51.7 3.6 %project.1 = (f32[1024,512]{1,0:T(8,128)S(1)}, bf16[2,2,4,2,64,384]{5,4,3,2,1,0:T(8,128)(2,1)S(1)}, bf16[2,4,2,2,64,384]{5,4,3,2,1,0:T(8,128)(2,1)S(1)}, bf16[2,2,2,4,64,256]{5,4,3,2,1,0:T(8,128)(2,1)S(1)}) custom-call(bf16[4,4,4,64,512]{4,3,2,1,0:T(8,128)(2,1)S(1)} %sum_grads.1.summed, bf16[2,4,2,64,384]{4,3,2,1,0:T(8,128)(2,1)S(1)} %pad_maximum_fusion.refs_0_, ...), custom_call_target="tpu_custom_call" | custom-call | flops 2147483648 | bytes 8388608 | tf_op jit(solution)/shard_map/project/pallas_call | solution.py:191
  55.4 3.3 %collective-permute-done.12.refs_1_.refs_3_ = bf16[2,4,2,64,384]{4,3,2,1,0:T(8,128)(2,1)} collective-permute-done((bf16[2,4,2,64,384]{4,3,2,1,0:T(8,128)(2,1)S(1)}, bf16[2,4,2,64,384]{4,3,2,1,0:T(8,128)(2,1)}, u32[]{:S(2)}, u32[]{:S(2)}) %collective-permute-start.12) | collective-permute-done | bytes 786464 | tf_op jit(solution)/shard_map/ppermute | solution.py:39
  58.7 5.2 %project_late.1 = (f32[1024,512]{1,0:T(8,128)S(1)}, f32[2,256,512]{2,1,0:T(8,128)S(1)}, bf16[2,2,4,2,64,384]{5,4,3,2,1,0:T(8,128)(2,1)S(1)}, bf16[2,4,2,2,64,384...) custom-call(bf16[4,4,4,64,512]{4,3,2,1,0:T(8,128)(2,1)S(1)} %sum_grads.1.summed, ...), custom_call_target="tpu_custom_call" | custom-call | flops 2147483648 | bytes 8388608 | tf_op jit(solution)/shard_map/project_late/pallas_call | solution.py:191
  63.8 7.2 %collective-permute-start.21 = (f32[2,256,512]{2,1,0:T(8,128)S(1)}, f32[2,256,512]{2,1,0:T(8,128)S(1)}, u32[]{:S(2)}, u32[]{:S(2)}) collective-permute-start(f32[2,256,512]{2,1,0:T(8,128)S(1)} %get-tuple-element.39), channel_id=1, source_target_pairs={{0,32},{1,33},{2,34},{3,35},{4,36},{5,37},{6,38},{7,39},{8,40},{9,... | collective-permute-start | bytes 3145736 | tf_op jit(solution)/shard_map/ppermute | solution.py:43
  71.6 1.7 %collective-permute-done.21.received = f32[2,256,512]{2,1,0:T(8,128)S(1)} collective-permute-done((f32[2,256,512]{2,1,0:T(8,128)S(1)}, f32[2,256,512]{2,1,0:T(8,128)S(1)}, u32[]{:S(2)}, u32[]{:S(2)}) %collective-permute-start.21) | collective-permute-done | bytes 1048608 | tf_op jit(solution)/shard_map/ppermute | solution.py:43
  74.8 9.0 %collective-permute-done.27.received = bf16[256,512]{1,0:T(8,128)(2,1)S(1)} collective-permute-done((bf16[256,512]{1,0:T(8,128)(2,1)S(1)}, bf16[256,512]{1,0:T(8,128)(2,1)S(1)}, u32[]{:S(2)}, u32[]{:S(2)}) %collective-permute-start.27) | collective-permute-done | bytes 262176 | tf_op jit(solution)/shard_map/ppermute | solution.py:47
  85.8 9.1 %collective-permute-done.29.refs_20_ = bf16[256,512]{1,0:T(8,128)(2,1)S(1)} collective-permute-done((bf16[256,512]{1,0:T(8,128)(2,1)S(1)}, bf16[256,512]{1,0:T(8,128)(2,1)S(1)}, u32[]{:S(2)}, u32[]{:S(2)}) %collective-permute-start.29) | collective-permute-done | bytes 262176 | tf_op jit(solution)/shard_map/ppermute | solution.py:47
  96.9 14.4 %back_project.1 = bf16[8192,512]{1,0:T(8,128)(2,1)} custom-call(s32[4]{0:T(128)S(1)} %pad_add_fusion.where.refs_6_, bf16[2,4,2,64,384]{4,3,2,1,0:T(8,128)(2,1)S(1)} %pad_maximum_fusion.refs_0_, bf16[2,4,2,64,384]{4,3,2,1,0:T(8,128)(2,1)S(1)} %constant_dynamic-update-slice_fusion.4.refs_1_, ...), custom_call_target="tpu_custom_call" | custom-call | flops 8589934592 | bytes 25165824 | tf_op jit(solution)/shard_map/back_project/pallas_call | solution.py:321
  (73 shorter events, 15.6 us)
Async XLA Ops:
  0.6 18.9 %collective-permute-start.5 = (bf16[8192,512]{1,0:T(8,128)(2,1)}, bf16[8192,512]{1,0:T(8,128)(2,1)}, u32[]{:S(2)}, u32[]{:S(2)}) collective-permute-start(bf16[8192,512]{1,0:T(8,128)(2,1)} %bitcast.16), channel_id=1, source_target_pairs={{0,32},{1,33},{2,34},{3,35},{4,36},{5,37},{6,38},{7,39},{8,40},{9,... | collective-permute-start | bytes 25165832 | tf_op jit(solution)/shard_map/ppermute | solution.py:43
  2.1 7.6 %collective-permute-start = (bf16[64,1024]{1,0:T(8,128)(2,1)}, bf16[64,1024]{1,0:T(8,128)(2,1)S(1)}, u32[]{:S(2)}, u32[]{:S(2)}) collective-permute-start(bf16[64,1024]{1,0:T(8,128)(2,1)} %source.1), channel_id=1, source_target_pairs={{0,3},{1,2},{2,1},{3,0},{4,7},{5,6},{6,5},{7,4},{8,11},{9,10},{10,... | collective-permute-start | bytes 393224 | tf_op jit(solution)/shard_map/ppermute | solution.py:39
  11.3 8.2 %collective-permute-start.4 = (bf16[3,64,1024]{2,1,0:T(8,128)(2,1)S(1)}, bf16[3,64,1024]{2,1,0:T(8,128)(2,1)S(1)}, u32[]{:S(2)}, u32[]{:S(2)}) collective-permute-start(bf16[3,64,1024]{2,1,0:T(8,128)(2,1)S(1)} %pad_maximum_fusion.3), channel_id=1, source_target_pairs={{0,16},{1,17},{2,18},{3,19},{4,20},{5,21},{6,22},{7,23},{8,24},{9,... | collective-permute-start | bytes 1179656 | tf_op jit(solution)/shard_map/ppermute | solution.py:39
  19.6 9.4 %collective-permute-start.6 = (bf16[2,2,2,64,384]{4,3,2,1,0:T(8,128)(2,1)S(1)}, bf16[2,2,2,64,384]{4,3,2,1,0:T(8,128)(2,1)S(1)}, u32[]{:S(2)}, u32[]{:S(2)}) collective-permute-start(bf16[2,2,2,64,384]{4,3,2,1,0:T(8,128)(2,1)S(1)} %get-tuple-element.52), channel_id=1, source_target_pairs={{0,4},{1,5},{2,6},{3,7},{4,0},{5,1},{6,2},{7,3},{8,12},{9,13},{10,... | collective-permute-start | bytes 1179656 | tf_op jit(solution)/shard_map/ppermute | solution.py:39
  25.0 8.5 %collective-permute-start.9 = (bf16[2,2,2,64,384]{4,3,2,1,0:T(8,128)(2,1)S(1)}, bf16[2,2,2,64,384]{4,3,2,1,0:T(8,128)(2,1)S(1)}, u32[]{:S(2)}, u32[]{:S(2)}) collective-permute-start(bf16[2,2,2,64,384]{4,3,2,1,0:T(8,128)(2,1)S(1)} %get-tuple-element.52), channel_id=1, source_target_pairs={{0,80},{1,81},{2,82},{3,83},{4,84},{5,85},{6,86},{7,87},{8,88},{9,... | collective-permute-start | bytes 1179656 | tf_op jit(solution)/shard_map/ppermute | solution.py:39
  26.5 9.7 %collective-permute-start.13 = (bf16[2,2,2,64,384]{4,3,2,1,0:T(8,128)(2,1)S(1)}, bf16[2,2,2,64,384]{4,3,2,1,0:T(8,128)(2,1)S(1)}, u32[]{:S(2)}, u32[]{:S(2)}) collective-permute-start(bf16[2,2,2,64,384]{4,3,2,1,0:T(8,128)(2,1)S(1)} %get-tuple-element.51), channel_id=1, source_target_pairs={{0,1},{1,0},{2,3},{3,2},{4,5},{5,4},{6,7},{7,6},{8,9},{9,8},{10,11... | collective-permute-start | bytes 1179656 | tf_op jit(solution)/shard_map/ppermute | solution.py:39
  29.4 8.3 %collective-permute-start.10 = (bf16[2,2,2,64,384]{4,3,2,1,0:T(8,128)(2,1)S(1)}, bf16[2,2,2,64,384]{4,3,2,1,0:T(8,128)(2,1)S(1)}, u32[]{:S(2)}, u32[]{:S(2)}) collective-permute-start(bf16[2,2,2,64,384]{4,3,2,1,0:T(8,128)(2,1)S(1)} %collective-permute-done.6), channel_id=1, source_target_pairs={{0,80},{1,81},{2,82},{3,83},{4,84},{5,85},{6,86},{7,87},{8,88},{9,... | collective-permute-start | bytes 1179656 | tf_op jit(solution)/shard_map/ppermute | solution.py:39
  30.7 14.3 %collective-permute-start.17 = (bf16[2,2,4,64,256]{4,3,2,1,0:T(8,128)(2,1)S(1)}, bf16[2,2,4,64,256]{4,3,2,1,0:T(8,128)(2,1)S(1)}, u32[]{:S(2)}, u32[]{:S(2)}) collective-permute-start(bf16[2,2,4,64,256]{4,3,2,1,0:T(8,128)(2,1)S(1)} %pad_maximum_fusion.2.refs_4_.refs_8_), channel_id=1, source_target_pairs={{0,4},{1,5},{2,6},{3,7},{4,0},{5,1},{6,2},{7,3},{8,12},{9,13},{10,... | collective-permute-start | bytes 1572872 | tf_op jit(solution)/shard_map/ppermute | solution.py:39
  30.9 14.3 %collective-permute-start.18 = (bf16[2,2,4,64,256]{4,3,2,1,0:T(8,128)(2,1)S(1)}, bf16[2,2,4,64,256]{4,3,2,1,0:T(8,128)(2,1)S(1)}, u32[]{:S(2)}, u32[]{:S(2)}) collective-permute-start(bf16[2,2,4,64,256]{4,3,2,1,0:T(8,128)(2,1)S(1)} %pad_maximum_fusion.2.refs_4_.refs_8_), channel_id=1, source_target_pairs={{0,80},{1,81},{2,82},{3,83},{4,84},{5,85},{6,86},{7,87},{8,88},{9,... | collective-permute-start | bytes 1572872 | tf_op jit(solution)/shard_map/ppermute | solution.py:39
  33.6 8.1 %collective-permute-start.14 = (bf16[2,2,2,64,384]{4,3,2,1,0:T(8,128)(2,1)S(1)}, bf16[2,2,2,64,384]{4,3,2,1,0:T(8,128)(2,1)S(1)}, u32[]{:S(2)}, u32[]{:S(2)}) collective-permute-start(bf16[2,2,2,64,384]{4,3,2,1,0:T(8,128)(2,1)S(1)} %collective-permute-done.7), channel_id=1, source_target_pairs={{0,1},{1,0},{2,3},{3,2},{4,5},{5,4},{6,7},{7,6},{8,9},{9,8},{10,11... | collective-permute-start | bytes 1179656 | tf_op jit(solution)/shard_map/ppermute | solution.py:39
  36.2 19.1 %collective-permute-start.11 = (bf16[2,4,2,64,384]{4,3,2,1,0:T(8,128)(2,1)S(1)}, bf16[2,4,2,64,384]{4,3,2,1,0:T(8,128)(2,1)}, u32[]{:S(2)}, u32[]{:S(2)}) collective-permute-start(bf16[2,4,2,64,384]{4,3,2,1,0:T(8,128)(2,1)S(1)} %pad_maximum_fusion.refs_0_), channel_id=1, source_target_pairs={{0,1},{1,0},{2,3},{3,2},{4,5},{5,4},{6,7},{7,6},{8,9},{9,8},{10,11... | collective-permute-start | bytes 2359304 | tf_op jit(solution)/shard_map/ppermute | solution.py:39
  37.8 17.6 %collective-permute-start.15 = (bf16[4,2,2,64,384]{4,3,2,1,0:T(8,128)(2,1)S(1)}, bf16[4,2,2,64,384]{4,3,2,1,0:T(8,128)(2,1)}, u32[]{:S(2)}, u32[]{:S(2)}) collective-permute-start(bf16[4,2,2,64,384]{4,3,2,1,0:T(8,128)(2,1)S(1)} %pad_maximum_fusion.1.refs_2_.refs_4_), channel_id=1, source_target_pairs={{0,4},{1,5},{2,6},{3,7},{4,0},{5,1},{6,2},{7,3},{8,12},{9,13},{10,... | collective-permute-start | bytes 2359304 | tf_op jit(solution)/shard_map/ppermute | solution.py:39
  41.7 17.0 %collective-permute-start.12 = (bf16[2,4,2,64,384]{4,3,2,1,0:T(8,128)(2,1)S(1)}, bf16[2,4,2,64,384]{4,3,2,1,0:T(8,128)(2,1)}, u32[]{:S(2)}, u32[]{:S(2)}) collective-permute-start(bf16[2,4,2,64,384]{4,3,2,1,0:T(8,128)(2,1)S(1)} %constant_dynamic-update-slice_fusion.4.refs_1_), channel_id=1, source_target_pairs={{0,1},{1,0},{2,3},{3,2},{4,5},{5,4},{6,7},{7,6},{8,9},{9,8},{10,11... | collective-permute-start | bytes 2359304 | tf_op jit(solution)/shard_map/ppermute | solution.py:39
  45.0 13.7 %collective-permute-start.16 = (bf16[4,2,2,64,384]{4,3,2,1,0:T(8,128)(2,1)}, bf16[4,2,2,64,384]{4,3,2,1,0:T(8,128)(2,1)}, u32[]{:S(2)}, u32[]{:S(2)}) collective-permute-start(bf16[4,2,2,64,384]{4,3,2,1,0:T(8,128)(2,1)} %constant_dynamic-update-slice_fusion.6.refs_3_.refs_5_), channel_id=1, source_target_pairs={{0,4},{1,5},{2,6},{3,7},{4,0},{5,1},{6,2},{7,3},{8,12},{9,13},{10,... | collective-permute-start | bytes 2359304 | tf_op jit(solution)/shard_map/ppermute | solution.py:39
  46.0 9.3 %collective-permute-start.19 = (bf16[2,2,4,64,256]{4,3,2,1,0:T(8,128)(2,1)S(1)}, bf16[2,2,4,64,256]{4,3,2,1,0:T(8,128)(2,1)}, u32[]{:S(2)}, u32[]{:S(2)}) collective-permute-start(bf16[2,2,4,64,256]{4,3,2,1,0:T(8,128)(2,1)S(1)} %collective-permute-done.17.refs_5_.refs_9_), channel_id=1, source_target_pairs={{0,80},{1,81},{2,82},{3,83},{4,84},{5,85},{6,86},{7,87},{8,88},{9,... | collective-permute-start | bytes 1572872 | tf_op jit(solution)/shard_map/ppermute | solution.py:39
  63.8 9.5 %collective-permute-start.21 = (f32[2,256,512]{2,1,0:T(8,128)S(1)}, f32[2,256,512]{2,1,0:T(8,128)S(1)}, u32[]{:S(2)}, u32[]{:S(2)}) collective-permute-start(f32[2,256,512]{2,1,0:T(8,128)S(1)} %get-tuple-element.39), channel_id=1, source_target_pairs={{0,32},{1,33},{2,34},{3,35},{4,36},{5,37},{6,38},{7,39},{8,40},{9,... | collective-permute-start | bytes 3145736 | tf_op jit(solution)/shard_map/ppermute | solution.py:43
  71.1 14.3 %collective-permute-start.20 = (bf16[2,2,4,2,64,384]{5,4,3,2,1,0:T(8,128)(2,1)S(1)}, bf16[2,2,4,2,64,384]{5,4,3,2,1,0:T(8,128)(2,1)S(1)}, u32[]{:S(2)}, u32[]{:S(2)}) collective-permute-start(bf16[2,2,4,2,64,384]{5,4,3,2,1,0:T(8,128)(2,1)S(1)} %get-tuple-element.36), channel_id=1, source_target_pairs={{0,32},{1,33},{2,34},{3,35},{4,36},{5,37},{6,38},{7,39},{8,40},{9,... | collective-permute-start | bytes 4718600 | tf_op jit(solution)/shard_map/ppermute | solution.py:43
  71.5 14.0 %collective-permute-start.23 = (bf16[2,4,2,2,64,384]{5,4,3,2,1,0:T(8,128)(2,1)S(1)}, bf16[2,4,2,2,64,384]{5,4,3,2,1,0:T(8,128)(2,1)S(1)}, u32[]{:S(2)}, u32[]{:S(2)}) collective-permute-start(bf16[2,4,2,2,64,384]{5,4,3,2,1,0:T(8,128)(2,1)S(1)} %get-tuple-element.45), channel_id=1, source_target_pairs={{0,32},{1,33},{2,34},{3,35},{4,36},{5,37},{6,38},{7,39},{8,40},{9,... | collective-permute-start | bytes 4718600 | tf_op jit(solution)/shard_map/ppermute | solution.py:43
  74.0 23.0 %collective-permute-start.22 = (bf16[2,2,4,2,64,384]{5,4,3,2,1,0:T(8,128)(2,1)S(1)}, bf16[2,2,4,2,64,384]{5,4,3,2,1,0:T(8,128)(2,1)S(1)}, u32[]{:S(2)}, u32[]{:S(2)}) collective-permute-start(bf16[2,2,4,2,64,384]{5,4,3,2,1,0:T(8,128)(2,1)S(1)} %get-tuple-element.44), channel_id=1, source_target_pairs={{0,32},{1,33},{2,34},{3,35},{4,36},{5,37},{6,38},{7,39},{8,40},{9,... | collective-permute-start | bytes 4718600 | tf_op jit(solution)/shard_map/ppermute | solution.py:43
  74.4 22.5 %collective-permute-start.24 = (bf16[2,4,2,2,64,384]{5,4,3,2,1,0:T(8,128)(2,1)S(1)}, bf16[2,4,2,2,64,384]{5,4,3,2,1,0:T(8,128)(2,1)S(1)}, u32[]{:S(2)}, u32[]{:S(2)}) collective-permute-start(bf16[2,4,2,2,64,384]{5,4,3,2,1,0:T(8,128)(2,1)S(1)} %get-tuple-element.46), channel_id=1, source_target_pairs={{0,32},{1,33},{2,34},{3,35},{4,36},{5,37},{6,38},{7,39},{8,40},{9,... | collective-permute-start | bytes 4718600 | tf_op jit(solution)/shard_map/ppermute | solution.py:43
  74.8 9.0 %collective-permute-start.27 = (bf16[256,512]{1,0:T(8,128)(2,1)S(1)}, bf16[256,512]{1,0:T(8,128)(2,1)S(1)}, u32[]{:S(2)}, u32[]{:S(2)}) collective-permute-start(bf16[256,512]{1,0:T(8,128)(2,1)S(1)} %get-tuple-element.50), channel_id=1, source_target_pairs={{0,64},{1,65},{2,66},{3,67},{4,68},{5,69},{6,70},{7,71},{8,72},{9,... | collective-permute-start | bytes 786440 | tf_op jit(solution)/shard_map/ppermute | solution.py:47
  83.8 13.1 %collective-permute-start.26 = (bf16[2,2,2,4,64,256]{5,4,3,2,1,0:T(8,128)(2,1)S(1)}, bf16[2,2,2,4,64,256]{5,4,3,2,1,0:T(8,128)(2,1)S(1)}, u32[]{:S(2)}, u32[]{:S(2)}) collective-permute-start(bf16[2,2,2,4,64,256]{5,4,3,2,1,0:T(8,128)(2,1)S(1)} %get-tuple-element.48), channel_id=1, source_target_pairs={{0,32},{1,33},{2,34},{3,35},{4,36},{5,37},{6,38},{7,39},{8,40},{9,... | collective-permute-start | bytes 3145736 | tf_op jit(solution)/shard_map/ppermute | solution.py:43
  85.4 9.5 %collective-permute-start.29 = (bf16[256,512]{1,0:T(8,128)(2,1)S(1)}, bf16[256,512]{1,0:T(8,128)(2,1)S(1)}, u32[]{:S(2)}, u32[]{:S(2)}) collective-permute-start(bf16[256,512]{1,0:T(8,128)(2,1)S(1)} %direction.1.refs_18_), channel_id=1, source_target_pairs={{0,64},{1,65},{2,66},{3,67},{4,68},{5,69},{6,70},{7,71},{8,72},{9,... | collective-permute-start | bytes 786440 | tf_op jit(solution)/shard_map/ppermute | solution.py:47
  85.5 11.4 %collective-permute-start.28 = (bf16[256,512]{1,0:T(8,128)(2,1)S(1)}, bf16[256,512]{1,0:T(8,128)(2,1)S(1)}, u32[]{:S(2)}, u32[]{:S(2)}) collective-permute-start(bf16[256,512]{1,0:T(8,128)(2,1)S(1)} %direction.1.refs_18_), channel_id=1, source_target_pairs={{0,32},{1,33},{2,34},{3,35},{4,36},{5,37},{6,38},{7,39},{8,40},{9,... | collective-permute-start | bytes 786440 | tf_op jit(solution)/shard_map/ppermute | solution.py:43
  (12 other events, 69.3 us)

commit v6 on v5

--- a/solution.py
+++ b/solution.py
@@ -148,7 +148,7 @@
         where, before, partial, sent, *refs = refs
     else:
         partial, *refs = refs
-    packed, scratch, (sems, pack_sem, out_sem) = refs[:3], refs[3:9], refs[9:]
+    packed, scratch, (sems, pack_sem) = refs[:3], refs[3:9], refs[9:]
     loads = [pltpu.make_async_copy(p, v, sems.at[k]) for k, (p, v) in enumerate(zip(pieces, scratch))]
     for load in loads:
         load.start()
@@ -174,8 +174,7 @@
         share = sent.shape[1]
         for far in range(2):
             row = pl.multiple_of((far * 2 + 1 - where[0]) * share, share)
-            pltpu.make_async_copy(partial.at[pl.ds(row, share)], sent.at[far], out_sem).start()
-        pltpu.make_async_copy(sent, sent, out_sem).wait()
+            sent[far] = partial[pl.ds(row, share)].astype(sent.dtype)
     for out in packed:
         pltpu.make_async_copy(out, out, pack_sem).wait()
 
@@ -186,15 +185,15 @@
     anywhere, inside = pl.BlockSpec(memory_space=pl.ANY), pl.BlockSpec(memory_space=pltpu.VMEM)
     result = [jax.ShapeDtypeStruct((1024, columns), jnp.float32)]
     if late:
-        result.append(jax.ShapeDtypeStruct((2, 256, columns), jnp.float32))
+        result.append(jax.ShapeDtypeStruct((2, 256, columns), jnp.bfloat16))
     packed = [jax.ShapeDtypeStruct((2, *piece.shape), piece.dtype) for piece in pieces[::2]]
     return pl.pallas_call(
         functools.partial(project_kernel, late),
         out_shape=result + packed,
         in_specs=[inside] + [anywhere] * 6 + [pl.BlockSpec(memory_space=pltpu.SMEM), inside] * late,
-        out_specs=[inside] + [anywhere] * (len(result) + 2),
+        out_specs=[inside] * len(result) + [anywhere] * 3,
         scratch_shapes=[pltpu.VMEM(piece.shape, jnp.bfloat16) for piece in pieces]
-        + [pltpu.SemaphoreType.DMA((6,)), pltpu.SemaphoreType.DMA, pltpu.SemaphoreType.DMA],
+        + [pltpu.SemaphoreType.DMA((6,)), pltpu.SemaphoreType.DMA],
         compiler_params=pltpu.CompilerParams(vmem_limit_bytes=32 * MIB),
         cost_estimate=pl.CostEstimate(
             flops=summed.size * 1024, bytes_accessed=2 * summed.size + 4 * MIB, transcendentals=0
@@ -208,7 +207,7 @@
     share = kept.shape[0]
 
     def total(f):
-        return partial[pl.ds(pl.multiple_of((f * 2 + core) * share, share), share)] + received[f]
+        return partial[pl.ds(pl.multiple_of((f * 2 + core) * share, share), share)] + received[f].astype(jnp.float32)
 
     sent[...] = total(1 - far).astype(jnp.bfloat16)
     kept[...] = total(far)
@@ -365,8 +364,7 @@
     partial, sent, *more = project(summed, late, where, partial)
 
     kept, sent = add_cores(where, partial, swap_core(sent))
-    kept, *more = together(kept, *more)
-    received = swap_far(sent)
+    received, *more = together(swap_far(sent), *more)
     direction = direct(kept, received, first_moment, second_moment)
     new_first, new_second = adam(kept, received, first_moment, second_moment)
 

time: 112 us -> 111 us (level)
  transfers between devices with their start and end apart: 31 -> 31, of which waited for: 13 -> 12; matrix products, arithmetic and copies ran while one was open for 3% -> 3% of each run, Pallas kernels for 9% -> 9%
where the time goes in v6:
time: 111 us; the launch traced here: 110 us
  starting transfers between devices  38 us (34%)
  waiting for transfers between devices  37.1 us (33%)
  Pallas kernels  29.1 us (26%)
  local copies, waits for them, and re-layouts  3.7 us (3%)
  other arithmetic  1.54 us (1%)
    ppermute x19, starting transfers between devices, exchange(): return lax.ppermute(value, BOTH, pairs(partner))  25.8 us
    ppermute x2, waiting for transfers between devices, swap_far(): return lax.ppermute(value, BOTH, pairs(lambda c, z, y, x: (c, z ^ 2, y, x)))  18.1 us
    ppermute x19, waiting for transfers between devices, exchange(): return lax.ppermute(value, BOTH, pairs(partner))  18 us
    pallas_call x1, Pallas kernels, back_project(): pl.pallas_call(update_kernel, out_shape=jax.ShapeDtypeStruct((rows, colum...  14.4 us
    ppermute x10, starting transfers between devices, swap_core(): return lax.ppermute(value, BOTH, pairs(lambda c, z, y, x: (1 - c, z, y, x)))  12.1 us
    pallas_call x2, Pallas kernels, project(): pl.pallas_call(functools.partial(project_kernel, late), out_shape=result...  8.72 us
    pallas_call x1, Pallas kernels, sum_grads(): pl.pallas_call(sum_kernel, out_shape=jax.ShapeDtypeStruct((4, 4, 4, 64, c...  4.79 us
    unnamed x17, local copies, waits for them, and re-layouts  2.65 us
  transfers between devices with their start and end apart: 31, of which 12 were waited for; matrix products, arithmetic and copies ran while one was open for 3% of the time, Pallas kernels for 9%

profile of v6, /device:TPU:1, one launch (start us, length us, event | category | flops | bytes accessed | tf_op | source)
XLA Modules:
  0.0 110.5 jit_solution(9821802593942323254)
XLA Ops:
  0.6 1.5 %collective-permute-start.5 = (bf16[8192,512]{1,0:T(8,128)(2,1)}, bf16[8192,512]{1,0:T(8,128)(2,1)}, u32[]{:S(2)}, u32[]{:S(2)}) collective-permute-start(bf16[8192,512]{1,0:T(8,128)(2,1)} %bitcast.16), channel_id=1, source_target_pairs={{0,32},{1,33},{2,34},{3,35},{4,36},{5,37},{6,38},{7,39},{8,40},{9,... | collective-permute-start | bytes 25165832 | tf_op jit(solution)/shard_map/ppermute | solution.py:43
  2.1 1.3 %collective-permute-start = (bf16[64,1024]{1,0:T(8,128)(2,1)}, bf16[64,1024]{1,0:T(8,128)(2,1)S(1)}, u32[]{:S(2)}, u32[]{:S(2)}) collective-permute-start(bf16[64,1024]{1,0:T(8,128)(2,1)} %source.1), channel_id=1, source_target_pairs={{0,3},{1,2},{2,1},{3,0},{4,7},{5,6},{6,5},{7,4},{8,11},{9,10},{10,... | collective-permute-start | bytes 393224 | tf_op jit(solution)/shard_map/ppermute | solution.py:39
  3.4 1.3 %collective-permute-start.1 = (bf16[64,1024]{1,0:T(8,128)(2,1)}, bf16[64,1024]{1,0:T(8,128)(2,1)S(1)}, u32[]{:S(2)}, u32[]{:S(2)}) collective-permute-start(bf16[64,1024]{1,0:T(8,128)(2,1)} %source.1), channel_id=1, source_target_pairs={{0,12},{1,13},{2,14},{3,15},{4,8},{5,9},{6,10},{7,11},{8,4},{9,5},... | collective-permute-start | bytes 393224 | tf_op jit(solution)/shard_map/ppermute | solution.py:39
  4.8 3.8 %collective-permute-start.3 = (bf16[64,1024]{1,0:T(8,128)(2,1)}, bf16[64,1024]{1,0:T(8,128)(2,1)S(1)}, u32[]{:S(2)}, u32[]{:S(2)}) collective-permute-start(bf16[64,1024]{1,0:T(8,128)(2,1)} %source.1), channel_id=1, source_target_pairs={{0,16},{1,17},{2,18},{3,19},{4,20},{5,21},{6,22},{7,23},{8,24},{9,... | collective-permute-start | bytes 393224 | tf_op jit(solution)/shard_map/ppermute | solution.py:39
  9.9 1.3 %collective-permute-done.3 = bf16[64,1024]{1,0:T(8,128)(2,1)S(1)} collective-permute-done((bf16[64,1024]{1,0:T(8,128)(2,1)}, bf16[64,1024]{1,0:T(8,128)(2,1)S(1)}, u32[]{:S(2)}, u32[]{:S(2)}) %collective-permute-start.3) | collective-permute-done | bytes 131104 | tf_op jit(solution)/shard_map/ppermute | solution.py:39
  11.3 3.0 %collective-permute-start.4 = (bf16[3,64,1024]{2,1,0:T(8,128)(2,1)S(1)}, bf16[3,64,1024]{2,1,0:T(8,128)(2,1)S(1)}, u32[]{:S(2)}, u32[]{:S(2)}) collective-permute-start(bf16[3,64,1024]{2,1,0:T(8,128)(2,1)S(1)} %pad_maximum_fusion.3), channel_id=1, source_target_pairs={{0,16},{1,17},{2,18},{3,19},{4,20},{5,21},{6,22},{7,23},{8,24},{9,... | collective-permute-start | bytes 1179656 | tf_op jit(solution)/shard_map/ppermute | solution.py:39
  14.4 5.1 %collective-permute-done.4 = bf16[3,64,1024]{2,1,0:T(8,128)(2,1)S(1)} collective-permute-done((bf16[3,64,1024]{2,1,0:T(8,128)(2,1)S(1)}, bf16[3,64,1024]{2,1,0:T(8,128)(2,1)S(1)}, u32[]{:S(2)}, u32[]{:S(2)}) %collective-permute-start.4) | collective-permute-done | bytes 393248 | tf_op jit(solution)/shard_map/ppermute | solution.py:39
  19.6 2.8 %collective-permute-start.6 = (bf16[2,2,2,64,384]{4,3,2,1,0:T(8,128)(2,1)S(1)}, bf16[2,2,2,64,384]{4,3,2,1,0:T(8,128)(2,1)S(1)}, u32[]{:S(2)}, u32[]{:S(2)}) collective-permute-start(bf16[2,2,2,64,384]{4,3,2,1,0:T(8,128)(2,1)S(1)} %get-tuple-element.52), channel_id=1, source_target_pairs={{0,4},{1,5},{2,6},{3,7},{4,0},{5,1},{6,2},{7,3},{8,12},{9,13},{10,... | collective-permute-start | bytes 1179656 | tf_op jit(solution)/shard_map/ppermute | solution.py:39
  22.5 2.6 %collective-permute-start.8 = (bf16[2,2,2,64,256]{4,3,2,1,0:T(8,128)(2,1)S(1)}, bf16[2,2,2,64,256]{4,3,2,1,0:T(8,128)(2,1)S(1)}, u32[]{:S(2)}, u32[]{:S(2)}) collective-permute-start(bf16[2,2,2,64,256]{4,3,2,1,0:T(8,128)(2,1)S(1)} %slice.12), channel_id=1, source_target_pairs={{0,1},{1,0},{2,3},{3,2},{4,5},{5,4},{6,7},{7,6},{8,9},{9,8},{10,11... | collective-permute-start | bytes 786440 | tf_op jit(solution)/shard_map/ppermute | solution.py:39
  25.0 1.5 %collective-permute-start.9 = (bf16[2,2,2,64,384]{4,3,2,1,0:T(8,128)(2,1)S(1)}, bf16[2,2,2,64,384]{4,3,2,1,0:T(8,128)(2,1)S(1)}, u32[]{:S(2)}, u32[]{:S(2)}) collective-permute-start(bf16[2,2,2,64,384]{4,3,2,1,0:T(8,128)(2,1)S(1)} %get-tuple-element.52), channel_id=1, source_target_pairs={{0,80},{1,81},{2,82},{3,83},{4,84},{5,85},{6,86},{7,87},{8,88},{9,... | collective-permute-start | bytes 1179656 | tf_op jit(solution)/shard_map/ppermute | solution.py:39
  26.7 2.3 %collective-permute-done.8 = bf16[2,2,2,64,256]{4,3,2,1,0:T(8,128)(2,1)S(1)} collective-permute-done((bf16[2,2,2,64,256]{4,3,2,1,0:T(8,128)(2,1)S(1)}, bf16[2,2,2,64,256]{4,3,2,1,0:T(8,128)(2,1)S(1)}, u32[]{:S(2)}, u32[]{:S(2)}) %collective-permute-start.8) | collective-permute-done | bytes 262176 | tf_op jit(solution)/shard_map/ppermute | solution.py:39
  30.9 1.4 %collective-permute-start.18 = (bf16[2,2,4,64,256]{4,3,2,1,0:T(8,128)(2,1)S(1)}, bf16[2,2,4,64,256]{4,3,2,1,0:T(8,128)(2,1)S(1)}, u32[]{:S(2)}, u32[]{:S(2)}) collective-permute-start(bf16[2,2,4,64,256]{4,3,2,1,0:T(8,128)(2,1)S(1)} %pad_maximum_fusion.2.refs_4_.refs_8_), channel_id=1, source_target_pairs={{0,80},{1,81},{2,82},{3,83},{4,84},{5,85},{6,86},{7,87},{8,88},{9,... | collective-permute-start | bytes 1572872 | tf_op jit(solution)/shard_map/ppermute | solution.py:39
  32.3 1.2 %collective-permute-done.9 = bf16[2,2,2,64,384]{4,3,2,1,0:T(8,128)(2,1)S(1)} collective-permute-done((bf16[2,2,2,64,384]{4,3,2,1,0:T(8,128)(2,1)S(1)}, bf16[2,2,2,64,384]{4,3,2,1,0:T(8,128)(2,1)S(1)}, u32[]{:S(2)}, u32[]{:S(2)}) %collective-permute-start.9) | collective-permute-done | bytes 393248 | tf_op jit(solution)/shard_map/ppermute | solution.py:39
  33.6 2.5 %collective-permute-start.14 = (bf16[2,2,2,64,384]{4,3,2,1,0:T(8,128)(2,1)S(1)}, bf16[2,2,2,64,384]{4,3,2,1,0:T(8,128)(2,1)S(1)}, u32[]{:S(2)}, u32[]{:S(2)}) collective-permute-start(bf16[2,2,2,64,384]{4,3,2,1,0:T(8,128)(2,1)S(1)} %collective-permute-done.7), channel_id=1, source_target_pairs={{0,1},{1,0},{2,3},{3,2},{4,5},{5,4},{6,7},{7,6},{8,9},{9,8},{10,11... | collective-permute-start | bytes 1179656 | tf_op jit(solution)/shard_map/ppermute | solution.py:39
  37.9 3.8 %collective-permute-done.14 = bf16[2,2,2,64,384]{4,3,2,1,0:T(8,128)(2,1)S(1)} collective-permute-done((bf16[2,2,2,64,384]{4,3,2,1,0:T(8,128)(2,1)S(1)}, bf16[2,2,2,64,384]{4,3,2,1,0:T(8,128)(2,1)S(1)}, u32[]{:S(2)}, u32[]{:S(2)}) %collective-permute-start.14) | collective-permute-done | bytes 393248 | tf_op jit(solution)/shard_map/ppermute | solution.py:39
  41.7 2.5 %collective-permute-start.12 = (bf16[2,4,2,64,384]{4,3,2,1,0:T(8,128)(2,1)S(1)}, bf16[2,4,2,64,384]{4,3,2,1,0:T(8,128)(2,1)}, u32[]{:S(2)}, u32[]{:S(2)}) collective-permute-start(bf16[2,4,2,64,384]{4,3,2,1,0:T(8,128)(2,1)S(1)} %constant_dynamic-update-slice_fusion.4.refs_1_), channel_id=1, source_target_pairs={{0,1},{1,0},{2,3},{3,2},{4,5},{5,4},{6,7},{7,6},{8,9},{9,8},{10,11... | collective-permute-start | bytes 2359304 | tf_op jit(solution)/shard_map/ppermute | solution.py:39
  46.9 4.8 %sum_grads.1.summed = bf16[4,4,4,64,512]{4,3,2,1,0:T(8,128)(2,1)S(1)} custom-call(s32[4]{0:T(128)S(1)} %pad_add_fusion.where.refs_6_, bf16[8192,512]{1,0:T(8,128)(2,1)} %bitcast.17, bf16[8192,512]{1,0:T(8,128)(2,1)} %collective-permute-done.5.theirs), custom_call_target="tpu_custom_call" | custom-call | flops 2097152 | bytes 12582912 | tf_op jit(solution)/shard_map/sum_grads/pallas_call | solution.py:129
  51.7 3.6 %project.1 = (f32[1024,512]{1,0:T(8,128)S(1)}, bf16[2,2,4,2,64,384]{5,4,3,2,1,0:T(8,128)(2,1)S(1)}, bf16[2,4,2,2,64,384]{5,4,3,2,1,0:T(8,128)(2,1)S(1)}, bf16[2,2,2,4,64,256]{5,4,3,2,1,0:T(8,128)(2,1)S(1)}) custom-call(bf16[4,4,4,64,512]{4,3,2,1,0:T(8,128)(2,1)S(1)} %sum_grads.1.summed, bf16[2,4,2,64,384]{4,3,2,1,0:T(8,128)(2,1)S(1)} %pad_maximum_fusion.refs_0_, ...), custom_call_target="tpu_custom_call" | custom-call | flops 2147483648 | bytes 8388608 | tf_op jit(solution)/shard_map/project/pallas_call | solution.py:190
  55.4 3.3 %collective-permute-done.12.refs_1_.refs_3_ = bf16[2,4,2,64,384]{4,3,2,1,0:T(8,128)(2,1)} collective-permute-done((bf16[2,4,2,64,384]{4,3,2,1,0:T(8,128)(2,1)S(1)}, bf16[2,4,2,64,384]{4,3,2,1,0:T(8,128)(2,1)}, u32[]{:S(2)}, u32[]{:S(2)}) %collective-permute-start.12) | collective-permute-done | bytes 786464 | tf_op jit(solution)/shard_map/ppermute | solution.py:39
  58.7 5.1 %project_late.1 = (f32[1024,512]{1,0:T(8,128)S(1)}, bf16[2,256,512]{2,1,0:T(8,128)(2,1)S(1)}, bf16[2,2,4,2,64,384]{5,4,3,2,1,0:T(8,128)(2,1)S(1)}, bf16[2,4,2,2,...) custom-call(bf16[4,4,4,64,512]{4,3,2,1,0:T(8,128)(2,1)S(1)} %sum_grads.1.summed, ...), custom_call_target="tpu_custom_call" | custom-call | flops 2147483648 | bytes 8388608 | tf_op jit(solution)/shard_map/project_late/pallas_call | solution.py:190
  63.8 7.2 %collective-permute-start.21 = (bf16[2,256,512]{2,1,0:T(8,128)(2,1)S(1)}, bf16[2,256,512]{2,1,0:T(8,128)(2,1)S(1)}, u32[]{:S(2)}, u32[]{:S(2)}) collective-permute-start(bf16[2,256,512]{2,1,0:T(8,128)(2,1)S(1)} %get-tuple-element.39), channel_id=1, source_target_pairs={{0,32},{1,33},{2,34},{3,35},{4,36},{5,37},{6,38},{7,39},{8,40},{9,... | collective-permute-start | bytes 1572872 | tf_op jit(solution)/shard_map/ppermute | solution.py:43
  73.3 9.0 %collective-permute-done.22.received = bf16[256,512]{1,0:T(8,128)(2,1)S(1)} collective-permute-done((bf16[256,512]{1,0:T(8,128)(2,1)S(1)}, bf16[256,512]{1,0:T(8,128)(2,1)S(1)}, u32[]{:S(2)}, u32[]{:S(2)}) %collective-permute-start.22) | collective-permute-done | bytes 262176 | tf_op jit(solution)/shard_map/ppermute | solution.py:47
  84.8 9.1 %collective-permute-done.29.refs_20_ = bf16[256,512]{1,0:T(8,128)(2,1)S(1)} collective-permute-done((bf16[256,512]{1,0:T(8,128)(2,1)S(1)}, bf16[256,512]{1,0:T(8,128)(2,1)S(1)}, u32[]{:S(2)}, u32[]{:S(2)}) %collective-permute-start.29) | collective-permute-done | bytes 262176 | tf_op jit(solution)/shard_map/ppermute | solution.py:47
  95.9 14.4 %back_project.1 = bf16[8192,512]{1,0:T(8,128)(2,1)} custom-call(s32[4]{0:T(128)S(1)} %pad_add_fusion.where.refs_6_, bf16[2,4,2,64,384]{4,3,2,1,0:T(8,128)(2,1)S(1)} %pad_maximum_fusion.refs_0_, bf16[2,4,2,64,384]{4,3,2,1,0:T(8,128)(2,1)S(1)} %constant_dynamic-update-slice_fusion.4.refs_1_, ...), custom_call_target="tpu_custom_call" | custom-call | flops 8589934592 | bytes 25165824 | tf_op jit(solution)/shard_map/back_project/pallas_call | solution.py:320
  (73 shorter events, 15.1 us)
Async XLA Ops:
  0.6 18.9 %collective-permute-start.5 = (bf16[8192,512]{1,0:T(8,128)(2,1)}, bf16[8192,512]{1,0:T(8,128)(2,1)}, u32[]{:S(2)}, u32[]{:S(2)}) collective-permute-start(bf16[8192,512]{1,0:T(8,128)(2,1)} %bitcast.16), channel_id=1, source_target_pairs={{0,32},{1,33},{2,34},{3,35},{4,36},{5,37},{6,38},{7,39},{8,40},{9,... | collective-permute-start | bytes 25165832 | tf_op jit(solution)/shard_map/ppermute | solution.py:43
  11.3 8.2 %collective-permute-start.4 = (bf16[3,64,1024]{2,1,0:T(8,128)(2,1)S(1)}, bf16[3,64,1024]{2,1,0:T(8,128)(2,1)S(1)}, u32[]{:S(2)}, u32[]{:S(2)}) collective-permute-start(bf16[3,64,1024]{2,1,0:T(8,128)(2,1)S(1)} %pad_maximum_fusion.3), channel_id=1, source_target_pairs={{0,16},{1,17},{2,18},{3,19},{4,20},{5,21},{6,22},{7,23},{8,24},{9,... | collective-permute-start | bytes 1179656 | tf_op jit(solution)/shard_map/ppermute | solution.py:39
  19.6 9.4 %collective-permute-start.6 = (bf16[2,2,2,64,384]{4,3,2,1,0:T(8,128)(2,1)S(1)}, bf16[2,2,2,64,384]{4,3,2,1,0:T(8,128)(2,1)S(1)}, u32[]{:S(2)}, u32[]{:S(2)}) collective-permute-start(bf16[2,2,2,64,384]{4,3,2,1,0:T(8,128)(2,1)S(1)} %get-tuple-element.52), channel_id=1, source_target_pairs={{0,4},{1,5},{2,6},{3,7},{4,0},{5,1},{6,2},{7,3},{8,12},{9,13},{10,... | collective-permute-start | bytes 1179656 | tf_op jit(solution)/shard_map/ppermute | solution.py:39
  25.0 8.5 %collective-permute-start.9 = (bf16[2,2,2,64,384]{4,3,2,1,0:T(8,128)(2,1)S(1)}, bf16[2,2,2,64,384]{4,3,2,1,0:T(8,128)(2,1)S(1)}, u32[]{:S(2)}, u32[]{:S(2)}) collective-permute-start(bf16[2,2,2,64,384]{4,3,2,1,0:T(8,128)(2,1)S(1)} %get-tuple-element.52), channel_id=1, source_target_pairs={{0,80},{1,81},{2,82},{3,83},{4,84},{5,85},{6,86},{7,87},{8,88},{9,... | collective-permute-start | bytes 1179656 | tf_op jit(solution)/shard_map/ppermute | solution.py:39
  26.5 9.7 %collective-permute-start.13 = (bf16[2,2,2,64,384]{4,3,2,1,0:T(8,128)(2,1)S(1)}, bf16[2,2,2,64,384]{4,3,2,1,0:T(8,128)(2,1)S(1)}, u32[]{:S(2)}, u32[]{:S(2)}) collective-permute-start(bf16[2,2,2,64,384]{4,3,2,1,0:T(8,128)(2,1)S(1)} %get-tuple-element.51), channel_id=1, source_target_pairs={{0,1},{1,0},{2,3},{3,2},{4,5},{5,4},{6,7},{7,6},{8,9},{9,8},{10,11... | collective-permute-start | bytes 1179656 | tf_op jit(solution)/shard_map/ppermute | solution.py:39
  29.4 8.3 %collective-permute-start.10 = (bf16[2,2,2,64,384]{4,3,2,1,0:T(8,128)(2,1)S(1)}, bf16[2,2,2,64,384]{4,3,2,1,0:T(8,128)(2,1)S(1)}, u32[]{:S(2)}, u32[]{:S(2)}) collective-permute-start(bf16[2,2,2,64,384]{4,3,2,1,0:T(8,128)(2,1)S(1)} %collective-permute-done.6), channel_id=1, source_target_pairs={{0,80},{1,81},{2,82},{3,83},{4,84},{5,85},{6,86},{7,87},{8,88},{9,... | collective-permute-start | bytes 1179656 | tf_op jit(solution)/shard_map/ppermute | solution.py:39
  30.7 14.3 %collective-permute-start.17 = (bf16[2,2,4,64,256]{4,3,2,1,0:T(8,128)(2,1)S(1)}, bf16[2,2,4,64,256]{4,3,2,1,0:T(8,128)(2,1)S(1)}, u32[]{:S(2)}, u32[]{:S(2)}) collective-permute-start(bf16[2,2,4,64,256]{4,3,2,1,0:T(8,128)(2,1)S(1)} %pad_maximum_fusion.2.refs_4_.refs_8_), channel_id=1, source_target_pairs={{0,4},{1,5},{2,6},{3,7},{4,0},{5,1},{6,2},{7,3},{8,12},{9,13},{10,... | collective-permute-start | bytes 1572872 | tf_op jit(solution)/shard_map/ppermute | solution.py:39
  30.9 14.3 %collective-permute-start.18 = (bf16[2,2,4,64,256]{4,3,2,1,0:T(8,128)(2,1)S(1)}, bf16[2,2,4,64,256]{4,3,2,1,0:T(8,128)(2,1)S(1)}, u32[]{:S(2)}, u32[]{:S(2)}) collective-permute-start(bf16[2,2,4,64,256]{4,3,2,1,0:T(8,128)(2,1)S(1)} %pad_maximum_fusion.2.refs_4_.refs_8_), channel_id=1, source_target_pairs={{0,80},{1,81},{2,82},{3,83},{4,84},{5,85},{6,86},{7,87},{8,88},{9,... | collective-permute-start | bytes 1572872 | tf_op jit(solution)/shard_map/ppermute | solution.py:39
  33.6 8.1 %collective-permute-start.14 = (bf16[2,2,2,64,384]{4,3,2,1,0:T(8,128)(2,1)S(1)}, bf16[2,2,2,64,384]{4,3,2,1,0:T(8,128)(2,1)S(1)}, u32[]{:S(2)}, u32[]{:S(2)}) collective-permute-start(bf16[2,2,2,64,384]{4,3,2,1,0:T(8,128)(2,1)S(1)} %collective-permute-done.7), channel_id=1, source_target_pairs={{0,1},{1,0},{2,3},{3,2},{4,5},{5,4},{6,7},{7,6},{8,9},{9,8},{10,11... | collective-permute-start | bytes 1179656 | tf_op jit(solution)/shard_map/ppermute | solution.py:39
  36.2 19.1 %collective-permute-start.11 = (bf16[2,4,2,64,384]{4,3,2,1,0:T(8,128)(2,1)S(1)}, bf16[2,4,2,64,384]{4,3,2,1,0:T(8,128)(2,1)}, u32[]{:S(2)}, u32[]{:S(2)}) collective-permute-start(bf16[2,4,2,64,384]{4,3,2,1,0:T(8,128)(2,1)S(1)} %pad_maximum_fusion.refs_0_), channel_id=1, source_target_pairs={{0,1},{1,0},{2,3},{3,2},{4,5},{5,4},{6,7},{7,6},{8,9},{9,8},{10,11... | collective-permute-start | bytes 2359304 | tf_op jit(solution)/shard_map/ppermute | solution.py:39
  37.8 17.6 %collective-permute-start.15 = (bf16[4,2,2,64,384]{4,3,2,1,0:T(8,128)(2,1)S(1)}, bf16[4,2,2,64,384]{4,3,2,1,0:T(8,128)(2,1)}, u32[]{:S(2)}, u32[]{:S(2)}) collective-permute-start(bf16[4,2,2,64,384]{4,3,2,1,0:T(8,128)(2,1)S(1)} %pad_maximum_fusion.1.refs_2_.refs_4_), channel_id=1, source_target_pairs={{0,4},{1,5},{2,6},{3,7},{4,0},{5,1},{6,2},{7,3},{8,12},{9,13},{10,... | collective-permute-start | bytes 2359304 | tf_op jit(solution)/shard_map/ppermute | solution.py:39
  41.7 17.0 %collective-permute-start.12 = (bf16[2,4,2,64,384]{4,3,2,1,0:T(8,128)(2,1)S(1)}, bf16[2,4,2,64,384]{4,3,2,1,0:T(8,128)(2,1)}, u32[]{:S(2)}, u32[]{:S(2)}) collective-permute-start(bf16[2,4,2,64,384]{4,3,2,1,0:T(8,128)(2,1)S(1)} %constant_dynamic-update-slice_fusion.4.refs_1_), channel_id=1, source_target_pairs={{0,1},{1,0},{2,3},{3,2},{4,5},{5,4},{6,7},{7,6},{8,9},{9,8},{10,11... | collective-permute-start | bytes 2359304 | tf_op jit(solution)/shard_map/ppermute | solution.py:39
  45.0 13.7 %collective-permute-start.16 = (bf16[4,2,2,64,384]{4,3,2,1,0:T(8,128)(2,1)}, bf16[4,2,2,64,384]{4,3,2,1,0:T(8,128)(2,1)}, u32[]{:S(2)}, u32[]{:S(2)}) collective-permute-start(bf16[4,2,2,64,384]{4,3,2,1,0:T(8,128)(2,1)} %constant_dynamic-update-slice_fusion.6.refs_3_.refs_5_), channel_id=1, source_target_pairs={{0,4},{1,5},{2,6},{3,7},{4,0},{5,1},{6,2},{7,3},{8,12},{9,13},{10,... | collective-permute-start | bytes 2359304 | tf_op jit(solution)/shard_map/ppermute | solution.py:39
  46.0 9.3 %collective-permute-start.19 = (bf16[2,2,4,64,256]{4,3,2,1,0:T(8,128)(2,1)S(1)}, bf16[2,2,4,64,256]{4,3,2,1,0:T(8,128)(2,1)}, u32[]{:S(2)}, u32[]{:S(2)}) collective-permute-start(bf16[2,2,4,64,256]{4,3,2,1,0:T(8,128)(2,1)S(1)} %collective-permute-done.17.refs_5_.refs_9_), channel_id=1, source_target_pairs={{0,80},{1,81},{2,82},{3,83},{4,84},{5,85},{6,86},{7,87},{8,88},{9,... | collective-permute-start | bytes 1572872 | tf_op jit(solution)/shard_map/ppermute | solution.py:39
  63.8 8.7 %collective-permute-start.21 = (bf16[2,256,512]{2,1,0:T(8,128)(2,1)S(1)}, bf16[2,256,512]{2,1,0:T(8,128)(2,1)S(1)}, u32[]{:S(2)}, u32[]{:S(2)}) collective-permute-start(bf16[2,256,512]{2,1,0:T(8,128)(2,1)S(1)} %get-tuple-element.39), channel_id=1, source_target_pairs={{0,32},{1,33},{2,34},{3,35},{4,36},{5,37},{6,38},{7,39},{8,40},{9,... | collective-permute-start | bytes 1572872 | tf_op jit(solution)/shard_map/ppermute | solution.py:43
  71.0 13.4 %collective-permute-start.20 = (bf16[2,2,4,2,64,384]{5,4,3,2,1,0:T(8,128)(2,1)S(1)}, bf16[2,2,4,2,64,384]{5,4,3,2,1,0:T(8,128)(2,1)S(1)}, u32[]{:S(2)}, u32[]{:S(2)}) collective-permute-start(bf16[2,2,4,2,64,384]{5,4,3,2,1,0:T(8,128)(2,1)S(1)} %get-tuple-element.36), channel_id=1, source_target_pairs={{0,32},{1,33},{2,34},{3,35},{4,36},{5,37},{6,38},{7,39},{8,40},{9,... | collective-permute-start | bytes 4718600 | tf_op jit(solution)/shard_map/ppermute | solution.py:43
  71.1 12.4 %collective-permute-start.26 = (bf16[2,2,2,4,64,256]{5,4,3,2,1,0:T(8,128)(2,1)S(1)}, bf16[2,2,2,4,64,256]{5,4,3,2,1,0:T(8,128)(2,1)S(1)}, u32[]{:S(2)}, u32[]{:S(2)}) collective-permute-start(bf16[2,2,2,4,64,256]{5,4,3,2,1,0:T(8,128)(2,1)S(1)} %get-tuple-element.47), channel_id=1, source_target_pairs={{0,32},{1,33},{2,34},{3,35},{4,36},{5,37},{6,38},{7,39},{8,40},{9,... | collective-permute-start | bytes 3145736 | tf_op jit(solution)/shard_map/ppermute | solution.py:43
  71.5 13.0 %collective-permute-start.24 = (bf16[2,4,2,2,64,384]{5,4,3,2,1,0:T(8,128)(2,1)S(1)}, bf16[2,4,2,2,64,384]{5,4,3,2,1,0:T(8,128)(2,1)S(1)}, u32[]{:S(2)}, u32[]{:S(2)}) collective-permute-start(bf16[2,4,2,2,64,384]{5,4,3,2,1,0:T(8,128)(2,1)S(1)} %get-tuple-element.45), channel_id=1, source_target_pairs={{0,32},{1,33},{2,34},{3,35},{4,36},{5,37},{6,38},{7,39},{8,40},{9,... | collective-permute-start | bytes 4718600 | tf_op jit(solution)/shard_map/ppermute | solution.py:43
  73.2 9.1 %collective-permute-start.22 = (bf16[256,512]{1,0:T(8,128)(2,1)S(1)}, bf16[256,512]{1,0:T(8,128)(2,1)S(1)}, u32[]{:S(2)}, u32[]{:S(2)}) collective-permute-start(bf16[256,512]{1,0:T(8,128)(2,1)S(1)} %get-tuple-element.40), channel_id=1, source_target_pairs={{0,64},{1,65},{2,66},{3,67},{4,68},{5,69},{6,70},{7,71},{8,72},{9,... | collective-permute-start | bytes 786440 | tf_op jit(solution)/shard_map/ppermute | solution.py:47
  82.3 13.6 %collective-permute-start.23 = (bf16[2,2,4,2,64,384]{5,4,3,2,1,0:T(8,128)(2,1)S(1)}, bf16[2,2,4,2,64,384]{5,4,3,2,1,0:T(8,128)(2,1)S(1)}, u32[]{:S(2)}, u32[]{:S(2)}) collective-permute-start(bf16[2,2,4,2,64,384]{5,4,3,2,1,0:T(8,128)(2,1)S(1)} %get-tuple-element.44), channel_id=1, source_target_pairs={{0,32},{1,33},{2,34},{3,35},{4,36},{5,37},{6,38},{7,39},{8,40},{9,... | collective-permute-start | bytes 4718600 | tf_op jit(solution)/shard_map/ppermute | solution.py:43
  83.5 12.4 %collective-permute-start.25 = (bf16[2,4,2,2,64,384]{5,4,3,2,1,0:T(8,128)(2,1)S(1)}, bf16[2,4,2,2,64,384]{5,4,3,2,1,0:T(8,128)(2,1)S(1)}, u32[]{:S(2)}, u32[]{:S(2)}) collective-permute-start(bf16[2,4,2,2,64,384]{5,4,3,2,1,0:T(8,128)(2,1)S(1)} %get-tuple-element.46), channel_id=1, source_target_pairs={{0,32},{1,33},{2,34},{3,35},{4,36},{5,37},{6,38},{7,39},{8,40},{9,... | collective-permute-start | bytes 4718600 | tf_op jit(solution)/shard_map/ppermute | solution.py:43
  83.5 12.4 %collective-permute-start.27 = (bf16[2,2,2,4,64,256]{5,4,3,2,1,0:T(8,128)(2,1)S(1)}, bf16[2,2,2,4,64,256]{5,4,3,2,1,0:T(8,128)(2,1)S(1)}, u32[]{:S(2)}, u32[]{:S(2)}) collective-permute-start(bf16[2,2,2,4,64,256]{5,4,3,2,1,0:T(8,128)(2,1)S(1)} %get-tuple-element.48), channel_id=1, source_target_pairs={{0,32},{1,33},{2,34},{3,35},{4,36},{5,37},{6,38},{7,39},{8,40},{9,... | collective-permute-start | bytes 3145736 | tf_op jit(solution)/shard_map/ppermute | solution.py:43
  84.4 9.5 %collective-permute-start.29 = (bf16[256,512]{1,0:T(8,128)(2,1)S(1)}, bf16[256,512]{1,0:T(8,128)(2,1)S(1)}, u32[]{:S(2)}, u32[]{:S(2)}) collective-permute-start(bf16[256,512]{1,0:T(8,128)(2,1)S(1)} %direction.1.refs_18_), channel_id=1, source_target_pairs={{0,64},{1,65},{2,66},{3,67},{4,68},{5,69},{6,70},{7,71},{8,72},{9,... | collective-permute-start | bytes 786440 | tf_op jit(solution)/shard_map/ppermute | solution.py:47
  84.5 11.4 %collective-permute-start.28 = (bf16[256,512]{1,0:T(8,128)(2,1)S(1)}, bf16[256,512]{1,0:T(8,128)(2,1)S(1)}, u32[]{:S(2)}, u32[]{:S(2)}) collective-permute-start(bf16[256,512]{1,0:T(8,128)(2,1)S(1)} %direction.1.refs_18_), channel_id=1, source_target_pairs={{0,32},{1,33},{2,34},{3,35},{4,36},{5,37},{6,38},{7,39},{8,40},{9,... | collective-permute-start | bytes 786440 | tf_op jit(solution)/shard_map/ppermute | solution.py:43
  (12 other events, 90.1 us)

commit v7 on v6

--- a/solution.py
+++ b/solution.py
@@ -364,9 +364,10 @@
     partial, sent, *more = project(summed, late, where, partial)
 
     kept, sent = add_cores(where, partial, swap_core(sent))
-    received, *more = together(swap_far(sent), *more)
+    received = swap_far(sent)
     direction = direct(kept, received, first_moment, second_moment)
     new_first, new_second = adam(kept, received, first_moment, second_moment)
+    new_first, *more = together(new_first, *more)
 
     distant = swap_far(direction)
     near = swap_core(direction)

time: 111 us -> 116 us (1.045)
  starting transfers between devices: 38 us -> 45.2 us
  waiting for transfers between devices: 37.1 us -> 35 us
    ppermute x2, waiting for transfers between devices: 18.1 us -> 12.2 us  [swap_far(): return lax.ppermute(value, BOTH, pairs(lambda c, z, y, x: (c, z ^ 2, y, x)))]
    ppermute x2, starting transfers between devices: 0.17 us -> 4.95 us  [swap_far(): return lax.ppermute(value, BOTH, pairs(lambda c, z, y, x: (c, z ^ 2, y, x)))]
    ppermute x10, starting transfers between devices: 12.1 us -> 14.5 us  [swap_core(): return lax.ppermute(value, BOTH, pairs(lambda c, z, y, x: (1 - c, z, y, x)))]
    ppermute x19, waiting for transfers between devices: 18 us -> 20.1 us  [exchange(): return lax.ppermute(value, BOTH, pairs(partner))]
    ppermute x10, waiting for transfers between devices: 0.96 us -> 2.72 us  [swap_core(): return lax.ppermute(value, BOTH, pairs(lambda c, z, y, x: (1 - c, z, y, x)))]
  transfers between devices with their start and end apart: 31 -> 31, of which waited for: 12 -> 11; matrix products, arithmetic and copies ran while one was open for 3% -> 3% of each run, Pallas kernels for 9% -> 8%
where the time goes in v7:
time: 116 us
  starting transfers between devices  45.2 us (39%)
  waiting for transfers between devices  35 us (30%)
  Pallas kernels  29.4 us (25%)
  local copies, waits for them, and re-layouts  3.69 us (3%)
  other arithmetic  1.55 us (1%)
    ppermute x19, starting transfers between devices, exchange(): return lax.ppermute(value, BOTH, pairs(partner))  25.8 us
    ppermute x19, waiting for transfers between devices, exchange(): return lax.ppermute(value, BOTH, pairs(partner))  20.1 us
    ppermute x10, starting transfers between devices, swap_core(): return lax.ppermute(value, BOTH, pairs(lambda c, z, y, x: (1 - c, z, y, x)))  14.5 us
    pallas_call x1, Pallas kernels, back_project(): pl.pallas_call(update_kernel, out_shape=jax.ShapeDtypeStruct((rows, colum...  14.3 us
    ppermute x2, waiting for transfers between devices, swap_far(): return lax.ppermute(value, BOTH, pairs(lambda c, z, y, x: (c, z ^ 2, y, x)))  12.2 us
    pallas_call x2, Pallas kernels, project(): pl.pallas_call(functools.partial(project_kernel, late), out_shape=result...  9.17 us
    ppermute x2, starting transfers between devices, swap_far(): return lax.ppermute(value, BOTH, pairs(lambda c, z, y, x: (c, z ^ 2, y, x)))  4.95 us
    pallas_call x1, Pallas kernels, sum_grads(): pl.pallas_call(sum_kernel, out_shape=jax.ShapeDtypeStruct((4, 4, 4, 64, c...  4.79 us
  transfers between devices with their start and end apart: 31, of which 11 were waited for; matrix products, arithmetic and copies ran while one was open for 3% of the time, Pallas kernels for 8%

profile of v7, /device:TPU:1, one launch (start us, length us, event | category | flops | bytes accessed | tf_op | source)
XLA Modules:
  0.0 115.9 jit_solution(4429312734252640806)
XLA Ops:
  0.6 1.5 %collective-permute-start.5 = (bf16[8192,512]{1,0:T(8,128)(2,1)}, bf16[8192,512]{1,0:T(8,128)(2,1)}, u32[]{:S(2)}, u32[]{:S(2)}) collective-permute-start(bf16[8192,512]{1,0:T(8,128)(2,1)} %bitcast.16), channel_id=1, source_target_pairs={{0,32},{1,33},{2,34},{3,35},{4,36},{5,37},{6,38},{7,39},{8,40},{9,... | collective-permute-start | bytes 25165832 | tf_op jit(solution)/shard_map/ppermute | solution.py:43
  4.7 3.8 %collective-permute-start.3 = (bf16[64,1024]{1,0:T(8,128)(2,1)}, bf16[64,1024]{1,0:T(8,128)(2,1)S(1)}, u32[]{:S(2)}, u32[]{:S(2)}) collective-permute-start(bf16[64,1024]{1,0:T(8,128)(2,1)} %source.1), channel_id=1, source_target_pairs={{0,16},{1,17},{2,18},{3,19},{4,20},{5,21},{6,22},{7,23},{8,24},{9,... | collective-permute-start | bytes 393224 | tf_op jit(solution)/shard_map/ppermute | solution.py:39
  9.8 1.6 %collective-permute-done.3 = bf16[64,1024]{1,0:T(8,128)(2,1)S(1)} collective-permute-done((bf16[64,1024]{1,0:T(8,128)(2,1)}, bf16[64,1024]{1,0:T(8,128)(2,1)S(1)}, u32[]{:S(2)}, u32[]{:S(2)}) %collective-permute-start.3) | collective-permute-done | bytes 131104 | tf_op jit(solution)/shard_map/ppermute | solution.py:39
  11.3 2.1 %collective-permute-done.2 = bf16[64,1024]{1,0:T(8,128)(2,1)S(1)} collective-permute-done((bf16[64,1024]{1,0:T(8,128)(2,1)}, bf16[64,1024]{1,0:T(8,128)(2,1)S(1)}, u32[]{:S(2)}, u32[]{:S(2)}) %collective-permute-start.2) | collective-permute-done | bytes 131104 | tf_op jit(solution)/shard_map/ppermute | solution.py:39
  14.2 7.2 %collective-permute-done.4 = bf16[3,64,1024]{2,1,0:T(8,128)(2,1)S(1)} collective-permute-done((bf16[3,64,1024]{2,1,0:T(8,128)(2,1)S(1)}, bf16[3,64,1024]{2,1,0:T(8,128)(2,1)S(1)}, u32[]{:S(2)}, u32[]{:S(2)}) %collective-permute-start.4) | collective-permute-done | bytes 393248 | tf_op jit(solution)/shard_map/ppermute | solution.py:39
  21.6 2.0 %collective-permute-start.6 = (bf16[2,2,2,64,384]{4,3,2,1,0:T(8,128)(2,1)S(1)}, bf16[2,2,2,64,384]{4,3,2,1,0:T(8,128)(2,1)S(1)}, u32[]{:S(2)}, u32[]{:S(2)}) collective-permute-start(bf16[2,2,2,64,384]{4,3,2,1,0:T(8,128)(2,1)S(1)} %get-tuple-element.52), channel_id=1, source_target_pairs={{0,4},{1,5},{2,6},{3,7},{4,0},{5,1},{6,2},{7,3},{8,12},{9,13},{10,... | collective-permute-start | bytes 1179656 | tf_op jit(solution)/shard_map/ppermute | solution.py:39
  23.7 2.2 %collective-permute-start.8 = (bf16[2,2,2,64,256]{4,3,2,1,0:T(8,128)(2,1)S(1)}, bf16[2,2,2,64,256]{4,3,2,1,0:T(8,128)(2,1)S(1)}, u32[]{:S(2)}, u32[]{:S(2)}) collective-permute-start(bf16[2,2,2,64,256]{4,3,2,1,0:T(8,128)(2,1)S(1)} %slice.12), channel_id=1, source_target_pairs={{0,1},{1,0},{2,3},{3,2},{4,5},{5,4},{6,7},{7,6},{8,9},{9,8},{10,11... | collective-permute-start | bytes 786440 | tf_op jit(solution)/shard_map/ppermute | solution.py:39
  27.8 2.4 %collective-permute-done.8 = bf16[2,2,2,64,256]{4,3,2,1,0:T(8,128)(2,1)S(1)} collective-permute-done((bf16[2,2,2,64,256]{4,3,2,1,0:T(8,128)(2,1)S(1)}, bf16[2,2,2,64,256]{4,3,2,1,0:T(8,128)(2,1)S(1)}, u32[]{:S(2)}, u32[]{:S(2)}) %collective-permute-start.8) | collective-permute-done | bytes 262176 | tf_op jit(solution)/shard_map/ppermute | solution.py:39
  30.3 1.5 %collective-permute-start.10 = (bf16[2,2,2,64,384]{4,3,2,1,0:T(8,128)(2,1)S(1)}, bf16[2,2,2,64,384]{4,3,2,1,0:T(8,128)(2,1)S(1)}, u32[]{:S(2)}, u32[]{:S(2)}) collective-permute-start(bf16[2,2,2,64,384]{4,3,2,1,0:T(8,128)(2,1)S(1)} %collective-permute-done.6), channel_id=1, source_target_pairs={{0,80},{1,81},{2,82},{3,83},{4,84},{5,85},{6,86},{7,87},{8,88},{9,... | collective-permute-start | bytes 1179656 | tf_op jit(solution)/shard_map/ppermute | solution.py:39
  31.7 2.1 %collective-permute-start.14 = (bf16[2,2,2,64,384]{4,3,2,1,0:T(8,128)(2,1)S(1)}, bf16[2,2,2,64,384]{4,3,2,1,0:T(8,128)(2,1)S(1)}, u32[]{:S(2)}, u32[]{:S(2)}) collective-permute-start(bf16[2,2,2,64,384]{4,3,2,1,0:T(8,128)(2,1)S(1)} %collective-permute-done.7), channel_id=1, source_target_pairs={{0,1},{1,0},{2,3},{3,2},{4,5},{5,4},{6,7},{7,6},{8,9},{9,8},{10,11... | collective-permute-start | bytes 1179656 | tf_op jit(solution)/shard_map/ppermute | solution.py:39
  35.8 1.8 %collective-permute-start.15 = (bf16[4,2,2,64,384]{4,3,2,1,0:T(8,128)(2,1)S(1)}, bf16[4,2,2,64,384]{4,3,2,1,0:T(8,128)(2,1)}, u32[]{:S(2)}, u32[]{:S(2)}) collective-permute-start(bf16[4,2,2,64,384]{4,3,2,1,0:T(8,128)(2,1)S(1)} %pad_maximum_fusion.1.refs_2_.refs_4_), channel_id=1, source_target_pairs={{0,4},{1,5},{2,6},{3,7},{4,0},{5,1},{6,2},{7,3},{8,12},{9,13},{10,... | collective-permute-start | bytes 2359304 | tf_op jit(solution)/shard_map/ppermute | solution.py:39
  38.4 1.5 %collective-permute-done.14 = bf16[2,2,2,64,384]{4,3,2,1,0:T(8,128)(2,1)S(1)} collective-permute-done((bf16[2,2,2,64,384]{4,3,2,1,0:T(8,128)(2,1)S(1)}, bf16[2,2,2,64,384]{4,3,2,1,0:T(8,128)(2,1)S(1)}, u32[]{:S(2)}, u32[]{:S(2)}) %collective-permute-start.14) | collective-permute-done | bytes 393248 | tf_op jit(solution)/shard_map/ppermute | solution.py:39
  39.9 2.1 %collective-permute-start.11 = (bf16[2,4,2,64,384]{4,3,2,1,0:T(8,128)(2,1)S(1)}, bf16[2,4,2,64,384]{4,3,2,1,0:T(8,128)(2,1)}, u32[]{:S(2)}, u32[]{:S(2)}) collective-permute-start(bf16[2,4,2,64,384]{4,3,2,1,0:T(8,128)(2,1)S(1)} %pad_maximum_fusion.refs_0_), channel_id=1, source_target_pairs={{0,1},{1,0},{2,3},{3,2},{4,5},{5,4},{6,7},{7,6},{8,9},{9,8},{10,11... | collective-permute-start | bytes 2359304 | tf_op jit(solution)/shard_map/ppermute | solution.py:39
  47.5 4.8 %sum_grads.1.summed = bf16[4,4,4,64,512]{4,3,2,1,0:T(8,128)(2,1)S(1)} custom-call(s32[4]{0:T(128)S(1)} %pad_add_fusion.where.refs_6_, bf16[8192,512]{1,0:T(8,128)(2,1)} %bitcast.17, bf16[8192,512]{1,0:T(8,128)(2,1)} %collective-permute-done.5.theirs), custom_call_target="tpu_custom_call" | custom-call | flops 2097152 | bytes 12582912 | tf_op jit(solution)/shard_map/sum_grads/pallas_call | solution.py:129
  52.3 4.1 %project.1 = (f32[1024,512]{1,0:T(8,128)S(1)}, bf16[2,2,4,2,64,384]{5,4,3,2,1,0:T(8,128)(2,1)S(1)}, bf16[2,4,2,2,64,384]{5,4,3,2,1,0:T(8,128)(2,1)S(1)}, bf16[2,2,2,4,64,256]{5,4,3,2,1,0:T(8,128)(2,1)S(1)}) custom-call(bf16[4,4,4,64,512]{4,3,2,1,0:T(8,128)(2,1)S(1)} %sum_grads.1.summed, bf16[2,4,2,64,384]{4,3,2,1,0:T(8,128)(2,1)S(1)} %pad_maximum_fusion.refs_0_, ...), custom_call_target="tpu_custom_call" | custom-call | flops 2147483648 | bytes 8388608 | tf_op jit(solution)/shard_map/project/pallas_call | solution.py:190
  56.4 4.7 %collective-permute-done.16.refs_3_.refs_7_ = bf16[4,2,2,64,384]{4,3,2,1,0:T(8,128)(2,1)} collective-permute-done((bf16[4,2,2,64,384]{4,3,2,1,0:T(8,128)(2,1)S(1)}, bf16[4,2,2,64,384]{4,3,2,1,0:T(8,128)(2,1)}, u32[]{:S(2)}, u32[]{:S(2)}) %collective-permute-start.16) | collective-permute-done | bytes 786464 | tf_op jit(solution)/shard_map/ppermute | solution.py:39
  61.2 5.1 %project_late.1 = (f32[1024,512]{1,0:T(8,128)S(1)}, bf16[2,256,512]{2,1,0:T(8,128)(2,1)S(1)}, bf16[2,2,4,2,64,384]{5,4,3,2,1,0:T(8,128)(2,1)S(1)}, bf16[2,4,2,2,...) custom-call(bf16[4,4,4,64,512]{4,3,2,1,0:T(8,128)(2,1)S(1)} %sum_grads.1.summed, ...), custom_call_target="tpu_custom_call" | custom-call | flops 2147483648 | bytes 8388608 | tf_op jit(solution)/shard_map/project_late/pallas_call | solution.py:190
  66.3 9.0 %collective-permute-start.21 = (bf16[2,256,512]{2,1,0:T(8,128)(2,1)S(1)}, bf16[2,256,512]{2,1,0:T(8,128)(2,1)S(1)}, u32[]{:S(2)}, u32[]{:S(2)}) collective-permute-start(bf16[2,256,512]{2,1,0:T(8,128)(2,1)S(1)} %get-tuple-element.39), channel_id=1, source_target_pairs={{0,32},{1,33},{2,34},{3,35},{4,36},{5,37},{6,38},{7,39},{8,40},{9,... | collective-permute-start | bytes 1572872 | tf_op jit(solution)/shard_map/ppermute | solution.py:43
  75.4 1.5 %collective-permute-done.21.received = bf16[2,256,512]{2,1,0:T(8,128)(2,1)S(1)} collective-permute-done((bf16[2,256,512]{2,1,0:T(8,128)(2,1)S(1)}, bf16[2,256,512]{2,1,0:T(8,128)(2,1)S(1)}, u32[]{:S(2)}, u32[]{:S(2)}) %collective-permute-start.21) | collective-permute-done | bytes 524320 | tf_op jit(solution)/shard_map/ppermute | solution.py:43
  77.6 2.5 %collective-permute-start.22 = (bf16[256,512]{1,0:T(8,128)(2,1)S(1)}, bf16[256,512]{1,0:T(8,128)(2,1)S(1)}, u32[]{:S(2)}, u32[]{:S(2)}) collective-permute-start(bf16[256,512]{1,0:T(8,128)(2,1)S(1)} %get-tuple-element.41), channel_id=1, source_target_pairs={{0,64},{1,65},{2,66},{3,67},{4,68},{5,69},{6,70},{7,71},{8,72},{9,... | collective-permute-start | bytes 786440 | tf_op jit(solution)/shard_map/ppermute | solution.py:47
  81.2 5.5 %collective-permute-done.22.received = bf16[256,512]{1,0:T(8,128)(2,1)S(1)} collective-permute-done((bf16[256,512]{1,0:T(8,128)(2,1)S(1)}, bf16[256,512]{1,0:T(8,128)(2,1)S(1)}, u32[]{:S(2)}, u32[]{:S(2)}) %collective-permute-start.22) | collective-permute-done | bytes 262176 | tf_op jit(solution)/shard_map/ppermute | solution.py:47
  90.0 2.5 %collective-permute-start.29 = (bf16[256,512]{1,0:T(8,128)(2,1)S(1)}, bf16[256,512]{1,0:T(8,128)(2,1)S(1)}, u32[]{:S(2)}, u32[]{:S(2)}) collective-permute-start(bf16[256,512]{1,0:T(8,128)(2,1)S(1)} %direction.1.refs_18_), channel_id=1, source_target_pairs={{0,64},{1,65},{2,66},{3,67},{4,68},{5,69},{6,70},{7,71},{8,72},{9,... | collective-permute-start | bytes 786440 | tf_op jit(solution)/shard_map/ppermute | solution.py:47
  92.7 6.8 %collective-permute-done.29.refs_20_ = bf16[256,512]{1,0:T(8,128)(2,1)S(1)} collective-permute-done((bf16[256,512]{1,0:T(8,128)(2,1)S(1)}, bf16[256,512]{1,0:T(8,128)(2,1)S(1)}, u32[]{:S(2)}, u32[]{:S(2)}) %collective-permute-start.29) | collective-permute-done | bytes 262176 | tf_op jit(solution)/shard_map/ppermute | solution.py:47
  101.4 14.3 %back_project.1 = bf16[8192,512]{1,0:T(8,128)(2,1)} custom-call(s32[4]{0:T(128)S(1)} %pad_add_fusion.where.refs_6_, bf16[2,4,2,64,384]{4,3,2,1,0:T(8,128)(2,1)S(1)} %pad_maximum_fusion.refs_0_, bf16[2,4,2,64,384]{4,3,2,1,0:T(8,128)(2,1)} %constant_dynamic-update-slice_fusion.4.refs_1_, bf16[2,4,2,64,384]{4,3,2,1,0:T(8,128)(2,1)} %collective-permute-done.11.refs_0_.refs_2_, ...), custom_call_target="tpu_custom_call" | custom-call | flops 8589934592 | bytes 25165824 | tf_op jit(solution)/shard_map/back_project/pallas_call | solution.py:320
  (73 shorter events, 22.5 us)
Async XLA Ops:
  0.6 20.8 %collective-permute-start.5 = (bf16[8192,512]{1,0:T(8,128)(2,1)}, bf16[8192,512]{1,0:T(8,128)(2,1)}, u32[]{:S(2)}, u32[]{:S(2)}) collective-permute-start(bf16[8192,512]{1,0:T(8,128)(2,1)} %bitcast.16), channel_id=1, source_target_pairs={{0,32},{1,33},{2,34},{3,35},{4,36},{5,37},{6,38},{7,39},{8,40},{9,... | collective-permute-start | bytes 25165832 | tf_op jit(solution)/shard_map/ppermute | solution.py:43
  13.5 7.9 %collective-permute-start.4 = (bf16[3,64,1024]{2,1,0:T(8,128)(2,1)S(1)}, bf16[3,64,1024]{2,1,0:T(8,128)(2,1)S(1)}, u32[]{:S(2)}, u32[]{:S(2)}) collective-permute-start(bf16[3,64,1024]{2,1,0:T(8,128)(2,1)S(1)} %pad_maximum_fusion.3), channel_id=1, source_target_pairs={{0,16},{1,17},{2,18},{3,19},{4,20},{5,21},{6,22},{7,23},{8,24},{9,... | collective-permute-start | bytes 1179656 | tf_op jit(solution)/shard_map/ppermute | solution.py:39
  21.5 8.6 %collective-permute-start.7 = (bf16[2,2,2,64,384]{4,3,2,1,0:T(8,128)(2,1)S(1)}, bf16[2,2,2,64,384]{4,3,2,1,0:T(8,128)(2,1)S(1)}, u32[]{:S(2)}, u32[]{:S(2)}) collective-permute-start(bf16[2,2,2,64,384]{4,3,2,1,0:T(8,128)(2,1)S(1)} %get-tuple-element.51), channel_id=1, source_target_pairs={{0,80},{1,81},{2,82},{3,83},{4,84},{5,85},{6,86},{7,87},{8,88},{9,... | collective-permute-start | bytes 1179656 | tf_op jit(solution)/shard_map/ppermute | solution.py:39
  21.6 8.5 %collective-permute-start.6 = (bf16[2,2,2,64,384]{4,3,2,1,0:T(8,128)(2,1)S(1)}, bf16[2,2,2,64,384]{4,3,2,1,0:T(8,128)(2,1)S(1)}, u32[]{:S(2)}, u32[]{:S(2)}) collective-permute-start(bf16[2,2,2,64,384]{4,3,2,1,0:T(8,128)(2,1)S(1)} %get-tuple-element.52), channel_id=1, source_target_pairs={{0,4},{1,5},{2,6},{3,7},{4,0},{5,1},{6,2},{7,3},{8,12},{9,13},{10,... | collective-permute-start | bytes 1179656 | tf_op jit(solution)/shard_map/ppermute | solution.py:39
  25.8 8.8 %collective-permute-start.13 = (bf16[2,2,2,64,384]{4,3,2,1,0:T(8,128)(2,1)S(1)}, bf16[2,2,2,64,384]{4,3,2,1,0:T(8,128)(2,1)S(1)}, u32[]{:S(2)}, u32[]{:S(2)}) collective-permute-start(bf16[2,2,2,64,384]{4,3,2,1,0:T(8,128)(2,1)S(1)} %get-tuple-element.51), channel_id=1, source_target_pairs={{0,1},{1,0},{2,3},{3,2},{4,5},{5,4},{6,7},{7,6},{8,9},{9,8},{10,11... | collective-permute-start | bytes 1179656 | tf_op jit(solution)/shard_map/ppermute | solution.py:39
  26.4 9.4 %collective-permute-start.9 = (bf16[2,2,2,64,384]{4,3,2,1,0:T(8,128)(2,1)S(1)}, bf16[2,2,2,64,384]{4,3,2,1,0:T(8,128)(2,1)S(1)}, u32[]{:S(2)}, u32[]{:S(2)}) collective-permute-start(bf16[2,2,2,64,384]{4,3,2,1,0:T(8,128)(2,1)S(1)} %get-tuple-element.52), channel_id=1, source_target_pairs={{0,80},{1,81},{2,82},{3,83},{4,84},{5,85},{6,86},{7,87},{8,88},{9,... | collective-permute-start | bytes 1179656 | tf_op jit(solution)/shard_map/ppermute | solution.py:39
  30.3 11.8 %collective-permute-start.10 = (bf16[2,2,2,64,384]{4,3,2,1,0:T(8,128)(2,1)S(1)}, bf16[2,2,2,64,384]{4,3,2,1,0:T(8,128)(2,1)S(1)}, u32[]{:S(2)}, u32[]{:S(2)}) collective-permute-start(bf16[2,2,2,64,384]{4,3,2,1,0:T(8,128)(2,1)S(1)} %collective-permute-done.6), channel_id=1, source_target_pairs={{0,80},{1,81},{2,82},{3,83},{4,84},{5,85},{6,86},{7,87},{8,88},{9,... | collective-permute-start | bytes 1179656 | tf_op jit(solution)/shard_map/ppermute | solution.py:39
  31.7 8.1 %collective-permute-start.14 = (bf16[2,2,2,64,384]{4,3,2,1,0:T(8,128)(2,1)S(1)}, bf16[2,2,2,64,384]{4,3,2,1,0:T(8,128)(2,1)S(1)}, u32[]{:S(2)}, u32[]{:S(2)}) collective-permute-start(bf16[2,2,2,64,384]{4,3,2,1,0:T(8,128)(2,1)S(1)} %collective-permute-done.7), channel_id=1, source_target_pairs={{0,1},{1,0},{2,3},{3,2},{4,5},{5,4},{6,7},{7,6},{8,9},{9,8},{10,11... | collective-permute-start | bytes 1179656 | tf_op jit(solution)/shard_map/ppermute | solution.py:39
  33.9 10.3 %collective-permute-start.18 = (bf16[2,2,4,64,256]{4,3,2,1,0:T(8,128)(2,1)S(1)}, bf16[2,2,4,64,256]{4,3,2,1,0:T(8,128)(2,1)S(1)}, u32[]{:S(2)}, u32[]{:S(2)}) collective-permute-start(bf16[2,2,4,64,256]{4,3,2,1,0:T(8,128)(2,1)S(1)} %pad_maximum_fusion.2.refs_4_.refs_8_), channel_id=1, source_target_pairs={{0,80},{1,81},{2,82},{3,83},{4,84},{5,85},{6,86},{7,87},{8,88},{9,... | collective-permute-start | bytes 1572872 | tf_op jit(solution)/shard_map/ppermute | solution.py:39
  34.7 11.4 %collective-permute-start.17 = (bf16[2,2,4,64,256]{4,3,2,1,0:T(8,128)(2,1)S(1)}, bf16[2,2,4,64,256]{4,3,2,1,0:T(8,128)(2,1)S(1)}, u32[]{:S(2)}, u32[]{:S(2)}) collective-permute-start(bf16[2,2,4,64,256]{4,3,2,1,0:T(8,128)(2,1)S(1)} %pad_maximum_fusion.2.refs_4_.refs_8_), channel_id=1, source_target_pairs={{0,4},{1,5},{2,6},{3,7},{4,0},{5,1},{6,2},{7,3},{8,12},{9,13},{10,... | collective-permute-start | bytes 1572872 | tf_op jit(solution)/shard_map/ppermute | solution.py:39
  35.8 20.6 %collective-permute-start.15 = (bf16[4,2,2,64,384]{4,3,2,1,0:T(8,128)(2,1)S(1)}, bf16[4,2,2,64,384]{4,3,2,1,0:T(8,128)(2,1)}, u32[]{:S(2)}, u32[]{:S(2)}) collective-permute-start(bf16[4,2,2,64,384]{4,3,2,1,0:T(8,128)(2,1)S(1)} %pad_maximum_fusion.1.refs_2_.refs_4_), channel_id=1, source_target_pairs={{0,4},{1,5},{2,6},{3,7},{4,0},{5,1},{6,2},{7,3},{8,12},{9,13},{10,... | collective-permute-start | bytes 2359304 | tf_op jit(solution)/shard_map/ppermute | solution.py:39
  39.9 16.6 %collective-permute-start.11 = (bf16[2,4,2,64,384]{4,3,2,1,0:T(8,128)(2,1)S(1)}, bf16[2,4,2,64,384]{4,3,2,1,0:T(8,128)(2,1)}, u32[]{:S(2)}, u32[]{:S(2)}) collective-permute-start(bf16[2,4,2,64,384]{4,3,2,1,0:T(8,128)(2,1)S(1)} %pad_maximum_fusion.refs_0_), channel_id=1, source_target_pairs={{0,1},{1,0},{2,3},{3,2},{4,5},{5,4},{6,7},{7,6},{8,9},{9,8},{10,11... | collective-permute-start | bytes 2359304 | tf_op jit(solution)/shard_map/ppermute | solution.py:39
  42.0 19.1 %collective-permute-start.16 = (bf16[4,2,2,64,384]{4,3,2,1,0:T(8,128)(2,1)S(1)}, bf16[4,2,2,64,384]{4,3,2,1,0:T(8,128)(2,1)}, u32[]{:S(2)}, u32[]{:S(2)}) collective-permute-start(bf16[4,2,2,64,384]{4,3,2,1,0:T(8,128)(2,1)S(1)} %constant_dynamic-update-slice_fusion.6.refs_3_.refs_5_), channel_id=1, source_target_pairs={{0,4},{1,5},{2,6},{3,7},{4,0},{5,1},{6,2},{7,3},{8,12},{9,13},{10,... | collective-permute-start | bytes 2359304 | tf_op jit(solution)/shard_map/ppermute | solution.py:39
  45.0 16.2 %collective-permute-start.12 = (bf16[2,4,2,64,384]{4,3,2,1,0:T(8,128)(2,1)}, bf16[2,4,2,64,384]{4,3,2,1,0:T(8,128)(2,1)}, u32[]{:S(2)}, u32[]{:S(2)}) collective-permute-start(bf16[2,4,2,64,384]{4,3,2,1,0:T(8,128)(2,1)} %constant_dynamic-update-slice_fusion.4.refs_1_), channel_id=1, source_target_pairs={{0,1},{1,0},{2,3},{3,2},{4,5},{5,4},{6,7},{7,6},{8,9},{9,8},{10,11... | collective-permute-start | bytes 2359304 | tf_op jit(solution)/shard_map/ppermute | solution.py:39
  46.1 10.3 %collective-permute-start.19 = (bf16[2,2,4,64,256]{4,3,2,1,0:T(8,128)(2,1)S(1)}, bf16[2,2,4,64,256]{4,3,2,1,0:T(8,128)(2,1)}, u32[]{:S(2)}, u32[]{:S(2)}) collective-permute-start(bf16[2,2,4,64,256]{4,3,2,1,0:T(8,128)(2,1)S(1)} %collective-permute-done.17.refs_5_.refs_9_), channel_id=1, source_target_pairs={{0,80},{1,81},{2,82},{3,83},{4,84},{5,85},{6,86},{7,87},{8,88},{9,... | collective-permute-start | bytes 1572872 | tf_op jit(solution)/shard_map/ppermute | solution.py:39
  66.3 10.6 %collective-permute-start.21 = (bf16[2,256,512]{2,1,0:T(8,128)(2,1)S(1)}, bf16[2,256,512]{2,1,0:T(8,128)(2,1)S(1)}, u32[]{:S(2)}, u32[]{:S(2)}) collective-permute-start(bf16[2,256,512]{2,1,0:T(8,128)(2,1)S(1)} %get-tuple-element.39), channel_id=1, source_target_pairs={{0,32},{1,33},{2,34},{3,35},{4,36},{5,37},{6,38},{7,39},{8,40},{9,... | collective-permute-start | bytes 1572872 | tf_op jit(solution)/shard_map/ppermute | solution.py:43
  77.6 9.1 %collective-permute-start.22 = (bf16[256,512]{1,0:T(8,128)(2,1)S(1)}, bf16[256,512]{1,0:T(8,128)(2,1)S(1)}, u32[]{:S(2)}, u32[]{:S(2)}) collective-permute-start(bf16[256,512]{1,0:T(8,128)(2,1)S(1)} %get-tuple-element.41), channel_id=1, source_target_pairs={{0,64},{1,65},{2,66},{3,67},{4,68},{5,69},{6,70},{7,71},{8,72},{9,... | collective-permute-start | bytes 786440 | tf_op jit(solution)/shard_map/ppermute | solution.py:47
  80.0 9.9 %collective-permute-start.20 = (bf16[2,2,4,2,64,384]{5,4,3,2,1,0:T(8,128)(2,1)S(1)}, bf16[2,2,4,2,64,384]{5,4,3,2,1,0:T(8,128)(2,1)S(1)}, u32[]{:S(2)}, u32[]{:S(2)}) collective-permute-start(bf16[2,2,4,2,64,384]{5,4,3,2,1,0:T(8,128)(2,1)S(1)} %get-tuple-element.36), channel_id=1, source_target_pairs={{0,32},{1,33},{2,34},{3,35},{4,36},{5,37},{6,38},{7,39},{8,40},{9,... | collective-permute-start | bytes 4718600 | tf_op jit(solution)/shard_map/ppermute | solution.py:43
  80.7 8.4 %collective-permute-start.26 = (bf16[2,2,2,4,64,256]{5,4,3,2,1,0:T(8,128)(2,1)S(1)}, bf16[2,2,2,4,64,256]{5,4,3,2,1,0:T(8,128)(2,1)S(1)}, u32[]{:S(2)}, u32[]{:S(2)}) collective-permute-start(bf16[2,2,2,4,64,256]{5,4,3,2,1,0:T(8,128)(2,1)S(1)} %get-tuple-element.48), channel_id=1, source_target_pairs={{0,32},{1,33},{2,34},{3,35},{4,36},{5,37},{6,38},{7,39},{8,40},{9,... | collective-permute-start | bytes 3145736 | tf_op jit(solution)/shard_map/ppermute | solution.py:43
  80.7 11.8 %collective-permute-start.24 = (bf16[2,4,2,2,64,384]{5,4,3,2,1,0:T(8,128)(2,1)S(1)}, bf16[2,4,2,2,64,384]{5,4,3,2,1,0:T(8,128)(2,1)S(1)}, u32[]{:S(2)}, u32[]{:S(2)}) collective-permute-start(bf16[2,4,2,2,64,384]{5,4,3,2,1,0:T(8,128)(2,1)S(1)} %get-tuple-element.46), channel_id=1, source_target_pairs={{0,32},{1,33},{2,34},{3,35},{4,36},{5,37},{6,38},{7,39},{8,40},{9,... | collective-permute-start | bytes 4718600 | tf_op jit(solution)/shard_map/ppermute | solution.py:43
  87.9 13.6 %collective-permute-start.23 = (bf16[2,2,4,2,64,384]{5,4,3,2,1,0:T(8,128)(2,1)S(1)}, bf16[2,2,4,2,64,384]{5,4,3,2,1,0:T(8,128)(2,1)S(1)}, u32[]{:S(2)}, u32[]{:S(2)}) collective-permute-start(bf16[2,2,4,2,64,384]{5,4,3,2,1,0:T(8,128)(2,1)S(1)} %get-tuple-element.45), channel_id=1, source_target_pairs={{0,32},{1,33},{2,34},{3,35},{4,36},{5,37},{6,38},{7,39},{8,40},{9,... | collective-permute-start | bytes 4718600 | tf_op jit(solution)/shard_map/ppermute | solution.py:43
  89.1 12.4 %collective-permute-start.25 = (bf16[2,4,2,2,64,384]{5,4,3,2,1,0:T(8,128)(2,1)S(1)}, bf16[2,4,2,2,64,384]{5,4,3,2,1,0:T(8,128)(2,1)S(1)}, u32[]{:S(2)}, u32[]{:S(2)}) collective-permute-start(bf16[2,4,2,2,64,384]{5,4,3,2,1,0:T(8,128)(2,1)S(1)} %get-tuple-element.47), channel_id=1, source_target_pairs={{0,32},{1,33},{2,34},{3,35},{4,36},{5,37},{6,38},{7,39},{8,40},{9,... | collective-permute-start | bytes 4718600 | tf_op jit(solution)/shard_map/ppermute | solution.py:43
  89.1 12.4 %collective-permute-start.27 = (bf16[2,2,2,4,64,256]{5,4,3,2,1,0:T(8,128)(2,1)S(1)}, bf16[2,2,2,4,64,256]{5,4,3,2,1,0:T(8,128)(2,1)S(1)}, u32[]{:S(2)}, u32[]{:S(2)}) collective-permute-start(bf16[2,2,2,4,64,256]{5,4,3,2,1,0:T(8,128)(2,1)S(1)} %get-tuple-element.49), channel_id=1, source_target_pairs={{0,32},{1,33},{2,34},{3,35},{4,36},{5,37},{6,38},{7,39},{8,40},{9,... | collective-permute-start | bytes 3145736 | tf_op jit(solution)/shard_map/ppermute | solution.py:43
  90.0 9.5 %collective-permute-start.29 = (bf16[256,512]{1,0:T(8,128)(2,1)S(1)}, bf16[256,512]{1,0:T(8,128)(2,1)S(1)}, u32[]{:S(2)}, u32[]{:S(2)}) collective-permute-start(bf16[256,512]{1,0:T(8,128)(2,1)S(1)} %direction.1.refs_18_), channel_id=1, source_target_pairs={{0,64},{1,65},{2,66},{3,67},{4,68},{5,69},{6,70},{7,71},{8,72},{9,... | collective-permute-start | bytes 786440 | tf_op jit(solution)/shard_map/ppermute | solution.py:47
  (12 other events, 92.9 us)
